TPU v7x, 32 devices: a whole 2x2x4 slice. The times are simulated.
32 devices in a mesh: leaf: 8 (over z, x), col: 4 (over y, core).
Axes of the slice: x: 2, y: 2, z: 4, core: 2. Of those that a mesh axis runs over, the one named last changes fastest.
Arguments:
- leaf_rhs: bfloat16 [8, 2048, 512], P('leaf', 'col'), may hold values from -6 to 6
- leaf_inverse: bfloat16 [8, 2048, 2048], P('leaf', None, 'col'), may hold values from -1 to 2, as said below
- panels: bfloat16 [8, 3, 128, 2048], P('leaf', None, None, 'col'), may hold values from -1 to 1
- pattern: int32 [8, 3], P('leaf'), may hold values 0 or 1
- offsets: int32 [8, 3], P('leaf'), may hold values from 0 to 128
- sep_inverse: float32 [8, 3, 256, 256], P('leaf'), may hold values from -2 to 2, as said below
- sep_link: float32 [8, 2, 256, 256], P('leaf'), may hold values from -1 to 1, as said below
- sep_rhs: float32 [8, 3, 256, 512], P('leaf'), may hold values from -4 to 4, as said below
Outputs:
- leaf_solution: bfloat16 [8, 2048, 512], P('leaf', 'col')
- sep_solution: float32 [8, 3, 256, 512], P('leaf', None, None, 'col')
Inputs may be any that keep to these rules, and one draw needn't show every extreme that they name: `pattern`: 1 where a leaf couples to its ancestor separator of that level, else 0. A coupling block touches rows offsets to offsets + 127 of its separator. `leaf_inverse`: each block is lower triangular with diagonal entries between 0.5 and 1.5. `sep_inverse`: each block is lower triangular with diagonal entries between 0.5 and 1.5; entries [i, k] are equal for all leaves i of one level-k node, the 2^(k+1) leaves that share i // 2^(k+1). `sep_link`: entries [i, k] are equal for all leaves i that share i // 2^(k+1). `sep_rhs`: entries [i, k] are equal for all leaves i that share i // 2^(k+1).
All inputs are finite; a program needn't handle non-finite values. No bound on the sum of `pattern` on one device may be relied on, other than what follows from the above.
Results may differ from a plain program's by a relative error of at most 0.0062.
Values may be sent and summed in bfloat16 or wider, within the bound.
No kernel may reach another device: no remote copies, remote signals or barrier semaphores. Data moves between devices by JAX's collectives and lax.ppermute only.
A program may use at most 64 MiB of HBM per device.

v0:
```python
import jax
import jax.numpy as jnp
from jax import lax
from jax.sharding import PartitionSpec as P


def from_partner(block, axis, stride):
    count = lax.axis_size(axis)
    route = []
    for low in range(count):
        high = low | 1 << stride
        if high != low and high < count:
            route += [(low, high), (high, low)]
    return lax.ppermute(block, axis, route)


def transposed(matrix, vector):
    return lax.dot_general(
        matrix, vector, (((0,), (0,)), ((), ())), precision=lax.Precision.HIGHEST
    )


def on_device(leaf_rhs, leaf_inverse, panels, pattern, offsets, sep_inverse, sep_link, sep_rhs):
    highest = lax.Precision.HIGHEST
    rhs_rows = leaf_rhs[0]
    inverse = leaf_inverse[0]
    leaf_panel = panels[0]
    coupling_on = pattern[0].astype(jnp.float32)
    starts = offsets[0]
    levels = lax.axis_size("leaf").bit_length() - 1
    sources = rhs_rows.shape[1]
    sep_rows = sep_inverse.shape[2]
    touched = leaf_panel.shape[1]
    column = lax.axis_index("col")
    groups = lax.axis_size("col")
    share_cols = sources // groups
    inv_rows = inverse
    solved = lax.psum_scatter(
        jnp.dot(inv_rows, rhs_rows, preferred_element_type=jnp.float32),
        "col",
        scatter_dimension=0,
        tiled=True,
    ).astype(jnp.bfloat16)
    partial_value = jnp.einsum(
        "kpr,rn->kpn", leaf_panel, solved, preferred_element_type=jnp.float32
    )
    partial_value = lax.psum_scatter(partial_value, "col", scatter_dimension=2, tiled=True)
    sep_right = lax.dynamic_slice_in_dim(sep_rhs[0], column * share_cols, share_cols, 2)
    placed = []
    for height in range(levels):
        zeros_block = jnp.zeros((sep_rows, share_cols), jnp.float32)
        placed.append(
            lax.dynamic_update_slice(
                zeros_block, coupling_on[height] * partial_value[height], (starts[height], 0)
            )
        )
    update = jnp.stack(placed)
    forward_sols = []
    for height in range(levels):
        remote = from_partner(update[height:], "leaf", height)
        update = update.at[height:].add(remote)
        answer = jnp.dot(
            sep_inverse[0, height], sep_right[height] - update[height], precision=highest
        )
        forward_sols.append(answer)
        if height + 1 < levels:
            update = update.at[height + 1].add(
                jnp.dot(sep_link[0, height], answer, precision=highest)
            )
    backward_sols = [None] * levels
    for height in reversed(range(levels)):
        residue = forward_sols[height]
        if height + 1 < levels:
            residue = residue - transposed(sep_link[0, height], backward_sols[height + 1])
        backward_sols[height] = transposed(sep_inverse[0, height], residue)
    solution = jnp.stack(backward_sols)
    rounded = lax.all_gather(solution.astype(jnp.bfloat16), "col", axis=2, tiled=True)
    sliced = jnp.stack(
        [
            lax.dynamic_slice(rounded[height], (starts[height], 0), (touched, sources))
            for height in range(levels)
        ]
    )
    sliced = sliced * pattern[0].astype(jnp.bfloat16)[:, None, None]
    coupled = jnp.einsum("kpr,kpn->rn", leaf_panel, sliced, preferred_element_type=jnp.float32)
    reduced = (solved.astype(jnp.float32) - coupled).astype(jnp.bfloat16)
    inv_rows = inverse
    final = lax.dot_general(
        inv_rows,
        lax.all_gather(reduced, "col", axis=0, tiled=True),
        (((0,), (0,)), ((), ())),
        preferred_element_type=jnp.float32,
    )
    return (final.astype(jnp.bfloat16)[None], solution[None])


def solution(mesh):
    in_specs = (
        P("leaf", "col", None),
        P("leaf", None, "col"),
        P("leaf", None, None, "col"),
        P("leaf", None),
        P("leaf", None),
        P("leaf", None, None, None),
        P("leaf", None, None, None),
        P("leaf", None, None, None),
    )
    out_specs = (P("leaf", "col", None), P("leaf", None, None, "col"))
    return jax.shard_map(
        on_device, mesh=mesh, in_specs=in_specs, out_specs=out_specs, check_vma=False
    )
```

profile of v0, /device:TPU:0, one launch (start us, length us, event | category | flops | bytes accessed | tf_op | source)
XLA Modules:
  0.0 175.4 jit_solution(17628473440097690816)
XLA Ops:
  7.2 1.5 copy-done
  8.8 4.2 %fusion.2 = f32[2048,512]{1,0:T(8,128)} fusion(bf16[1,2048,512]{2,1,0:T(8,128)(2,1)S(1)} %copy-done, bf16[1,512,512]{2,1,0:T(8,128)(2,1)} %param.20), kind=kOutput, calls=%fused_computation.2 | convolution fusion | flops 1073741824 | bytes 6815744 | tf_op jit(solution)/shard_map/dot_general | solution.py:39
  13.1 47.3 %reduce-scatter.3.cloned.1.call-done = f32[512,512]{1,0:T(8,128)} async-done(((f32[2048,512]{1,0:T(8,128)}), f32[512,512]{1,0:T(8,128)}) %reduce-scatter.3.cloned.1.call-update) | async-done | bytes 1048592 | tf_op jit(solution)/shard_map/reduce_scatter | solution.py:38
  60.4 2.6 %convolution_bitcast_fusion.1 = f32[3,128,512]{1,2,0:T(8,128)} fusion(bf16[1,3,128,512]{3,2,1,0:T(8,128)(2,1)S(1)} %copy-done.6, f32[512,512]{1,0:T(8,128)} %reduce-scatter.3.cloned.1.call-done), kind=kOutput, calls=%fused_computation.7 | convolution fusion | flops 201588736 | bytes 2228224 | tf_op jit(solution)/shard_map/kpr,rn->kpn/dot_general | solution.py:44
  70.3 16.2 %reduce-scatter.5.cloned.1.call-done = f32[3,128,128]{1,2,0:T(8,128)} async-done(((f32[3,128,512]{1,2,0:T(8,128)}), f32[3,128,128]{1,2,0:T(8,128)}) %reduce-scatter.5.cloned.1.call-update) | async-done | bytes 196624 | tf_op jit(solution)/shard_map/reduce_scatter | solution.py:47
  86.5 3.0 %slice_multiply_fusion.2 = (f32[1,128,128]{1,2,0:T(8,128)S(1)}, f32[1,128,128]{1,2,0:T(8,128)S(1)}, f32[1,128,128]{1,2,0:T(8,128)S(1)}) fusion(f32[3,128,128]{1,2,0:T(8,128)} %reduce-scatter.5.cloned.1.call-done, f32[]{:T(128)} %bitcast.2, f32[]{:T(128)} %bitcast.9, f32[]{:T(128)} %bitcast.7), kind=kLoop, calls=%fused_computation.69 | loop fusion | flops 49152 | bytes 393228 | tf_op jit(solution)/shard_map/mul | solution.py:54
  89.4 0.8 dynamic_update_slice.12
  90.3 0.8 dynamic_update_slice.13
  91.2 0.8 dynamic_update_slice.14
  92.8 1.5 collective-permute-start
  94.3 1.7 constant_dynamic-slice_fusion.1
  96.8 7.2 %collective-permute-done = f32[3,256,128]{1,2,0:T(8,128)} collective-permute-done((f32[3,256,128]{1,2,0:T(8,128)}, f32[3,256,128]{1,2,0:T(8,128)}, u32[]{:S(2)}, u32[]{:S(2)}) %collective-permute-start) | collective-permute-done | bytes 393248 | tf_op jit(solution)/shard_map/ppermute | solution.py:14
  104.0 1.1 fusion.59
  105.1 1.3 fusion.35
  106.4 1.4 fusion.52
  108.6 1.3 collective-permute-start.1
  109.8 1.6 copy.18
  111.5 4.4 %collective-permute-done.1 = f32[2,256,128]{1,2,0:T(8,128)S(1)} collective-permute-done((f32[2,256,128]{1,2,0:T(8,128)}, f32[2,256,128]{1,2,0:T(8,128)S(1)}, u32[]{:S(2)}, u32[]{:S(2)}) %collective-permute-start.1) | collective-permute-done | bytes 262176 | tf_op jit(solution)/shard_map/ppermute | solution.py:14
  116.0 1.4 fusion.30
  117.4 2.1 %slice_add_fusion = f32[1,256,128]{1,2,0:T(8,128)} fusion(f32[2,256,128]{1,2,0:T(8,128)S(1)} %slice_add_fusion.2, f32[128,256]{1,0:T(8,128)S(1)} %fusion.30, f32[1,2,256,256]{3,2,1,0:T(8,128)} %param.26), kind=kOutput, calls=%fused_computation.55 | convolution fusion | flops 100696064 | bytes 655360 | tf_op jit(solution)/shard_map/dot_general | solution.py:68
  119.4 2.4 %collective-permute-start.2 = (f32[1,256,128]{1,2,0:T(8,128)}, f32[1,256,128]{1,2,0:T(8,128)}, u32[]{:S(2)}, u32[]{:S(2)}) collective-permute-start(f32[1,256,128]{1,2,0:T(8,128)} %slice_add_fusion), channel_id=1, source_target_pairs={{0,16},{16,0},{4,20},{20,4},{8,24},{24,8},{12,28},{28,12},{1,17},{... | collective-permute-start | bytes 393224 | tf_op jit(solution)/shard_map/ppermute | solution.py:14
  121.8 1.7 copy.19
  123.5 3.5 %collective-permute-done.2 = f32[1,256,128]{1,2,0:T(8,128)} collective-permute-done((f32[1,256,128]{1,2,0:T(8,128)}, f32[1,256,128]{1,2,0:T(8,128)}, u32[]{:S(2)}, u32[]{:S(2)}) %collective-permute-start.2) | collective-permute-done | bytes 131104 | tf_op jit(solution)/shard_map/ppermute | solution.py:14
  127.0 1.4 fusion.24
  128.7 1.2 convolution_subtract_fusion.1
  130.2 1.2 convolution_subtract_fusion
  131.8 7.9 %all_gather.6 = bf16[3,256,512]{1,2,0:T(8,128)(2,1)S(1)} all-gather(bf16[3,256,128]{1,2,0:T(8,128)(2,1)S(1)} %fusion.21), channel_id=1, replica_groups=mesh['leaf'=8,'col'=4] {'col'}, dimensions={2}, use_global_device_ids=true | all-gather | bytes 983040 | tf_op jit(solution)/shard_map/all_gather | solution.py:77
  140.1 1.3 fusion.8
  141.6 0.9 copy.13
  142.5 22.6 %all-gather.2.cloned.1.call-done = bf16[2048,512]{1,0:T(8,128)(2,1)} async-done(((bf16[512,512]{1,0:T(8,128)(2,1)}), bf16[2048,512]{1,0:T(8,128)(2,1)}) %all-gather.2.cloned.1.call-update) | async-done | bytes 2097168 | tf_op jit(solution)/shard_map/all_gather | solution.py:90
  165.0 2.9 %fusion.9 = bf16[1,512,512]{1,2,0:T(8,128)(2,1)S(1)} fusion(bf16[2048,512]{1,0:T(8,128)(2,1)} %all-gather.2.cloned.1.call-done, bf16[1,2048,512]{2,1,0:T(8,128)(2,1)S(1)} %copy-done), kind=kOutput, calls=%fused_computation.9 | convolution fusion | flops 1074003968 | bytes 4718592 | tf_op jit(solution)/shard_map/dot_general | solution.py:88
  167.9 1.0 copy.12
  (49 shorter events, 5.1 us)
Async XLA Ops:
  7.2 1.6 copy-start
  7.2 53.2 %reduce-scatter.3.cloned.1.call-start = ((), (), s32[]{:S(2)}) async-start(), calls=%async_computation.2 | async-start | bytes 5242880 | tf_op jit(solution)/shard_map/reduce_scatter | solution.py:38
  13.0 47.4 %copy-start.6 = (bf16[1,3,128,512]{3,2,1,0:T(8,128)(2,1)S(1)}, bf16[1,3,128,512]{3,2,1,0:T(8,128)(2,1)}, u32[]{:S(2)}) copy-start(bf16[1,3,128,512]{3,2,1,0:T(8,128)(2,1)} %param.22) | copy-start | bytes 1179652
  13.0 50.0 %copy-start.11 = (s32[1,3]{1,0:T(1,128)S(1)}, s32[1,3]{1,0:T(1,128)}, u32[]{:S(2)}) copy-start(s32[1,3]{1,0:T(1,128)} %param.24) | copy-start | bytes 40
  13.0 56.6 %copy-start.12 = (s32[1,3]{1,0:T(1,128)S(1)}, s32[1,3]{1,0:T(1,128)}, u32[]{:S(2)}) copy-start(s32[1,3]{1,0:T(1,128)} %param.23) | copy-start | bytes 40
  13.0 73.4 %reduce-scatter.5.cloned.1.call-start = ((), (), s32[]{:S(2)}) async-start(), calls=%async_computation.3 | async-start | bytes 983040 | tf_op jit(solution)/shard_map/reduce_scatter | solution.py:47
  63.0 102.0 %all-gather.2.cloned.1.call-start = ((), (), s32[]{:S(2)}) async-start(), calls=%async_computation.4 | async-start | bytes 2621440 | tf_op jit(solution)/shard_map/all_gather | solution.py:90
  86.5 18.6 %copy-start.2 = (f32[1,3,256,256]{3,2,1,0:T(8,128)S(1)}, f32[1,3,256,256]{3,2,1,0:T(8,128)}, u32[]{:S(2)}) copy-start(f32[1,3,256,256]{3,2,1,0:T(8,128)} %param.25) | copy-start | bytes 2359300
  91.2 5.6 %copy-start.10 = (f32[1,256,128]{1,2,0:T(8,128)}, f32[1,256,128]{1,2,0:T(8,128)S(1)}, u32[]{:S(2)}) copy-start(f32[1,256,128]{1,2,0:T(8,128)S(1)} %dynamic_update_slice.13) | copy-start | bytes 393220
  92.8 11.2 %collective-permute-start = (f32[3,256,128]{1,2,0:T(8,128)}, f32[3,256,128]{1,2,0:T(8,128)}, u32[]{:S(2)}, u32[]{:S(2)}) collective-permute-start(f32[3,256,128]{1,2,0:T(8,128)} %pad_maximum_fusion), channel_id=1, source_target_pairs={{0,4},{4,0},{8,12},{12,8},{16,20},{20,16},{24,28},{28,24},{1,5},{5... | collective-permute-start | bytes 1179656 | tf_op jit(solution)/shard_map/ppermute | solution.py:14
  106.4 1.5 copy-start.8
  108.6 7.4 %collective-permute-start.1 = (f32[2,256,128]{1,2,0:T(8,128)}, f32[2,256,128]{1,2,0:T(8,128)S(1)}, u32[]{:S(2)}, u32[]{:S(2)}) collective-permute-start(f32[2,256,128]{1,2,0:T(8,128)} %slice.227), channel_id=1, source_target_pairs={{0,8},{8,0},{4,12},{12,4},{16,24},{24,16},{20,28},{28,20},{1,9},{9... | collective-permute-start | bytes 786440 | tf_op jit(solution)/shard_map/ppermute | solution.py:14
  116.0 12.8 %copy-start.3 = (f32[1,2,256,256]{3,2,1,0:T(8,128)S(1)}, f32[1,2,256,256]{3,2,1,0:T(8,128)}, u32[]{:S(2)}) copy-start(f32[1,2,256,256]{3,2,1,0:T(8,128)} %param.26) | copy-start | bytes 1572868
  117.4 9.7 %copy-start.9 = (f32[128,256]{1,0:T(8,128)}, f32[128,256]{1,0:T(8,128)S(1)}, u32[]{:S(2)}) copy-start(f32[128,256]{1,0:T(8,128)S(1)} %fusion.30) | copy-start | bytes 393220
  119.4 7.6 %collective-permute-start.2 = (f32[1,256,128]{1,2,0:T(8,128)}, f32[1,256,128]{1,2,0:T(8,128)}, u32[]{:S(2)}, u32[]{:S(2)}) collective-permute-start(f32[1,256,128]{1,2,0:T(8,128)} %slice_add_fusion), channel_id=1, source_target_pairs={{0,16},{16,0},{4,20},{20,4},{8,24},{24,8},{12,28},{28,12},{1,17},{... | collective-permute-start | bytes 393224 | tf_op jit(solution)/shard_map/ppermute | solution.py:14
  130.2 1.6 copy-start.4
  131.8 8.4 %copy-start.1 = (f32[512,512]{1,0:T(8,128)S(1)}, f32[512,512]{1,0:T(8,128)}, u32[]{:S(2)}) copy-start(f32[512,512]{1,0:T(8,128)} %reduce-scatter.3.cloned.1.call-done) | copy-start | bytes 3145732
  131.8 8.4 %copy-start.7 = (bf16[1,3,128,512]{3,2,1,0:T(8,128)(2,1)S(1)}, bf16[1,3,128,512]{3,2,1,0:T(8,128)(2,1)}, u32[]{:S(2)}) copy-start(bf16[1,3,128,512]{3,2,1,0:T(8,128)(2,1)} %param.22) | copy-start | bytes 1179652
  139.8 1.7 copy-start.5
Sparse Core Ops, SparseCore 0:
  13.1 47.2 reduce-scatter.2
  63.1 23.2 reduce-scatter.4
  141.6 23.3 all-gather.1
where the time goes:
time: 176 us; the launch traced here: 175 us
  waiting for transfers between devices  101 us (57%)
  matrix products  21.9 us (12%)
  between operations  20 us (11%)
  local copies, waits for them, and re-layouts  14.2 us (8%)
  blocking collectives  7.94 us (5%)
  starting transfers between devices  5.28 us (3%)
  other arithmetic  4.91 us (3%)
    reduce_scatter x1, waiting for transfers between devices, on_device(): lax.psum_scatter(jnp.dot(inv_rows, rhs_rows, preferred_element_type=jnp.f...  47.3 us
    all_gather x1, waiting for transfers between devices, on_device(): lax.all_gather(reduced, 'col', axis=0, tiled=True)  22.6 us
    reduce_scatter x1, waiting for transfers between devices, on_device(): lax.psum_scatter(partial_value, 'col', scatter_dimension=2, tiled=True)  16.2 us
    ppermute x3, waiting for transfers between devices, from_partner(): return lax.ppermute(block, axis, route)  15.2 us
    all_gather x1, blocking collectives, on_device(): lax.all_gather(solution.astype(jnp.bfloat16), 'col', axis=2, tiled=True)  7.94 us
    unnamed x31, local copies, waits for them, and re-layouts  7.58 us
    ppermute x3, starting transfers between devices, from_partner(): return lax.ppermute(block, axis, route)  5.16 us
    dot_general x1, matrix products, on_device(): jnp.dot(inv_rows, rhs_rows, preferred_element_type=jnp.float32)  4.23 us
  transfers between devices with their start and end apart: 6, of which 6 were waited for; matrix products, arithmetic and copies ran while one was open for 5% of the time, Pallas kernels for 0%

commit v1 on v0

v1 whole, which is shorter than its diff:
```python
import functools

import jax
import jax.numpy as jnp
from jax import lax
from jax.experimental import pallas as pl
from jax.experimental.pallas import tpu as pltpu
from jax.sharding import PartitionSpec as P

F32 = jnp.float32
BF16 = jnp.bfloat16
HIGHEST = lax.Precision.HIGHEST
NN = (((1,), (0,)), ((), ()))
NT = (((1,), (1,)), ((), ()))
TN = (((0,), (0,)), ((), ()))
AXES = ("leaf", "col")


def moved(block, leaf_flip, col_flip):
    leaves, groups = lax.axis_size("leaf"), lax.axis_size("col")
    route = [
        (leaf * groups + col, (leaf ^ leaf_flip) * groups + (col ^ col_flip))
        for leaf in range(leaves)
        for col in range(groups)
    ]
    return lax.ppermute(block, AXES, route)


def call(body, outs, smem, vmem, scratch=(), limit=24):
    specs = [pl.BlockSpec(memory_space=pltpu.SMEM)] * len(smem)
    specs += [pl.BlockSpec(memory_space=pltpu.VMEM)] * len(vmem)
    return pl.pallas_call(
        body,
        out_shape=outs,
        in_specs=specs,
        out_specs=[pl.BlockSpec(memory_space=pltpu.VMEM)] * len(outs),
        scratch_shapes=scratch,
        compiler_params=pltpu.CompilerParams(vmem_limit_bytes=limit << 20),
        cost_estimate=pl.CostEstimate(flops=0, bytes_accessed=0, transcendentals=0),
        name=getattr(body, "func", body).__name__,
    )(*smem, *vmem)


def dot(a, b, dims):
    return lax.dot_general(a, b, dims, preferred_element_type=F32)


def split(value):
    high = value.astype(BF16)
    return high, (value - high.astype(F32)).astype(BF16)


def dot_split(value, high, low, dims):
    first, second = split(value)
    return dot(first, high, dims) + (dot(first, low, dims) + dot(second, high, dims))


def rows_at(start, size):
    return pl.ds(pl.multiple_of(start, size), size)


def prepare(ids, inverse, link, rhs, q_high, q_low, k_high, k_low, right):
    column, side = ids[0], ids[1]
    levels, share, _ = right.shape
    wide = 2 * share
    for k in range(levels):
        block = inverse[k]
        high, low = split(
            lax.dot_general(block, block, TN, precision=HIGHEST, preferred_element_type=F32)
        )
        q_high[k] = high
        q_low[k] = low
        if k + 1 < levels:
            high, low = split(
                lax.dot_general(link[k], block, NN, precision=HIGHEST, preferred_element_type=F32)
            )
            k_high[k] = high
            k_low[k] = low
        part = rhs[k, :, rows_at(column * wide, wide)].T
        right[k] = jnp.where(side == 0, part[:share], part[share:])


def leaf_products(ids, inverse, rhs, keep, turned, *sends):
    column = ids[0]
    rows = rhs.shape[0]
    half = len(sends) + 1
    turned[...] = rhs[...].T
    for j in range(half):
        for top in range(2):
            block = ((column ^ j) & (half - 1)) + top * half
            value = dot(inverse[rows_at(block * rows, rows), :], rhs[...], NN)
            if j == 0:
                keep[top] = value
            else:
                sends[j - 1][top] = value.astype(BF16)


def add_products(count, ids, keep, *refs):
    low, high, high_own = refs[count:]
    value = keep[0]
    for r in refs[:count]:
        value += r[0].astype(F32)
    low[...] = value.astype(BF16)
    value = keep[1]
    for r in refs[:count]:
        value += r[1].astype(F32)
    high[...] = value.astype(BF16)
    high_own[...] = value


def panel_products(masks, ids, inverse, *refs):
    panels, out = refs[: len(masks)], refs[-1]
    column = ids[0]
    rows = inverse.shape[1]
    total = None
    for mask, panel in zip(masks, panels):
        value = dot(panel[...], inverse[rows_at((column ^ mask) * rows, rows), :], NN)
        total = value if total is None else total + value
    out[...] = total


def partials(masks, ids, inverse, early, turned, *refs):
    panels = refs[: len(masks)]
    weight, keep, *sends = refs[len(masks) :]
    scratch = sends.pop()
    column = ids[0]
    rows = inverse.shape[1]
    total = early[...]
    for mask, panel in zip(masks, panels):
        total += dot(panel[...], inverse[rows_at((column ^ mask) * rows, rows), :], NN)
    weight[...] = total.astype(BF16)
    scratch[...] = dot(turned[...], weight[...], NT)
    half = len(sends) + 1
    wide = keep.shape[0] // 2
    for j in range(half):
        for top in range(2):
            block = ((column ^ j) & (half - 1)) + top * half
            value = scratch[rows_at(block * wide, wide), :]
            if j == 0:
                keep[top * wide : (top + 1) * wide] = value
            else:
                sends[j - 1][top * wide : (top + 1) * wide] = value.astype(BF16)


def spread(count, ids, keep, *refs):
    received = refs[:count]
    own, same, other, cross = refs[count:]
    top, side = ids[2], ids[1]
    share = own.shape[0]

    def piece(which_top, which_side):
        at = rows_at((which_top * 2 + which_side) * share, share)
        value = keep[at, :]
        for r in received:
            value += r[at, :].astype(F32)
        return value

    own[...] = piece(top, side)
    same[...] = piece(1 - top, side).astype(BF16)
    other[...] = piece(top, 1 - side).astype(BF16)
    cross[...] = piece(1 - top, 1 - side).astype(BF16)


def upward(touched, ids, spots, own, same, other, cross, right, k_high, k_low, kept, *sends):
    levels, share, sep_rows = right.shape
    mine = own[...] + same[...].astype(F32)
    theirs = other[...].astype(F32) + cross[...].astype(F32)
    blank = jnp.zeros((share, sep_rows - touched), F32)

    def placed(value, row, k):
        block = value[:, k * touched : (k + 1) * touched] * spots[row + 1, k].astype(F32)
        return pltpu.roll(jnp.concatenate([block, blank], axis=1), spots[row, k], 1)

    carried = None
    for k in range(levels):
        value = placed(mine, 0, k) + placed(theirs, 2, k)
        if k > 0:
            value += carried
        kept[k] = value
        for j in range(min(k, len(sends))):
            sends[j][k - 1 - j] = value.astype(BF16)
        if k + 1 < levels:
            rest = right[k] * (0.5**k) - value
            carried = dot_split(rest, k_high[k], k_low[k], NT)


def downward(touched, lengths, ids, spots, kept, right, q_high, q_low, k_high, k_low, *refs):
    received = refs[: len(lengths)]
    solution, passed, mine, theirs = refs[len(lengths) :]
    levels, _, sep_rows = right.shape
    parent = None
    for k in reversed(range(levels)):
        value = right[k] - kept[k]
        for length, block in zip(lengths, received):
            if length <= k:
                value -= block[k - length].astype(F32)
        answer = dot_split(value, q_high[k], q_low[k], NN)
        if parent is not None:
            answer -= dot_split(parent, k_high[k], k_low[k], NN)
        parent = answer
        solution[k] = answer
        passed[k] = answer
        rounded = answer.astype(BF16).astype(F32)
        for row, out in ((0, mine), (2, theirs)):
            shift = (sep_rows - spots[row, k]) % sep_rows
            piece = pltpu.roll(rounded, shift, 1)[:, :touched] * spots[row + 1, k].astype(F32)
            out[:, k * touched : (k + 1) * touched] = piece.astype(BF16)


def leaf_transposed(count, ids, inverse, weight, *refs):
    out, weight_turned = refs[-2:]
    blocks = refs[:-2]
    column = ids[0]
    rows = inverse.shape[1]
    half = count
    weight_turned[...] = weight[...].T
    total = None
    for j in range(half):
        for top in range(2):
            block = ((column ^ j) & (half - 1)) + top * half
            value = dot(inverse[rows_at(block * rows, rows), :], blocks[2 * j + top][...], TN)
            total = value if total is None else total + value
    out[...] = total


def finish(half, ids, base, weight_turned, *refs):
    out, gathered = refs[-2:]
    blocks = refs[:-2]
    column, side, top = ids[0], ids[1], ids[2]
    share = blocks[0].shape[0]
    for j in range(half):
        inner = (column ^ j) & (half - 1)
        for n, (flip_side, flip_top) in enumerate(((0, 0), (0, 1), (1, 0), (1, 1))):
            which_top = top ^ flip_top
            which_side = side ^ flip_side
            at = ((which_top * half + inner) * 2 + which_side) * share
            gathered[rows_at(at, share), :] = blocks[4 * j + n][...]
    out[...] = (base[...] - dot(weight_turned[...], gathered[...], NT)).astype(BF16)


def assemble(ids, mine, theirs, out):
    side = ids[1]
    for k in range(mine.shape[0]):
        first = jnp.where(side == 0, mine[k], theirs[k])
        second = jnp.where(side == 0, theirs[k], mine[k])
        out[k] = jnp.concatenate([first, second], axis=0).T


def on_device(leaf_rhs, leaf_inverse, panels, pattern, offsets, sep_inverse, sep_link, sep_rhs):
    rhs, inverse = leaf_rhs[0], leaf_inverse[0]
    rows, sources = rhs.shape
    leaves, groups = lax.axis_size("leaf"), lax.axis_size("col")
    levels = leaves.bit_length() - 1
    half = groups // 2
    touched, sep_rows = panels.shape[2], sep_inverse.shape[2]
    share = sources // groups // 2
    panel = panels[0].reshape(levels * touched, rows)
    column = lax.axis_index("col")
    side = lax.axis_index("leaf") & 1
    ids = jnp.stack([column, side, column // half]).astype(jnp.int32)

    def shape(dims, dtype=F32):
        return jax.ShapeDtypeStruct(dims, dtype)

    held = {0: panel}
    for bit in reversed(range(groups.bit_length() - 1)):
        for mask in list(held):
            held[mask | 1 << bit] = moved(held[mask], 0, 1 << bit)
    spots = jnp.concatenate([offsets, pattern], axis=0)
    spots = jnp.concatenate([spots, moved(spots, 1, 0)], axis=0)

    keep, turned, *sends = call(
        leaf_products,
        [shape((2, rows, sources)), shape((sources, rows), BF16)]
        + [shape((2, rows, sources), BF16)] * (half - 1),
        [ids],
        [inverse, rhs],
    )
    q_high, q_low, k_high, k_low, right = call(
        prepare,
        [shape((levels, sep_rows, sep_rows), BF16)] * 2
        + [shape((levels - 1, sep_rows, sep_rows), BF16)] * 2
        + [shape((levels, share, sep_rows))],
        [ids],
        [sep_inverse[0], sep_link[0], sep_rhs[0]],
    )
    received = [moved(block, 0, j + 1) for j, block in enumerate(sends)]
    low, high, high_own = call(
        functools.partial(add_products, half - 1),
        [shape((rows, sources), BF16)] * 2 + [shape((rows, sources))],
        [ids],
        [keep, *received],
    )

    near = [mask for mask in held if mask < half]
    far = [mask for mask in held if mask >= half]
    early = call(
        functools.partial(panel_products, near),
        [shape(panel.shape)],
        [ids],
        [inverse] + [held[mask] for mask in near],
    )[0]
    names = [shape(panel.shape, BF16), shape((sources // half, levels * touched))]
    names += [shape((sources // half, levels * touched), BF16)] * (half - 1)
    weight, part_keep, *part_sends = call(
        functools.partial(partials, far),
        names,
        [ids],
        [inverse, early, turned] + [held[mask] for mask in far],
        [pltpu.VMEM((sources, levels * touched), F32)],
    )
    part_received = [moved(block, 0, j + 1) for j, block in enumerate(part_sends)]
    piece = (share, levels * touched)
    own, same, other, cross = call(
        functools.partial(spread, half - 1),
        [shape(piece)] + [shape(piece, BF16)] * 3,
        [ids],
        [part_keep, *part_received],
    )
    same, other, cross = moved(same, 0, half), moved(other, 1, 0), moved(cross, 1, half)

    high, own = lax.optimization_barrier((high, own))
    solved_high = (high_own + moved(high, 0, half).astype(F32)).astype(BF16)
    solved = [low, solved_high]
    for j in range(1, half):
        solved += [moved(low, 0, j), moved(solved_high, 0, j)]
    base, weight_turned = call(
        functools.partial(leaf_transposed, half),
        [shape((rows, sources)), shape((rows, levels * touched), BF16)],
        [ids],
        [inverse, weight, *solved],
    )

    kept, *up_sends = call(
        functools.partial(upward, touched),
        [shape((levels, share, sep_rows))]
        + [shape((levels - length, share, sep_rows), BF16) for length in range(1, levels)],
        [ids, spots],
        [own, same, other, cross, right, k_high, k_low],
    )
    lengths, up_received = [], []
    for delta in range(1, leaves // 2):
        lengths.append(delta.bit_length())
        up_received.append(moved(up_sends[delta.bit_length() - 1], 2 * delta, 0))
    answer, passed, mine, theirs = call(
        functools.partial(downward, touched, lengths),
        [shape((levels, share, sep_rows))] * 2 + [shape(piece, BF16)] * 2,
        [ids, spots],
        [kept, right, q_high, q_low, k_high, k_low, *up_received],
    )

    blocks = [mine, moved(mine, 0, half), moved(theirs, 1, 0), moved(theirs, 1, half)]
    passed = moved(passed, 1, 0)
    for j in range(1, half):
        blocks += [moved(block, 0, j) for block in blocks[:4]]
    final = call(
        functools.partial(finish, half),
        [shape((rows, sources), BF16)],
        [ids],
        [base, weight_turned, *blocks],
        [pltpu.VMEM((sources, levels * touched), BF16)],
    )[0]
    solution_rows = call(
        assemble, [shape((levels, sep_rows, 2 * share))], [ids], [answer, passed]
    )[0]
    return final[None], solution_rows[None]


def solution(mesh):
    in_specs = (
        P("leaf", "col", None),
        P("leaf", None, "col"),
        P("leaf", None, None, "col"),
        P("leaf", None),
        P("leaf", None),
        P("leaf", None, None, None),
        P("leaf", None, None, None),
        P("leaf", None, None, None),
    )
    out_specs = (P("leaf", "col", None), P("leaf", None, None, "col"))
    return jax.shard_map(
        on_device, mesh=mesh, in_specs=in_specs, out_specs=out_specs, check_vma=False
    )
```

time: 176 us -> 77.6 us (0.44)
  waiting for transfers between devices: 101 us -> 38.5 us
  matrix products: 21.9 us -> 0 us
  between operations: 20 us -> 0.85 us
  Pallas kernels: 0 us -> 15.3 us
  starting transfers between devices: 5.28 us -> 19.8 us
  local copies, waits for them, and re-layouts: 14.2 us -> 2.68 us
  blocking collectives: 7.94 us -> 0 us
  other arithmetic: 4.91 us -> 0.26 us
    reduce_scatter x2 -> x0, waiting for transfers between devices: 63.5 us -> none  [the longest x1 47.3 us: on_device(): lax.psum_scatter(jnp.dot(inv_rows, rhs_rows, preferred_element_type=jnp.f...]
    ppermute x3 -> x23, waiting for transfers between devices: 15.2 us -> 38.5 us  [moved(): return lax.ppermute(block, AXES, route)]
    all_gather x1 -> x0, waiting for transfers between devices: 22.6 us -> none  [on_device(): lax.all_gather(reduced, 'col', axis=0, tiled=True)]
    dot_general x14 -> x0, matrix products: 21.9 us -> none  [the longest x1 4.23 us: on_device(): jnp.dot(inv_rows, rhs_rows, preferred_element_type=jnp.float32)]
    pallas_call x0 -> x11, Pallas kernels: none -> 15.3 us  [call(): pl.pallas_call(body, out_shape=outs, in_specs=specs, out_specs=[pl.BlockS...]
    ppermute x3 -> x23, starting transfers between devices: 5.16 us -> 19.8 us  [moved(): return lax.ppermute(block, AXES, route)]
    all_gather x1 -> x0, blocking collectives: 7.94 us -> none  [on_device(): lax.all_gather(solution.astype(jnp.bfloat16), 'col', axis=2, tiled=True)]
    unnamed x31 -> x18, local copies, waits for them, and re-layouts: 7.58 us -> 2.68 us
  transfers between devices with their start and end apart: 6 -> 23, of which waited for: 6 -> 12; matrix products, arithmetic and copies ran while one was open for 5% -> 0% of each run, Pallas kernels for 0% -> 14%
where the time goes in v1:
time: 77.6 us; the launch traced here: 77.4 us
  waiting for transfers between devices  38.5 us (50%)
  starting transfers between devices  19.8 us (26%)
  Pallas kernels  15.3 us (20%)
  local copies, waits for them, and re-layouts  2.68 us (3%)
  between operations  0.85 us (1%)
    ppermute x23, waiting for transfers between devices, moved(): return lax.ppermute(block, AXES, route)  38.5 us
    ppermute x23, starting transfers between devices, moved(): return lax.ppermute(block, AXES, route)  19.8 us
    pallas_call x11, Pallas kernels, call(): pl.pallas_call(body, out_shape=outs, in_specs=specs, out_specs=[pl.BlockS...  15.3 us
    unnamed x18, local copies, waits for them, and re-layouts  2.68 us
  transfers between devices with their start and end apart: 23, of which 12 were waited for; matrix products, arithmetic and copies ran while one was open for 0% of the time, Pallas kernels for 14%

profile of v1, /device:TPU:0, one launch (start us, length us, event | category | flops | bytes accessed | tf_op | source)
XLA Modules:
  0.0 77.4 jit_solution(1708919189062130574)
XLA Ops:
  0.7 1.6 %copy-done = bf16[1,2048,512]{2,1,0:T(8,128)(2,1)S(1)} copy-done((bf16[1,2048,512]{2,1,0:T(8,128)(2,1)S(1)}, bf16[1,2048,512]{2,1,0:T(8,128)(2,1)}, u32[]{:S(2)}) %copy-start) | copy-done | bytes 2097176
  2.3 1.0 %copy-done.4 = bf16[1,512,512]{2,1,0:T(8,128)(2,1)S(1)} copy-done((bf16[1,512,512]{2,1,0:T(8,128)(2,1)S(1)}, bf16[1,512,512]{2,1,0:T(8,128)(2,1)}, u32[]{:S(2)}) %copy-start.4) | copy-done | bytes 524312
  3.4 1.8 %leaf_products.1 = (f32[2,512,512]{2,1,0:T(8,128)S(1)}, bf16[512,512]{1,0:T(8,128)(2,1)S(1)}, bf16[2,512,512]{2,1,0:T(8,128)(2,1)S(1)}) custom-call(s32[3]{0:T(128)S(1)} %pad_add_fusion.2.ids, bf16[2048,512]{1,0:T(8,128)(2,1)S(1)} %bitcast.11, bf16[512,512]{1,0:T(8,128)(2,1)S(1)} %bitcast.17), custom_call_target="tpu_custom_call" | custom-call | tf_op jit(solution)/shard_map/leaf_products/pallas_call | solution.py:32
  5.7 2.6 %collective-permute-start.1 = (bf16[384,512]{1,0:T(8,128)(2,1)S(1)}, bf16[384,512]{1,0:T(8,128)(2,1)S(1)}, u32[]{:S(2)}, u32[]{:S(2)}) collective-permute-start(bf16[384,512]{1,0:T(8,128)(2,1)S(1)} %bitcast.19), channel_id=1, source_target_pairs={{0,2},{1,3},{2,0},{3,1},{4,6},{5,7},{6,4},{7,5},{8,10},{9,11},{10,... | collective-permute-start | bytes 1179656 | tf_op jit(solution)/shard_map/ppermute | solution.py:26
  8.4 9.5 %collective-permute-done.1.refs_0_ = bf16[384,512]{1,0:T(8,128)(2,1)S(1)} collective-permute-done((bf16[384,512]{1,0:T(8,128)(2,1)S(1)}, bf16[384,512]{1,0:T(8,128)(2,1)S(1)}, u32[]{:S(2)}, u32[]{:S(2)}) %collective-permute-start.1) | collective-permute-done | bytes 393248 | tf_op jit(solution)/shard_map/ppermute | solution.py:26
  18.0 1.1 %panel_products.1.early = f32[384,512]{1,0:T(8,128)S(1)} custom-call(s32[3]{0:T(128)S(1)} %pad_add_fusion.2.ids, bf16[2048,512]{1,0:T(8,128)(2,1)S(1)} %bitcast.12, bf16[384,512]{1,0:T(8,128)(2,1)S(1)} %bitcast.21, bf16[384,512]{1,0:T(8,128)(2,1)S(1)} %collective-permute-done.refs_1_), custom_call_target="tpu_custom_call" | custom-call | tf_op jit(solution)/shard_map/panel_products/pallas_call | solution.py:32
  19.7 1.6 %partials.1 = (bf16[384,512]{1,0:T(8,128)(2,1)S(1)}, f32[256,384]{1,0:T(8,128)S(1)}, bf16[256,384]{1,0:T(8,128)(2,1)S(1)}) custom-call(s32[3]{0:T(128)S(1)} %pad_add_fusion.2.ids, bf16[2048,512]{1,0:T(8,128)(2,1)S(1)} %bitcast.13, f32[384,512]{1,0:T(8,128)S(1)} %panel_products.1.early, bf16[512,512]{1,0:T(8,128)(2,1)S(1)} %get-tuple-element.31.turned, ...), custom_call_target="tpu_custom_call" | custom-call | tf_op jit(solution)/shard_map/partials/pallas_call | solution.py:32
  21.5 1.3 %collective-permute-done.4.refs_0_ = bf16[256,384]{1,0:T(8,128)(2,1)S(1)} collective-permute-done((bf16[256,384]{1,0:T(8,128)(2,1)S(1)}, bf16[256,384]{1,0:T(8,128)(2,1)S(1)}, u32[]{:S(2)}, u32[]{:S(2)}) %collective-permute-start.4) | collective-permute-done | bytes 196640 | tf_op jit(solution)/shard_map/ppermute | solution.py:26
  23.5 0.7 add_products.1
  24.2 1.8 %collective-permute-start.5 = (bf16[512,512]{1,0:T(8,128)(2,1)S(1)}, bf16[512,512]{1,0:T(8,128)(2,1)S(1)}, u32[]{:S(2)}, u32[]{:S(2)}) collective-permute-start(bf16[512,512]{1,0:T(8,128)(2,1)S(1)} %get-tuple-element.41), channel_id=1, source_target_pairs={{0,2},{1,3},{2,0},{3,1},{4,6},{5,7},{6,4},{7,5},{8,10},{9,11},{10,... | collective-permute-start | bytes 1572872 | tf_op jit(solution)/shard_map/ppermute | solution.py:26
  26.1 12.2 %collective-permute-done.5 = bf16[512,512]{1,0:T(8,128)(2,1)S(1)} collective-permute-done((bf16[512,512]{1,0:T(8,128)(2,1)S(1)}, bf16[512,512]{1,0:T(8,128)(2,1)S(1)}, u32[]{:S(2)}, u32[]{:S(2)}) %collective-permute-start.5) | collective-permute-done | bytes 524320 | tf_op jit(solution)/shard_map/ppermute | solution.py:26
  38.6 1.8 %collective-permute-start.8 = (s32[2,3]{1,0:T(2,128)S(1)}, s32[2,3]{1,0:T(2,128)S(1)}, u32[]{:S(2)}, u32[]{:S(2)}) collective-permute-start(s32[2,3]{1,0:T(2,128)S(1)} %pad_add_fusion.1), channel_id=1, source_target_pairs={{0,4},{1,5},{2,6},{3,7},{4,0},{5,1},{6,2},{7,3},{8,12},{9,13},{10,... | collective-permute-start | bytes 80 | tf_op jit(solution)/shard_map/ppermute | solution.py:26
  40.4 1.9 %prepare.1 = (bf16[3,256,256]{2,1,0:T(8,128)(2,1)S(1)}, bf16[3,256,256]{2,1,0:T(8,128)(2,1)S(1)}, bf16[2,256,256]{2,1,0:T(8,128)(2,1)S(1)}, bf16[2,256,256]{2,1,0:T(8,128)(2,1)S(1)}, f32[3,64,256]{2,1,0:T(8,128)S(1)}) custom-call(s32[3]{0:T(128)S(1)} %pad_add_fusion.2.ids, f32[3,256,256]{2,1,0:T(8,128)S(1)} %bitcast.16, f32[2,256,256]{2,1,0:T(8,128)S(1)} %bitcast.18, ...), custom_call_target="tpu_custom_call" | custom-call | tf_op jit(solution)/shard_map/prepare/pallas_call | solution.py:32
  42.6 2.7 %collective-permute-start.11 = (bf16[64,384]{1,0:T(8,128)(2,1)S(1)}, bf16[64,384]{1,0:T(8,128)(2,1)S(1)}, u32[]{:S(2)}, u32[]{:S(2)}) collective-permute-start(bf16[64,384]{1,0:T(8,128)(2,1)S(1)} %get-tuple-element.47), channel_id=1, source_target_pairs={{0,6},{1,7},{2,4},{3,5},{4,2},{5,3},{6,0},{7,1},{8,14},{9,15},{10,... | collective-permute-start | bytes 147464 | tf_op jit(solution)/shard_map/ppermute | solution.py:26
  45.8 0.8 collective-permute-done.10.other
  46.6 1.7 %collective-permute-done.11.cross = bf16[64,384]{1,0:T(8,128)(2,1)S(1)} collective-permute-done((bf16[64,384]{1,0:T(8,128)(2,1)S(1)}, bf16[64,384]{1,0:T(8,128)(2,1)S(1)}, u32[]{:S(2)}, u32[]{:S(2)}) %collective-permute-start.11) | collective-permute-done | bytes 49184 | tf_op jit(solution)/shard_map/ppermute | solution.py:26
  48.2 1.1 %collective-permute-done.9.same = bf16[64,384]{1,0:T(8,128)(2,1)S(1)} collective-permute-done((bf16[64,384]{1,0:T(8,128)(2,1)S(1)}, bf16[64,384]{1,0:T(8,128)(2,1)S(1)}, u32[]{:S(2)}, u32[]{:S(2)}) %collective-permute-start.9) | collective-permute-done | bytes 49184 | tf_op jit(solution)/shard_map/ppermute | solution.py:26
  49.4 1.2 %upward.1 = (f32[3,64,256]{2,1,0:T(8,128)S(1)}, bf16[2,64,256]{2,1,0:T(8,128)(2,1)S(1)}, bf16[1,64,256]{2,1,0:T(8,128)(2,1)S(1)}) custom-call(s32[3]{0:T(128)S(1)} %pad_add_fusion.2.ids, s32[4,3]{1,0:T(4,128)S(1)} %pad_add_fusion.spots, f32[64,384]{1,0:T(8,128)S(1)} %get-tuple-element.44.own, bf16[64,384]{1,0:T(8,128)(2,1)S(1)} %collective-permute-done.9.same, ...), custom_call_target="tpu_custom_call" | custom-call | tf_op jit(solution)/shard_map/upward/pallas_call | solution.py:32
  50.6 1.6 %collective-permute-start.12 = (bf16[2,64,256]{2,1,0:T(8,128)(2,1)S(1)}, bf16[2,64,256]{2,1,0:T(8,128)(2,1)S(1)}, u32[]{:S(2)}, u32[]{:S(2)}) collective-permute-start(bf16[2,64,256]{2,1,0:T(8,128)(2,1)S(1)} %get-tuple-element.54), channel_id=1, source_target_pairs={{0,8},{1,9},{2,10},{3,11},{4,12},{5,13},{6,14},{7,15},{8,0},{9,1},... | collective-permute-start | bytes 196616 | tf_op jit(solution)/shard_map/ppermute | solution.py:26
  52.2 2.6 %collective-permute-start.13 = (bf16[1,64,256]{2,1,0:T(8,128)(2,1)S(1)}, bf16[1,64,256]{2,1,0:T(8,128)(2,1)S(1)}, u32[]{:S(2)}, u32[]{:S(2)}) collective-permute-start(bf16[1,64,256]{2,1,0:T(8,128)(2,1)S(1)} %get-tuple-element.55), channel_id=1, source_target_pairs={{0,16},{1,17},{2,18},{3,19},{4,20},{5,21},{6,22},{7,23},{8,24},{9,... | collective-permute-start | bytes 98312 | tf_op jit(solution)/shard_map/ppermute | solution.py:26
  55.0 2.0 %collective-permute-done.13.refs_1_ = bf16[1,64,256]{2,1,0:T(8,128)(2,1)S(1)} collective-permute-done((bf16[1,64,256]{2,1,0:T(8,128)(2,1)S(1)}, bf16[1,64,256]{2,1,0:T(8,128)(2,1)S(1)}, u32[]{:S(2)}, u32[]{:S(2)}) %collective-permute-start.13) | collective-permute-done | bytes 32800 | tf_op jit(solution)/shard_map/ppermute | solution.py:26
  57.0 3.5 %collective-permute-done.14.refs_2_ = bf16[1,64,256]{2,1,0:T(8,128)(2,1)S(1)} collective-permute-done((bf16[1,64,256]{2,1,0:T(8,128)(2,1)S(1)}, bf16[1,64,256]{2,1,0:T(8,128)(2,1)S(1)}, u32[]{:S(2)}, u32[]{:S(2)}) %collective-permute-start.14) | collective-permute-done | bytes 32800 | tf_op jit(solution)/shard_map/ppermute | solution.py:26
  60.5 1.3 %downward.1 = (f32[3,64,256]{2,1,0:T(8,128)S(1)}, f32[3,64,256]{2,1,0:T(8,128)S(1)}, bf16[64,384]{1,0:T(8,128)(2,1)S(1)}, bf16[64,384]{1,0:T(8,128)(2,1)S(1)}) custom-call(s32[3]{0:T(128)S(1)} %pad_add_fusion.2.ids, s32[4,3]{1,0:T(4,128)S(1)} %pad_add_fusion.spots, f32[3,64,256]{2,1,0:T(8,128)S(1)} %get-tuple-element.51.kept, ...), custom_call_target="tpu_custom_call" | custom-call | tf_op jit(solution)/shard_map/downward/pallas_call | solution.py:32
  61.8 0.6 collective-permute-start.22
  62.4 1.0 %collective-permute-start.15 = (bf16[64,384]{1,0:T(8,128)(2,1)S(1)}, bf16[64,384]{1,0:T(8,128)(2,1)S(1)}, u32[]{:S(2)}, u32[]{:S(2)}) collective-permute-start(bf16[64,384]{1,0:T(8,128)(2,1)S(1)} %get-tuple-element.56.refs_0_), channel_id=1, source_target_pairs={{0,2},{1,3},{2,0},{3,1},{4,6},{5,7},{6,4},{7,5},{8,10},{9,11},{10,... | collective-permute-start | bytes 147464 | tf_op jit(solution)/shard_map/ppermute | solution.py:26
  63.4 1.0 %collective-permute-start.16 = (bf16[64,384]{1,0:T(8,128)(2,1)S(1)}, bf16[64,384]{1,0:T(8,128)(2,1)S(1)}, u32[]{:S(2)}, u32[]{:S(2)}) collective-permute-start(bf16[64,384]{1,0:T(8,128)(2,1)S(1)} %get-tuple-element.57), channel_id=1, source_target_pairs={{0,4},{1,5},{2,6},{3,7},{4,0},{5,1},{6,2},{7,3},{8,12},{9,13},{10,... | collective-permute-start | bytes 147464 | tf_op jit(solution)/shard_map/ppermute | solution.py:26
  64.5 2.2 %collective-permute-done.15.refs_1_ = bf16[64,384]{1,0:T(8,128)(2,1)S(1)} collective-permute-done((bf16[64,384]{1,0:T(8,128)(2,1)S(1)}, bf16[64,384]{1,0:T(8,128)(2,1)S(1)}, u32[]{:S(2)}, u32[]{:S(2)}) %collective-permute-start.15) | collective-permute-done | bytes 49184 | tf_op jit(solution)/shard_map/ppermute | solution.py:26
  66.7 1.4 %collective-permute-start.17 = (bf16[64,384]{1,0:T(8,128)(2,1)S(1)}, bf16[64,384]{1,0:T(8,128)(2,1)S(1)}, u32[]{:S(2)}, u32[]{:S(2)}) collective-permute-start(bf16[64,384]{1,0:T(8,128)(2,1)S(1)} %get-tuple-element.57), channel_id=1, source_target_pairs={{0,6},{1,7},{2,4},{3,5},{4,2},{5,3},{6,0},{7,1},{8,14},{9,15},{10,... | collective-permute-start | bytes 147464 | tf_op jit(solution)/shard_map/ppermute | solution.py:26
  68.5 3.2 %collective-permute-done.17.refs_3_ = bf16[64,384]{1,0:T(8,128)(2,1)S(1)} collective-permute-done((bf16[64,384]{1,0:T(8,128)(2,1)S(1)}, bf16[64,384]{1,0:T(8,128)(2,1)S(1)}, u32[]{:S(2)}, u32[]{:S(2)}) %collective-permute-start.17) | collective-permute-done | bytes 49184 | tf_op jit(solution)/shard_map/ppermute | solution.py:26
  72.2 1.5 %assemble.1 = f32[3,256,128]{2,1,0:T(8,128)} custom-call(s32[3]{0:T(128)S(1)} %pad_add_fusion.2.ids, f32[3,64,256]{2,1,0:T(8,128)S(1)} %get-tuple-element.58.mine, f32[3,64,256]{2,1,0:T(8,128)S(1)} %collective-permute-done.22.theirs), custom_call_target="tpu_custom_call" | custom-call | tf_op jit(solution)/shard_map/assemble/pallas_call | solution.py:32
  73.7 1.8 %leaf_transposed.1 = (f32[512,512]{1,0:T(8,128)S(1)}, bf16[512,384]{1,0:T(8,128)(2,1)S(1)}) custom-call(s32[3]{0:T(128)S(1)} %pad_add_fusion.2.ids, bf16[2048,512]{1,0:T(8,128)(2,1)S(1)} %bitcast.14, bf16[384,512]{1,0:T(8,128)(2,1)S(1)} %get-tuple-element.32.weight, bf16[512,512]{1,0:T(8,128)(2,1)S(1)} %get-tuple-element.35.refs_0_, ...), custom_call_target="tpu_custom_call" | custom-call | tf_op jit(solution)/shard_map/leaf_transposed/pallas_call | solution.py:32
  75.6 1.8 %finish.1 = bf16[512,512]{1,0:T(8,128)(2,1)} custom-call(s32[3]{0:T(128)S(1)} %pad_add_fusion.2.ids, f32[512,512]{1,0:T(8,128)S(1)} %get-tuple-element.42.base, bf16[512,384]{1,0:T(8,128)(2,1)S(1)} %get-tuple-element.43.weight_turned, bf16[64,384]{1,0:T(8,128)(2,1)S(1)} %get-tuple-element.56.refs_0_, bf16[64,384]{1,0:T(8,128)(2,1)S(1)} %collective-permute-done.15.refs_1_, ...), custom_call_target="tpu_custom_call" | custom-call | tf_op jit(solution)/shard_map/finish/pallas_call | solution.py:32
  (47 shorter events, 4.5 us)
Async XLA Ops:
  0.7 1.6 %copy-start = (bf16[1,2048,512]{2,1,0:T(8,128)(2,1)S(1)}, bf16[1,2048,512]{2,1,0:T(8,128)(2,1)}, u32[]{:S(2)}) copy-start(bf16[1,2048,512]{2,1,0:T(8,128)(2,1)} %param.9) | copy-start | bytes 6291460
  2.3 1.0 %copy-start.4 = (bf16[1,512,512]{2,1,0:T(8,128)(2,1)S(1)}, bf16[1,512,512]{2,1,0:T(8,128)(2,1)}, u32[]{:S(2)}) copy-start(bf16[1,512,512]{2,1,0:T(8,128)(2,1)} %param.8) | copy-start | bytes 1572868
  3.4 2.3 %copy-start.6 = (bf16[1,3,128,512]{3,2,1,0:T(8,128)(2,1)S(1)}, bf16[1,3,128,512]{3,2,1,0:T(8,128)(2,1)}, u32[]{:S(2)}) copy-start(bf16[1,3,128,512]{3,2,1,0:T(8,128)(2,1)} %param.10) | copy-start | bytes 1179652
  5.2 18.3 %collective-permute-start.3 = (bf16[2,512,512]{2,1,0:T(8,128)(2,1)S(1)}, bf16[2,512,512]{2,1,0:T(8,128)(2,1)S(1)}, u32[]{:S(2)}, u32[]{:S(2)}) collective-permute-start(bf16[2,512,512]{2,1,0:T(8,128)(2,1)S(1)} %get-tuple-element.34), channel_id=1, source_target_pairs={{0,1},{1,0},{2,3},{3,2},{4,5},{5,4},{6,7},{7,6},{8,9},{9,8},{10,11... | collective-permute-start | bytes 3145736 | tf_op jit(solution)/shard_map/ppermute | solution.py:26
  5.7 12.3 %collective-permute-start.1 = (bf16[384,512]{1,0:T(8,128)(2,1)S(1)}, bf16[384,512]{1,0:T(8,128)(2,1)S(1)}, u32[]{:S(2)}, u32[]{:S(2)}) collective-permute-start(bf16[384,512]{1,0:T(8,128)(2,1)S(1)} %bitcast.19), channel_id=1, source_target_pairs={{0,2},{1,3},{2,0},{3,1},{4,6},{5,7},{6,4},{7,5},{8,10},{9,11},{10,... | collective-permute-start | bytes 1179656 | tf_op jit(solution)/shard_map/ppermute | solution.py:26
  8.3 9.7 %collective-permute-start = (bf16[384,512]{1,0:T(8,128)(2,1)S(1)}, bf16[384,512]{1,0:T(8,128)(2,1)S(1)}, u32[]{:S(2)}, u32[]{:S(2)}) collective-permute-start(bf16[384,512]{1,0:T(8,128)(2,1)S(1)} %bitcast.20), channel_id=1, source_target_pairs={{0,1},{1,0},{2,3},{3,2},{4,5},{5,4},{6,7},{7,6},{8,9},{9,8},{10,11... | collective-permute-start | bytes 1179656 | tf_op jit(solution)/shard_map/ppermute | solution.py:26
  18.0 1.7 %collective-permute-start.2 = (bf16[384,512]{1,0:T(8,128)(2,1)S(1)}, bf16[384,512]{1,0:T(8,128)(2,1)S(1)}, u32[]{:S(2)}, u32[]{:S(2)}) collective-permute-start(bf16[384,512]{1,0:T(8,128)(2,1)S(1)} %collective-permute-done.1.refs_0_), channel_id=1, source_target_pairs={{0,1},{1,0},{2,3},{3,2},{4,5},{5,4},{6,7},{7,6},{8,9},{9,8},{10,11... | collective-permute-start | bytes 1179656 | tf_op jit(solution)/shard_map/ppermute | solution.py:26
  21.3 1.5 %collective-permute-start.4 = (bf16[256,384]{1,0:T(8,128)(2,1)S(1)}, bf16[256,384]{1,0:T(8,128)(2,1)S(1)}, u32[]{:S(2)}, u32[]{:S(2)}) collective-permute-start(bf16[256,384]{1,0:T(8,128)(2,1)S(1)} %get-tuple-element.39), channel_id=1, source_target_pairs={{0,1},{1,0},{2,3},{3,2},{4,5},{5,4},{6,7},{7,6},{8,9},{9,8},{10,11... | collective-permute-start | bytes 589832 | tf_op jit(solution)/shard_map/ppermute | solution.py:26
  23.4 15.1 %copy-start.7 = (s32[1,3]{1,0:T(1,128)S(1)}, s32[1,3]{1,0:T(1,128)}, u32[]{:S(2)}) copy-start(s32[1,3]{1,0:T(1,128)} %param.11) | copy-start | bytes 40
  23.4 15.1 %copy-start.8 = (s32[1,3]{1,0:T(1,128)S(1)}, s32[1,3]{1,0:T(1,128)}, u32[]{:S(2)}) copy-start(s32[1,3]{1,0:T(1,128)} %param.12) | copy-start | bytes 40
  23.5 16.9 %copy-start.2 = (f32[1,3,256,512]{3,2,1,0:T(8,128)S(1)}, f32[1,3,256,512]{3,2,1,0:T(8,128)}, u32[]{:S(2)}) copy-start(f32[1,3,256,512]{3,2,1,0:T(8,128)} %param.15) | copy-start | bytes 4718596
  23.5 16.9 %copy-start.3 = (f32[1,3,256,256]{3,2,1,0:T(8,128)S(1)}, f32[1,3,256,256]{3,2,1,0:T(8,128)}, u32[]{:S(2)}) copy-start(f32[1,3,256,256]{3,2,1,0:T(8,128)} %param.13) | copy-start | bytes 2359300
  23.5 16.9 %copy-start.5 = (f32[1,2,256,256]{3,2,1,0:T(8,128)S(1)}, f32[1,2,256,256]{3,2,1,0:T(8,128)}, u32[]{:S(2)}) copy-start(f32[1,2,256,256]{3,2,1,0:T(8,128)} %param.14) | copy-start | bytes 1572868
  24.2 14.1 %collective-permute-start.5 = (bf16[512,512]{1,0:T(8,128)(2,1)S(1)}, bf16[512,512]{1,0:T(8,128)(2,1)S(1)}, u32[]{:S(2)}, u32[]{:S(2)}) collective-permute-start(bf16[512,512]{1,0:T(8,128)(2,1)S(1)} %get-tuple-element.41), channel_id=1, source_target_pairs={{0,2},{1,3},{2,0},{3,1},{4,6},{5,7},{6,4},{7,5},{8,10},{9,11},{10,... | collective-permute-start | bytes 1572872 | tf_op jit(solution)/shard_map/ppermute | solution.py:26
  26.1 46.1 %collective-permute-start.6 = (bf16[512,512]{1,0:T(8,128)(2,1)S(1)}, bf16[512,512]{1,0:T(8,128)(2,1)S(1)}, u32[]{:S(2)}, u32[]{:S(2)}) collective-permute-start(bf16[512,512]{1,0:T(8,128)(2,1)S(1)} %get-tuple-element.35.refs_0_), channel_id=1, source_target_pairs={{0,1},{1,0},{2,3},{3,2},{4,5},{5,4},{6,7},{7,6},{8,9},{9,8},{10,11... | collective-permute-start | bytes 1572872 | tf_op jit(solution)/shard_map/ppermute | solution.py:26
  38.5 35.3 %collective-permute-start.7 = (bf16[512,512]{1,0:T(8,128)(2,1)S(1)}, bf16[512,512]{1,0:T(8,128)(2,1)S(1)}, u32[]{:S(2)}, u32[]{:S(2)}) collective-permute-start(bf16[512,512]{1,0:T(8,128)(2,1)S(1)} %add_convert_fusion.refs_1_), channel_id=1, source_target_pairs={{0,1},{1,0},{2,3},{3,2},{4,5},{5,4},{6,7},{7,6},{8,9},{9,8},{10,11... | collective-permute-start | bytes 1572872 | tf_op jit(solution)/shard_map/ppermute | solution.py:26
  38.6 6.7 %collective-permute-start.8 = (s32[2,3]{1,0:T(2,128)S(1)}, s32[2,3]{1,0:T(2,128)S(1)}, u32[]{:S(2)}, u32[]{:S(2)}) collective-permute-start(s32[2,3]{1,0:T(2,128)S(1)} %pad_add_fusion.1), channel_id=1, source_target_pairs={{0,4},{1,5},{2,6},{3,7},{4,0},{5,1},{6,2},{7,3},{8,12},{9,13},{10,... | collective-permute-start | bytes 80 | tf_op jit(solution)/shard_map/ppermute | solution.py:26
  42.2 31.5 %copy-start.1 = (bf16[1,2048,512]{2,1,0:T(8,128)(2,1)S(1)}, bf16[1,2048,512]{2,1,0:T(8,128)(2,1)}, u32[]{:S(2)}) copy-start(bf16[1,2048,512]{2,1,0:T(8,128)(2,1)} %param.9) | copy-start | bytes 6291460
  42.2 4.3 %collective-permute-start.10 = (bf16[64,384]{1,0:T(8,128)(2,1)S(1)}, bf16[64,384]{1,0:T(8,128)(2,1)S(1)}, u32[]{:S(2)}, u32[]{:S(2)}) collective-permute-start(bf16[64,384]{1,0:T(8,128)(2,1)S(1)} %get-tuple-element.46), channel_id=1, source_target_pairs={{0,4},{1,5},{2,6},{3,7},{4,0},{5,1},{6,2},{7,3},{8,12},{9,13},{10,... | collective-permute-start | bytes 147464 | tf_op jit(solution)/shard_map/ppermute | solution.py:26
  42.6 5.6 %collective-permute-start.11 = (bf16[64,384]{1,0:T(8,128)(2,1)S(1)}, bf16[64,384]{1,0:T(8,128)(2,1)S(1)}, u32[]{:S(2)}, u32[]{:S(2)}) collective-permute-start(bf16[64,384]{1,0:T(8,128)(2,1)S(1)} %get-tuple-element.47), channel_id=1, source_target_pairs={{0,6},{1,7},{2,4},{3,5},{4,2},{5,3},{6,0},{7,1},{8,14},{9,15},{10,... | collective-permute-start | bytes 147464 | tf_op jit(solution)/shard_map/ppermute | solution.py:26
  45.3 4.1 %collective-permute-start.9 = (bf16[64,384]{1,0:T(8,128)(2,1)S(1)}, bf16[64,384]{1,0:T(8,128)(2,1)S(1)}, u32[]{:S(2)}, u32[]{:S(2)}) collective-permute-start(bf16[64,384]{1,0:T(8,128)(2,1)S(1)} %get-tuple-element.45), channel_id=1, source_target_pairs={{0,2},{1,3},{2,0},{3,1},{4,6},{5,7},{6,4},{7,5},{8,10},{9,11},{10,... | collective-permute-start | bytes 147464 | tf_op jit(solution)/shard_map/ppermute | solution.py:26
  50.6 9.9 %collective-permute-start.12 = (bf16[2,64,256]{2,1,0:T(8,128)(2,1)S(1)}, bf16[2,64,256]{2,1,0:T(8,128)(2,1)S(1)}, u32[]{:S(2)}, u32[]{:S(2)}) collective-permute-start(bf16[2,64,256]{2,1,0:T(8,128)(2,1)S(1)} %get-tuple-element.54), channel_id=1, source_target_pairs={{0,8},{1,9},{2,10},{3,11},{4,12},{5,13},{6,14},{7,15},{8,0},{9,1},... | collective-permute-start | bytes 196616 | tf_op jit(solution)/shard_map/ppermute | solution.py:26
  52.2 4.8 %collective-permute-start.13 = (bf16[1,64,256]{2,1,0:T(8,128)(2,1)S(1)}, bf16[1,64,256]{2,1,0:T(8,128)(2,1)S(1)}, u32[]{:S(2)}, u32[]{:S(2)}) collective-permute-start(bf16[1,64,256]{2,1,0:T(8,128)(2,1)S(1)} %get-tuple-element.55), channel_id=1, source_target_pairs={{0,16},{1,17},{2,18},{3,19},{4,20},{5,21},{6,22},{7,23},{8,24},{9,... | collective-permute-start | bytes 98312 | tf_op jit(solution)/shard_map/ppermute | solution.py:26
  54.8 5.7 %collective-permute-start.14 = (bf16[1,64,256]{2,1,0:T(8,128)(2,1)S(1)}, bf16[1,64,256]{2,1,0:T(8,128)(2,1)S(1)}, u32[]{:S(2)}, u32[]{:S(2)}) collective-permute-start(bf16[1,64,256]{2,1,0:T(8,128)(2,1)S(1)} %get-tuple-element.55), channel_id=1, source_target_pairs={{0,24},{1,25},{2,26},{3,27},{4,28},{5,29},{6,30},{7,31},{8,16},{9,... | collective-permute-start | bytes 98312 | tf_op jit(solution)/shard_map/ppermute | solution.py:26
  61.8 9.9 %collective-permute-start.22 = (f32[3,64,256]{2,1,0:T(8,128)S(1)}, f32[3,64,256]{2,1,0:T(8,128)S(1)}, u32[]{:S(2)}, u32[]{:S(2)}) collective-permute-start(f32[3,64,256]{2,1,0:T(8,128)S(1)} %get-tuple-element.59), channel_id=1, source_target_pairs={{0,4},{1,5},{2,6},{3,7},{4,0},{5,1},{6,2},{7,3},{8,12},{9,13},{10,... | collective-permute-start | bytes 589832 | tf_op jit(solution)/shard_map/ppermute | solution.py:26
  62.4 4.2 %collective-permute-start.15 = (bf16[64,384]{1,0:T(8,128)(2,1)S(1)}, bf16[64,384]{1,0:T(8,128)(2,1)S(1)}, u32[]{:S(2)}, u32[]{:S(2)}) collective-permute-start(bf16[64,384]{1,0:T(8,128)(2,1)S(1)} %get-tuple-element.56.refs_0_), channel_id=1, source_target_pairs={{0,2},{1,3},{2,0},{3,1},{4,6},{5,7},{6,4},{7,5},{8,10},{9,11},{10,... | collective-permute-start | bytes 147464 | tf_op jit(solution)/shard_map/ppermute | solution.py:26
  63.4 5.0 %collective-permute-start.16 = (bf16[64,384]{1,0:T(8,128)(2,1)S(1)}, bf16[64,384]{1,0:T(8,128)(2,1)S(1)}, u32[]{:S(2)}, u32[]{:S(2)}) collective-permute-start(bf16[64,384]{1,0:T(8,128)(2,1)S(1)} %get-tuple-element.57), channel_id=1, source_target_pairs={{0,4},{1,5},{2,6},{3,7},{4,0},{5,1},{6,2},{7,3},{8,12},{9,13},{10,... | collective-permute-start | bytes 147464 | tf_op jit(solution)/shard_map/ppermute | solution.py:26
  66.7 5.0 %collective-permute-start.17 = (bf16[64,384]{1,0:T(8,128)(2,1)S(1)}, bf16[64,384]{1,0:T(8,128)(2,1)S(1)}, u32[]{:S(2)}, u32[]{:S(2)}) collective-permute-start(bf16[64,384]{1,0:T(8,128)(2,1)S(1)} %get-tuple-element.57), channel_id=1, source_target_pairs={{0,6},{1,7},{2,4},{3,5},{4,2},{5,3},{6,0},{7,1},{8,14},{9,15},{10,... | collective-permute-start | bytes 147464 | tf_op jit(solution)/shard_map/ppermute | solution.py:26
  68.5 7.1 %collective-permute-start.18 = (bf16[64,384]{1,0:T(8,128)(2,1)S(1)}, bf16[64,384]{1,0:T(8,128)(2,1)S(1)}, u32[]{:S(2)}, u32[]{:S(2)}) collective-permute-start(bf16[64,384]{1,0:T(8,128)(2,1)S(1)} %get-tuple-element.56.refs_0_), channel_id=1, source_target_pairs={{0,1},{1,0},{2,3},{3,2},{4,5},{5,4},{6,7},{7,6},{8,9},{9,8},{10,11... | collective-permute-start | bytes 147464 | tf_op jit(solution)/shard_map/ppermute | solution.py:26
  71.7 3.9 %collective-permute-start.19 = (bf16[64,384]{1,0:T(8,128)(2,1)S(1)}, bf16[64,384]{1,0:T(8,128)(2,1)S(1)}, u32[]{:S(2)}, u32[]{:S(2)}) collective-permute-start(bf16[64,384]{1,0:T(8,128)(2,1)S(1)} %collective-permute-done.15.refs_1_), channel_id=1, source_target_pairs={{0,1},{1,0},{2,3},{3,2},{4,5},{5,4},{6,7},{7,6},{8,9},{9,8},{10,11... | collective-permute-start | bytes 147464 | tf_op jit(solution)/shard_map/ppermute | solution.py:26
  71.7 3.9 %collective-permute-start.20 = (bf16[64,384]{1,0:T(8,128)(2,1)S(1)}, bf16[64,384]{1,0:T(8,128)(2,1)S(1)}, u32[]{:S(2)}, u32[]{:S(2)}) collective-permute-start(bf16[64,384]{1,0:T(8,128)(2,1)S(1)} %collective-permute-done.16.refs_2_), channel_id=1, source_target_pairs={{0,1},{1,0},{2,3},{3,2},{4,5},{5,4},{6,7},{7,6},{8,9},{9,8},{10,11... | collective-permute-start | bytes 147464 | tf_op jit(solution)/shard_map/ppermute | solution.py:26
  72.2 3.4 %collective-permute-start.21 = (bf16[64,384]{1,0:T(8,128)(2,1)S(1)}, bf16[64,384]{1,0:T(8,128)(2,1)S(1)}, u32[]{:S(2)}, u32[]{:S(2)}) collective-permute-start(bf16[64,384]{1,0:T(8,128)(2,1)S(1)} %collective-permute-done.17.refs_3_), channel_id=1, source_target_pairs={{0,1},{1,0},{2,3},{3,2},{4,5},{5,4},{6,7},{7,6},{8,9},{9,8},{10,11... | collective-permute-start | bytes 147464 | tf_op jit(solution)/shard_map/ppermute | solution.py:26

commit v2 on v1

--- a/solution.py
+++ b/solution.py
@@ -36,7 +36,7 @@
         out_specs=[pl.BlockSpec(memory_space=pltpu.VMEM)] * len(outs),
         scratch_shapes=scratch,
         compiler_params=pltpu.CompilerParams(vmem_limit_bytes=limit << 20),
-        cost_estimate=pl.CostEstimate(flops=0, bytes_accessed=0, transcendentals=0),
+        cost_estimate=pl.CostEstimate(flops=5 * 10**9, bytes_accessed=0, transcendentals=0),
         name=getattr(body, "func", body).__name__,
     )(*smem, *vmem)
 

time: 77.6 us -> 55.4 us (0.71)
  waiting for transfers between devices: 38.5 us -> 16.6 us
    ppermute x23, waiting for transfers between devices: 38.5 us -> 16.6 us  [moved(): return lax.ppermute(block, AXES, route)]
  transfers between devices with their start and end apart: 23 -> 23, of which waited for: 12 -> 9; matrix products, arithmetic and copies ran while one was open for 0% -> 0% of each run, Pallas kernels for 14% -> 22%
where the time goes in v2:
time: 55.4 us; the launch traced here: 55.2 us
  starting transfers between devices  19.6 us (35%)
  waiting for transfers between devices  16.6 us (30%)
  Pallas kernels  15.3 us (28%)
  local copies, waits for them, and re-layouts  2.66 us (5%)
  between operations  0.79 us (1%)
    ppermute x23, starting transfers between devices, moved(): return lax.ppermute(block, AXES, route)  19.6 us
    ppermute x23, waiting for transfers between devices, moved(): return lax.ppermute(block, AXES, route)  16.6 us
    pallas_call x11, Pallas kernels, call(): pl.pallas_call(body, out_shape=outs, in_specs=specs, out_specs=[pl.BlockS...  15.3 us
    unnamed x18, local copies, waits for them, and re-layouts  2.66 us
  transfers between devices with their start and end apart: 23, of which 9 were waited for; matrix products, arithmetic and copies ran while one was open for 0% of the time, Pallas kernels for 22%

profile of v2, /device:TPU:0, one launch (start us, length us, event | category | flops | bytes accessed | tf_op | source)
XLA Modules:
  0.0 55.2 jit_solution(12073770230132724460)
XLA Ops:
  1.1 2.6 %collective-permute-start.1 = (bf16[384,512]{1,0:T(8,128)(2,1)}, bf16[384,512]{1,0:T(8,128)(2,1)S(1)}, u32[]{:S(2)}, u32[]{:S(2)}) collective-permute-start(bf16[384,512]{1,0:T(8,128)(2,1)} %bitcast.20), channel_id=1, source_target_pairs={{0,2},{1,3},{2,0},{3,1},{4,6},{5,7},{6,4},{7,5},{8,10},{9,11},{10,... | collective-permute-start | bytes 1179656 | tf_op jit(solution)/shard_map/ppermute | solution.py:26
  3.8 1.6 %copy-done = bf16[1,2048,512]{2,1,0:T(8,128)(2,1)S(1)} copy-done((bf16[1,2048,512]{2,1,0:T(8,128)(2,1)S(1)}, bf16[1,2048,512]{2,1,0:T(8,128)(2,1)}, u32[]{:S(2)}) %copy-start) | copy-done | bytes 2097176
  5.4 1.0 %copy-done.4 = bf16[1,512,512]{2,1,0:T(8,128)(2,1)S(1)} copy-done((bf16[1,512,512]{2,1,0:T(8,128)(2,1)S(1)}, bf16[1,512,512]{2,1,0:T(8,128)(2,1)}, u32[]{:S(2)}) %copy-start.4) | copy-done | bytes 524312
  6.5 1.8 %leaf_products.1 = (f32[2,512,512]{2,1,0:T(8,128)S(1)}, bf16[512,512]{1,0:T(8,128)(2,1)S(1)}, bf16[2,512,512]{2,1,0:T(8,128)(2,1)S(1)}) custom-call(s32[3]{0:T(128)S(1)} %pad_add_fusion.2.ids, bf16[2048,512]{1,0:T(8,128)(2,1)S(1)} %bitcast.11, bf16[512,512]{1,0:T(8,128)(2,1)S(1)} %bitcast.17), custom_call_target="tpu_custom_call" | custom-call | flops 5000000000 | tf_op jit(solution)/shard_map/leaf_products/pallas_call | solution.py:32
  8.5 1.6 %collective-permute-start.8 = (s32[2,3]{1,0:T(2,128)S(1)}, s32[2,3]{1,0:T(2,128)S(1)}, u32[]{:S(2)}, u32[]{:S(2)}) collective-permute-start(s32[2,3]{1,0:T(2,128)S(1)} %pad_add_fusion.1), channel_id=1, source_target_pairs={{0,4},{1,5},{2,6},{3,7},{4,0},{5,1},{6,2},{7,3},{8,12},{9,13},{10,... | collective-permute-start | bytes 80 | tf_op jit(solution)/shard_map/ppermute | solution.py:26
  10.1 3.6 %collective-permute-done.1.refs_0_ = bf16[384,512]{1,0:T(8,128)(2,1)S(1)} collective-permute-done((bf16[384,512]{1,0:T(8,128)(2,1)}, bf16[384,512]{1,0:T(8,128)(2,1)S(1)}, u32[]{:S(2)}, u32[]{:S(2)}) %collective-permute-start.1) | collective-permute-done | bytes 393248 | tf_op jit(solution)/shard_map/ppermute | solution.py:26
  13.7 1.1 %panel_products.1.early = f32[384,512]{1,0:T(8,128)S(1)} custom-call(s32[3]{0:T(128)S(1)} %pad_add_fusion.2.ids, bf16[2048,512]{1,0:T(8,128)(2,1)S(1)} %bitcast.12, bf16[384,512]{1,0:T(8,128)(2,1)S(1)} %bitcast.21, bf16[384,512]{1,0:T(8,128)(2,1)S(1)} %collective-permute-done.refs_1_), custom_call_target="tpu_custom_call" | custom-call | flops 5000000000 | tf_op jit(solution)/shard_map/panel_products/pallas_call | solution.py:32
  14.8 0.6 %collective-permute-done.2.refs_1_ = bf16[384,512]{1,0:T(8,128)(2,1)S(1)} collective-permute-done((bf16[384,512]{1,0:T(8,128)(2,1)S(1)}, bf16[384,512]{1,0:T(8,128)(2,1)S(1)}, u32[]{:S(2)}, u32[]{:S(2)}) %collective-permute-start.2) | collective-permute-done | bytes 393248 | tf_op jit(solution)/shard_map/ppermute | solution.py:26
  15.4 1.6 %partials.1 = (bf16[384,512]{1,0:T(8,128)(2,1)S(1)}, f32[256,384]{1,0:T(8,128)S(1)}, bf16[256,384]{1,0:T(8,128)(2,1)S(1)}) custom-call(s32[3]{0:T(128)S(1)} %pad_add_fusion.2.ids, bf16[2048,512]{1,0:T(8,128)(2,1)S(1)} %bitcast.13, f32[384,512]{1,0:T(8,128)S(1)} %panel_products.1.early, bf16[512,512]{1,0:T(8,128)(2,1)S(1)} %get-tuple-element.31.turned, ...), custom_call_target="tpu_custom_call" | custom-call | flops 5000000000 | tf_op jit(solution)/shard_map/partials/pallas_call | solution.py:32
  17.2 1.9 %prepare.1 = (bf16[3,256,256]{2,1,0:T(8,128)(2,1)S(1)}, bf16[3,256,256]{2,1,0:T(8,128)(2,1)S(1)}, bf16[2,256,256]{2,1,0:T(8,128)(2,1)S(1)}, bf16[2,256,256]{2,1,0:T(8,128)(2,1)S(1)}, f32[3,64,256]{2,1,0:T(8,128)S(1)}) custom-call(s32[3]{0:T(128)S(1)} %pad_add_fusion.2.ids, f32[3,256,256]{2,1,0:T(8,128)S(1)} %bitcast.16, f32[2,256,256]{2,1,0:T(8,128)S(1)} %bitcast.18, ...), custom_call_target="tpu_custom_call" | custom-call | flops 5000000000 | tf_op jit(solution)/shard_map/prepare/pallas_call | solution.py:32
  19.7 1.8 %collective-permute-start.10 = (bf16[64,384]{1,0:T(8,128)(2,1)S(1)}, bf16[64,384]{1,0:T(8,128)(2,1)S(1)}, u32[]{:S(2)}, u32[]{:S(2)}) collective-permute-start(bf16[64,384]{1,0:T(8,128)(2,1)S(1)} %get-tuple-element.46), channel_id=1, source_target_pairs={{0,4},{1,5},{2,6},{3,7},{4,0},{5,1},{6,2},{7,3},{8,12},{9,13},{10,... | collective-permute-start | bytes 147464 | tf_op jit(solution)/shard_map/ppermute | solution.py:26
  21.6 1.5 %collective-permute-start.11 = (bf16[64,384]{1,0:T(8,128)(2,1)S(1)}, bf16[64,384]{1,0:T(8,128)(2,1)S(1)}, u32[]{:S(2)}, u32[]{:S(2)}) collective-permute-start(bf16[64,384]{1,0:T(8,128)(2,1)S(1)} %get-tuple-element.47), channel_id=1, source_target_pairs={{0,6},{1,7},{2,4},{3,5},{4,2},{5,3},{6,0},{7,1},{8,14},{9,15},{10,... | collective-permute-start | bytes 147464 | tf_op jit(solution)/shard_map/ppermute | solution.py:26
  23.3 0.7 %add_products.1 = (bf16[512,512]{1,0:T(8,128)(2,1)S(1)}, bf16[512,512]{1,0:T(8,128)(2,1)S(1)}, f32[512,512]{1,0:T(8,128)S(1)}) custom-call(s32[3]{0:T(128)S(1)} %pad_add_fusion.2.ids, f32[2,512,512]{2,1,0:T(8,128)S(1)} %get-tuple-element.33.keep, bf16[2,512,512]{2,1,0:T(8,128)(2,1)S(1)} %collective-permute-done.3.refs_0_), custom_call_target="tpu_custom_call" | custom-call | flops 5000000000 | tf_op jit(solution)/shard_map/add_products/pallas_call | solution.py:32
  24.1 2.5 %collective-permute-done.11.cross = bf16[64,384]{1,0:T(8,128)(2,1)S(1)} collective-permute-done((bf16[64,384]{1,0:T(8,128)(2,1)S(1)}, bf16[64,384]{1,0:T(8,128)(2,1)S(1)}, u32[]{:S(2)}, u32[]{:S(2)}) %collective-permute-start.11) | collective-permute-done | bytes 49184 | tf_op jit(solution)/shard_map/ppermute | solution.py:26
  26.6 0.6 %collective-permute-done.9.same = bf16[64,384]{1,0:T(8,128)(2,1)S(1)} collective-permute-done((bf16[64,384]{1,0:T(8,128)(2,1)S(1)}, bf16[64,384]{1,0:T(8,128)(2,1)S(1)}, u32[]{:S(2)}, u32[]{:S(2)}) %collective-permute-start.9) | collective-permute-done | bytes 49184 | tf_op jit(solution)/shard_map/ppermute | solution.py:26
  27.2 1.2 %upward.1 = (f32[3,64,256]{2,1,0:T(8,128)S(1)}, bf16[2,64,256]{2,1,0:T(8,128)(2,1)S(1)}, bf16[1,64,256]{2,1,0:T(8,128)(2,1)S(1)}) custom-call(s32[3]{0:T(128)S(1)} %pad_add_fusion.2.ids, s32[4,3]{1,0:T(4,128)S(1)} %pad_add_fusion.spots, f32[64,384]{1,0:T(8,128)S(1)} %get-tuple-element.44.own, bf16[64,384]{1,0:T(8,128)(2,1)S(1)} %collective-permute-done.9.same, ...), custom_call_target="tpu_custom_call" | custom-call | flops 5000000000 | tf_op jit(solution)/shard_map/upward/pallas_call | solution.py:32
  28.4 1.6 %collective-permute-start.12 = (bf16[2,64,256]{2,1,0:T(8,128)(2,1)S(1)}, bf16[2,64,256]{2,1,0:T(8,128)(2,1)S(1)}, u32[]{:S(2)}, u32[]{:S(2)}) collective-permute-start(bf16[2,64,256]{2,1,0:T(8,128)(2,1)S(1)} %get-tuple-element.54), channel_id=1, source_target_pairs={{0,8},{1,9},{2,10},{3,11},{4,12},{5,13},{6,14},{7,15},{8,0},{9,1},... | collective-permute-start | bytes 196616 | tf_op jit(solution)/shard_map/ppermute | solution.py:26
  30.1 1.0 %collective-permute-start.5 = (bf16[512,512]{1,0:T(8,128)(2,1)S(1)}, bf16[512,512]{1,0:T(8,128)(2,1)S(1)}, u32[]{:S(2)}, u32[]{:S(2)}) collective-permute-start(bf16[512,512]{1,0:T(8,128)(2,1)S(1)} %get-tuple-element.41), channel_id=1, source_target_pairs={{0,2},{1,3},{2,0},{3,1},{4,6},{5,7},{6,4},{7,5},{8,10},{9,11},{10,... | collective-permute-start | bytes 1572872 | tf_op jit(solution)/shard_map/ppermute | solution.py:26
  31.1 2.6 %collective-permute-start.13 = (bf16[1,64,256]{2,1,0:T(8,128)(2,1)S(1)}, bf16[1,64,256]{2,1,0:T(8,128)(2,1)S(1)}, u32[]{:S(2)}, u32[]{:S(2)}) collective-permute-start(bf16[1,64,256]{2,1,0:T(8,128)(2,1)S(1)} %get-tuple-element.55), channel_id=1, source_target_pairs={{0,16},{1,17},{2,18},{3,19},{4,20},{5,21},{6,22},{7,23},{8,24},{9,... | collective-permute-start | bytes 98312 | tf_op jit(solution)/shard_map/ppermute | solution.py:26
  33.9 2.2 %collective-permute-done.13.refs_1_ = bf16[1,64,256]{2,1,0:T(8,128)(2,1)S(1)} collective-permute-done((bf16[1,64,256]{2,1,0:T(8,128)(2,1)S(1)}, bf16[1,64,256]{2,1,0:T(8,128)(2,1)S(1)}, u32[]{:S(2)}, u32[]{:S(2)}) %collective-permute-start.13) | collective-permute-done | bytes 32800 | tf_op jit(solution)/shard_map/ppermute | solution.py:26
  36.1 3.3 %collective-permute-done.14.refs_2_ = bf16[1,64,256]{2,1,0:T(8,128)(2,1)S(1)} collective-permute-done((bf16[1,64,256]{2,1,0:T(8,128)(2,1)S(1)}, bf16[1,64,256]{2,1,0:T(8,128)(2,1)S(1)}, u32[]{:S(2)}, u32[]{:S(2)}) %collective-permute-start.14) | collective-permute-done | bytes 32800 | tf_op jit(solution)/shard_map/ppermute | solution.py:26
  39.4 1.3 %downward.1 = (f32[3,64,256]{2,1,0:T(8,128)S(1)}, f32[3,64,256]{2,1,0:T(8,128)S(1)}, bf16[64,384]{1,0:T(8,128)(2,1)S(1)}, bf16[64,384]{1,0:T(8,128)(2,1)S(1)}) custom-call(s32[3]{0:T(128)S(1)} %pad_add_fusion.2.ids, s32[4,3]{1,0:T(4,128)S(1)} %pad_add_fusion.spots, f32[3,64,256]{2,1,0:T(8,128)S(1)} %get-tuple-element.51.kept, ...), custom_call_target="tpu_custom_call" | custom-call | flops 5000000000 | tf_op jit(solution)/shard_map/downward/pallas_call | solution.py:32
  40.6 1.1 %collective-permute-start.22 = (f32[3,64,256]{2,1,0:T(8,128)S(1)}, f32[3,64,256]{2,1,0:T(8,128)S(1)}, u32[]{:S(2)}, u32[]{:S(2)}) collective-permute-start(f32[3,64,256]{2,1,0:T(8,128)S(1)} %get-tuple-element.59), channel_id=1, source_target_pairs={{0,4},{1,5},{2,6},{3,7},{4,0},{5,1},{6,2},{7,3},{8,12},{9,13},{10,... | collective-permute-start | bytes 589832 | tf_op jit(solution)/shard_map/ppermute | solution.py:26
  41.8 1.5 %collective-permute-done.5 = bf16[512,512]{1,0:T(8,128)(2,1)S(1)} collective-permute-done((bf16[512,512]{1,0:T(8,128)(2,1)S(1)}, bf16[512,512]{1,0:T(8,128)(2,1)S(1)}, u32[]{:S(2)}, u32[]{:S(2)}) %collective-permute-start.5) | collective-permute-done | bytes 524320 | tf_op jit(solution)/shard_map/ppermute | solution.py:26
  43.5 1.0 %collective-permute-start.16 = (bf16[64,384]{1,0:T(8,128)(2,1)S(1)}, bf16[64,384]{1,0:T(8,128)(2,1)S(1)}, u32[]{:S(2)}, u32[]{:S(2)}) collective-permute-start(bf16[64,384]{1,0:T(8,128)(2,1)S(1)} %get-tuple-element.57), channel_id=1, source_target_pairs={{0,4},{1,5},{2,6},{3,7},{4,0},{5,1},{6,2},{7,3},{8,12},{9,13},{10,... | collective-permute-start | bytes 147464 | tf_op jit(solution)/shard_map/ppermute | solution.py:26
  44.5 0.8 %collective-permute-start.17 = (bf16[64,384]{1,0:T(8,128)(2,1)S(1)}, bf16[64,384]{1,0:T(8,128)(2,1)S(1)}, u32[]{:S(2)}, u32[]{:S(2)}) collective-permute-start(bf16[64,384]{1,0:T(8,128)(2,1)S(1)} %get-tuple-element.57), channel_id=1, source_target_pairs={{0,6},{1,7},{2,4},{3,5},{4,2},{5,3},{6,0},{7,1},{8,14},{9,15},{10,... | collective-permute-start | bytes 147464 | tf_op jit(solution)/shard_map/ppermute | solution.py:26
  45.3 1.0 %collective-permute-done.22.theirs = f32[3,64,256]{2,1,0:T(8,128)S(1)} collective-permute-done((f32[3,64,256]{2,1,0:T(8,128)S(1)}, f32[3,64,256]{2,1,0:T(8,128)S(1)}, u32[]{:S(2)}, u32[]{:S(2)}) %collective-permute-start.22) | collective-permute-done | bytes 196640 | tf_op jit(solution)/shard_map/ppermute | solution.py:26
  46.4 1.4 %collective-permute-start.15 = (bf16[64,384]{1,0:T(8,128)(2,1)S(1)}, bf16[64,384]{1,0:T(8,128)(2,1)S(1)}, u32[]{:S(2)}, u32[]{:S(2)}) collective-permute-start(bf16[64,384]{1,0:T(8,128)(2,1)S(1)} %get-tuple-element.56.refs_0_), channel_id=1, source_target_pairs={{0,2},{1,3},{2,0},{3,1},{4,6},{5,7},{6,4},{7,5},{8,10},{9,11},{10,... | collective-permute-start | bytes 147464 | tf_op jit(solution)/shard_map/ppermute | solution.py:26
  47.8 1.5 %assemble.1 = f32[3,256,128]{2,1,0:T(8,128)} custom-call(s32[3]{0:T(128)S(1)} %pad_add_fusion.2.ids, f32[3,64,256]{2,1,0:T(8,128)S(1)} %get-tuple-element.58.mine, f32[3,64,256]{2,1,0:T(8,128)S(1)} %collective-permute-done.22.theirs), custom_call_target="tpu_custom_call" | custom-call | flops 5000000000 | tf_op jit(solution)/shard_map/assemble/pallas_call | solution.py:32
  49.3 1.2 %collective-permute-done.15.refs_1_ = bf16[64,384]{1,0:T(8,128)(2,1)S(1)} collective-permute-done((bf16[64,384]{1,0:T(8,128)(2,1)S(1)}, bf16[64,384]{1,0:T(8,128)(2,1)S(1)}, u32[]{:S(2)}, u32[]{:S(2)}) %collective-permute-start.15) | collective-permute-done | bytes 49184 | tf_op jit(solution)/shard_map/ppermute | solution.py:26
  51.5 1.8 %leaf_transposed.1 = (f32[512,512]{1,0:T(8,128)S(1)}, bf16[512,384]{1,0:T(8,128)(2,1)S(1)}) custom-call(s32[3]{0:T(128)S(1)} %pad_add_fusion.2.ids, bf16[2048,512]{1,0:T(8,128)(2,1)S(1)} %bitcast.14, bf16[384,512]{1,0:T(8,128)(2,1)S(1)} %get-tuple-element.32.weight, bf16[512,512]{1,0:T(8,128)(2,1)S(1)} %get-tuple-element.35.refs_0_, ...), custom_call_target="tpu_custom_call" | custom-call | flops 5000000000 | tf_op jit(solution)/shard_map/leaf_transposed/pallas_call | solution.py:32
  53.4 1.8 %finish.1 = bf16[512,512]{1,0:T(8,128)(2,1)} custom-call(s32[3]{0:T(128)S(1)} %pad_add_fusion.2.ids, f32[512,512]{1,0:T(8,128)S(1)} %get-tuple-element.42.base, bf16[512,384]{1,0:T(8,128)(2,1)S(1)} %get-tuple-element.43.weight_turned, bf16[64,384]{1,0:T(8,128)(2,1)S(1)} %get-tuple-element.56.refs_0_, bf16[64,384]{1,0:T(8,128)(2,1)S(1)} %collective-permute-done.15.refs_1_, ...), custom_call_target="tpu_custom_call" | custom-call | flops 5000000000 | tf_op jit(solution)/shard_map/finish/pallas_call | solution.py:32
  (47 shorter events, 3.5 us)
Async XLA Ops:
  0.6 13.0 %collective-permute-start = (bf16[384,512]{1,0:T(8,128)(2,1)}, bf16[384,512]{1,0:T(8,128)(2,1)S(1)}, u32[]{:S(2)}, u32[]{:S(2)}) collective-permute-start(bf16[384,512]{1,0:T(8,128)(2,1)} %bitcast.19), channel_id=1, source_target_pairs={{0,1},{1,0},{2,3},{3,2},{4,5},{5,4},{6,7},{7,6},{8,9},{9,8},{10,11... | collective-permute-start | bytes 1179656 | tf_op jit(solution)/shard_map/ppermute | solution.py:26
  1.1 12.5 %collective-permute-start.1 = (bf16[384,512]{1,0:T(8,128)(2,1)}, bf16[384,512]{1,0:T(8,128)(2,1)S(1)}, u32[]{:S(2)}, u32[]{:S(2)}) collective-permute-start(bf16[384,512]{1,0:T(8,128)(2,1)} %bitcast.20), channel_id=1, source_target_pairs={{0,2},{1,3},{2,0},{3,1},{4,6},{5,7},{6,4},{7,5},{8,10},{9,11},{10,... | collective-permute-start | bytes 1179656 | tf_op jit(solution)/shard_map/ppermute | solution.py:26
  3.8 1.6 %copy-start = (bf16[1,2048,512]{2,1,0:T(8,128)(2,1)S(1)}, bf16[1,2048,512]{2,1,0:T(8,128)(2,1)}, u32[]{:S(2)}) copy-start(bf16[1,2048,512]{2,1,0:T(8,128)(2,1)} %param.9) | copy-start | bytes 6291460
  5.4 1.0 %copy-start.4 = (bf16[1,512,512]{2,1,0:T(8,128)(2,1)S(1)}, bf16[1,512,512]{2,1,0:T(8,128)(2,1)}, u32[]{:S(2)}) copy-start(bf16[1,512,512]{2,1,0:T(8,128)(2,1)} %param.8) | copy-start | bytes 1572868
  6.5 2.0 %copy-start.7 = (s32[1,3]{1,0:T(1,128)S(1)}, s32[1,3]{1,0:T(1,128)}, u32[]{:S(2)}) copy-start(s32[1,3]{1,0:T(1,128)} %param.11) | copy-start | bytes 40
  6.5 2.0 %copy-start.8 = (s32[1,3]{1,0:T(1,128)S(1)}, s32[1,3]{1,0:T(1,128)}, u32[]{:S(2)}) copy-start(s32[1,3]{1,0:T(1,128)} %param.12) | copy-start | bytes 40
  6.5 7.2 %copy-start.6 = (bf16[1,3,128,512]{3,2,1,0:T(8,128)(2,1)S(1)}, bf16[1,3,128,512]{3,2,1,0:T(8,128)(2,1)}, u32[]{:S(2)}) copy-start(bf16[1,3,128,512]{3,2,1,0:T(8,128)(2,1)} %param.10) | copy-start | bytes 1179652
  8.3 15.1 %collective-permute-start.3 = (bf16[2,512,512]{2,1,0:T(8,128)(2,1)S(1)}, bf16[2,512,512]{2,1,0:T(8,128)(2,1)S(1)}, u32[]{:S(2)}, u32[]{:S(2)}) collective-permute-start(bf16[2,512,512]{2,1,0:T(8,128)(2,1)S(1)} %get-tuple-element.34), channel_id=1, source_target_pairs={{0,1},{1,0},{2,3},{3,2},{4,5},{5,4},{6,7},{7,6},{8,9},{9,8},{10,11... | collective-permute-start | bytes 3145736 | tf_op jit(solution)/shard_map/ppermute | solution.py:26
  8.5 10.6 %collective-permute-start.8 = (s32[2,3]{1,0:T(2,128)S(1)}, s32[2,3]{1,0:T(2,128)S(1)}, u32[]{:S(2)}, u32[]{:S(2)}) collective-permute-start(s32[2,3]{1,0:T(2,128)S(1)} %pad_add_fusion.1), channel_id=1, source_target_pairs={{0,4},{1,5},{2,6},{3,7},{4,0},{5,1},{6,2},{7,3},{8,12},{9,13},{10,... | collective-permute-start | bytes 80 | tf_op jit(solution)/shard_map/ppermute | solution.py:26
  13.7 1.7 %collective-permute-start.2 = (bf16[384,512]{1,0:T(8,128)(2,1)S(1)}, bf16[384,512]{1,0:T(8,128)(2,1)S(1)}, u32[]{:S(2)}, u32[]{:S(2)}) collective-permute-start(bf16[384,512]{1,0:T(8,128)(2,1)S(1)} %collective-permute-done.1.refs_0_), channel_id=1, source_target_pairs={{0,1},{1,0},{2,3},{3,2},{4,5},{5,4},{6,7},{7,6},{8,9},{9,8},{10,11... | collective-permute-start | bytes 1179656 | tf_op jit(solution)/shard_map/ppermute | solution.py:26
  15.4 1.9 %copy-start.2 = (f32[1,3,256,512]{3,2,1,0:T(8,128)S(1)}, f32[1,3,256,512]{3,2,1,0:T(8,128)}, u32[]{:S(2)}) copy-start(f32[1,3,256,512]{3,2,1,0:T(8,128)} %param.15) | copy-start | bytes 4718596
  15.4 1.9 %copy-start.3 = (f32[1,3,256,256]{3,2,1,0:T(8,128)S(1)}, f32[1,3,256,256]{3,2,1,0:T(8,128)}, u32[]{:S(2)}) copy-start(f32[1,3,256,256]{3,2,1,0:T(8,128)} %param.13) | copy-start | bytes 2359300
  15.4 1.9 %copy-start.5 = (f32[1,2,256,256]{3,2,1,0:T(8,128)S(1)}, f32[1,2,256,256]{3,2,1,0:T(8,128)}, u32[]{:S(2)}) copy-start(f32[1,2,256,256]{3,2,1,0:T(8,128)} %param.14) | copy-start | bytes 1572868
  17.0 2.1 %collective-permute-start.4 = (bf16[256,384]{1,0:T(8,128)(2,1)S(1)}, bf16[256,384]{1,0:T(8,128)(2,1)S(1)}, u32[]{:S(2)}, u32[]{:S(2)}) collective-permute-start(bf16[256,384]{1,0:T(8,128)(2,1)S(1)} %get-tuple-element.39), channel_id=1, source_target_pairs={{0,1},{1,0},{2,3},{3,2},{4,5},{5,4},{6,7},{7,6},{8,9},{9,8},{10,11... | collective-permute-start | bytes 589832 | tf_op jit(solution)/shard_map/ppermute | solution.py:26
  19.7 4.3 %collective-permute-start.10 = (bf16[64,384]{1,0:T(8,128)(2,1)S(1)}, bf16[64,384]{1,0:T(8,128)(2,1)S(1)}, u32[]{:S(2)}, u32[]{:S(2)}) collective-permute-start(bf16[64,384]{1,0:T(8,128)(2,1)S(1)} %get-tuple-element.46), channel_id=1, source_target_pairs={{0,4},{1,5},{2,6},{3,7},{4,0},{5,1},{6,2},{7,3},{8,12},{9,13},{10,... | collective-permute-start | bytes 147464 | tf_op jit(solution)/shard_map/ppermute | solution.py:26
  21.6 5.0 %collective-permute-start.11 = (bf16[64,384]{1,0:T(8,128)(2,1)S(1)}, bf16[64,384]{1,0:T(8,128)(2,1)S(1)}, u32[]{:S(2)}, u32[]{:S(2)}) collective-permute-start(bf16[64,384]{1,0:T(8,128)(2,1)S(1)} %get-tuple-element.47), channel_id=1, source_target_pairs={{0,6},{1,7},{2,4},{3,5},{4,2},{5,3},{6,0},{7,1},{8,14},{9,15},{10,... | collective-permute-start | bytes 147464 | tf_op jit(solution)/shard_map/ppermute | solution.py:26
  23.0 4.2 %collective-permute-start.9 = (bf16[64,384]{1,0:T(8,128)(2,1)S(1)}, bf16[64,384]{1,0:T(8,128)(2,1)S(1)}, u32[]{:S(2)}, u32[]{:S(2)}) collective-permute-start(bf16[64,384]{1,0:T(8,128)(2,1)S(1)} %get-tuple-element.45), channel_id=1, source_target_pairs={{0,2},{1,3},{2,0},{3,1},{4,6},{5,7},{6,4},{7,5},{8,10},{9,11},{10,... | collective-permute-start | bytes 147464 | tf_op jit(solution)/shard_map/ppermute | solution.py:26
  28.4 10.9 %collective-permute-start.12 = (bf16[2,64,256]{2,1,0:T(8,128)(2,1)S(1)}, bf16[2,64,256]{2,1,0:T(8,128)(2,1)S(1)}, u32[]{:S(2)}, u32[]{:S(2)}) collective-permute-start(bf16[2,64,256]{2,1,0:T(8,128)(2,1)S(1)} %get-tuple-element.54), channel_id=1, source_target_pairs={{0,8},{1,9},{2,10},{3,11},{4,12},{5,13},{6,14},{7,15},{8,0},{9,1},... | collective-permute-start | bytes 196616 | tf_op jit(solution)/shard_map/ppermute | solution.py:26
  30.1 13.2 %collective-permute-start.5 = (bf16[512,512]{1,0:T(8,128)(2,1)S(1)}, bf16[512,512]{1,0:T(8,128)(2,1)S(1)}, u32[]{:S(2)}, u32[]{:S(2)}) collective-permute-start(bf16[512,512]{1,0:T(8,128)(2,1)S(1)} %get-tuple-element.41), channel_id=1, source_target_pairs={{0,2},{1,3},{2,0},{3,1},{4,6},{5,7},{6,4},{7,5},{8,10},{9,11},{10,... | collective-permute-start | bytes 1572872 | tf_op jit(solution)/shard_map/ppermute | solution.py:26
  31.1 5.1 %collective-permute-start.13 = (bf16[1,64,256]{2,1,0:T(8,128)(2,1)S(1)}, bf16[1,64,256]{2,1,0:T(8,128)(2,1)S(1)}, u32[]{:S(2)}, u32[]{:S(2)}) collective-permute-start(bf16[1,64,256]{2,1,0:T(8,128)(2,1)S(1)} %get-tuple-element.55), channel_id=1, source_target_pairs={{0,16},{1,17},{2,18},{3,19},{4,20},{5,21},{6,22},{7,23},{8,24},{9,... | collective-permute-start | bytes 98312 | tf_op jit(solution)/shard_map/ppermute | solution.py:26
  33.6 5.7 %collective-permute-start.14 = (bf16[1,64,256]{2,1,0:T(8,128)(2,1)S(1)}, bf16[1,64,256]{2,1,0:T(8,128)(2,1)S(1)}, u32[]{:S(2)}, u32[]{:S(2)}) collective-permute-start(bf16[1,64,256]{2,1,0:T(8,128)(2,1)S(1)} %get-tuple-element.55), channel_id=1, source_target_pairs={{0,24},{1,25},{2,26},{3,27},{4,28},{5,29},{6,30},{7,31},{8,16},{9,... | collective-permute-start | bytes 98312 | tf_op jit(solution)/shard_map/ppermute | solution.py:26
  33.9 17.2 %collective-permute-start.6 = (bf16[512,512]{1,0:T(8,128)(2,1)S(1)}, bf16[512,512]{1,0:T(8,128)(2,1)S(1)}, u32[]{:S(2)}, u32[]{:S(2)}) collective-permute-start(bf16[512,512]{1,0:T(8,128)(2,1)S(1)} %get-tuple-element.35.refs_0_), channel_id=1, source_target_pairs={{0,1},{1,0},{2,3},{3,2},{4,5},{5,4},{6,7},{7,6},{8,9},{9,8},{10,11... | collective-permute-start | bytes 1572872 | tf_op jit(solution)/shard_map/ppermute | solution.py:26
  40.6 5.7 %collective-permute-start.22 = (f32[3,64,256]{2,1,0:T(8,128)S(1)}, f32[3,64,256]{2,1,0:T(8,128)S(1)}, u32[]{:S(2)}, u32[]{:S(2)}) collective-permute-start(f32[3,64,256]{2,1,0:T(8,128)S(1)} %get-tuple-element.59), channel_id=1, source_target_pairs={{0,4},{1,5},{2,6},{3,7},{4,0},{5,1},{6,2},{7,3},{8,12},{9,13},{10,... | collective-permute-start | bytes 589832 | tf_op jit(solution)/shard_map/ppermute | solution.py:26
  43.4 8.0 %collective-permute-start.7 = (bf16[512,512]{1,0:T(8,128)(2,1)S(1)}, bf16[512,512]{1,0:T(8,128)(2,1)S(1)}, u32[]{:S(2)}, u32[]{:S(2)}) collective-permute-start(bf16[512,512]{1,0:T(8,128)(2,1)S(1)} %add_convert_fusion.refs_1_), channel_id=1, source_target_pairs={{0,1},{1,0},{2,3},{3,2},{4,5},{5,4},{6,7},{7,6},{8,9},{9,8},{10,11... | collective-permute-start | bytes 1572872 | tf_op jit(solution)/shard_map/ppermute | solution.py:26
  43.5 6.9 %collective-permute-start.16 = (bf16[64,384]{1,0:T(8,128)(2,1)S(1)}, bf16[64,384]{1,0:T(8,128)(2,1)S(1)}, u32[]{:S(2)}, u32[]{:S(2)}) collective-permute-start(bf16[64,384]{1,0:T(8,128)(2,1)S(1)} %get-tuple-element.57), channel_id=1, source_target_pairs={{0,4},{1,5},{2,6},{3,7},{4,0},{5,1},{6,2},{7,3},{8,12},{9,13},{10,... | collective-permute-start | bytes 147464 | tf_op jit(solution)/shard_map/ppermute | solution.py:26
  44.5 6.4 %collective-permute-start.17 = (bf16[64,384]{1,0:T(8,128)(2,1)S(1)}, bf16[64,384]{1,0:T(8,128)(2,1)S(1)}, u32[]{:S(2)}, u32[]{:S(2)}) collective-permute-start(bf16[64,384]{1,0:T(8,128)(2,1)S(1)} %get-tuple-element.57), channel_id=1, source_target_pairs={{0,6},{1,7},{2,4},{3,5},{4,2},{5,3},{6,0},{7,1},{8,14},{9,15},{10,... | collective-permute-start | bytes 147464 | tf_op jit(solution)/shard_map/ppermute | solution.py:26
  46.4 4.1 %collective-permute-start.15 = (bf16[64,384]{1,0:T(8,128)(2,1)S(1)}, bf16[64,384]{1,0:T(8,128)(2,1)S(1)}, u32[]{:S(2)}, u32[]{:S(2)}) collective-permute-start(bf16[64,384]{1,0:T(8,128)(2,1)S(1)} %get-tuple-element.56.refs_0_), channel_id=1, source_target_pairs={{0,2},{1,3},{2,0},{3,1},{4,6},{5,7},{6,4},{7,5},{8,10},{9,11},{10,... | collective-permute-start | bytes 147464 | tf_op jit(solution)/shard_map/ppermute | solution.py:26
  47.8 3.7 %copy-start.1 = (bf16[1,2048,512]{2,1,0:T(8,128)(2,1)S(1)}, bf16[1,2048,512]{2,1,0:T(8,128)(2,1)}, u32[]{:S(2)}) copy-start(bf16[1,2048,512]{2,1,0:T(8,128)(2,1)} %param.9) | copy-start | bytes 6291460
  50.5 2.9 %collective-permute-start.18 = (bf16[64,384]{1,0:T(8,128)(2,1)S(1)}, bf16[64,384]{1,0:T(8,128)(2,1)S(1)}, u32[]{:S(2)}, u32[]{:S(2)}) collective-permute-start(bf16[64,384]{1,0:T(8,128)(2,1)S(1)} %get-tuple-element.56.refs_0_), channel_id=1, source_target_pairs={{0,1},{1,0},{2,3},{3,2},{4,5},{5,4},{6,7},{7,6},{8,9},{9,8},{10,11... | collective-permute-start | bytes 147464 | tf_op jit(solution)/shard_map/ppermute | solution.py:26
  50.5 2.9 %collective-permute-start.19 = (bf16[64,384]{1,0:T(8,128)(2,1)S(1)}, bf16[64,384]{1,0:T(8,128)(2,1)S(1)}, u32[]{:S(2)}, u32[]{:S(2)}) collective-permute-start(bf16[64,384]{1,0:T(8,128)(2,1)S(1)} %collective-permute-done.15.refs_1_), channel_id=1, source_target_pairs={{0,1},{1,0},{2,3},{3,2},{4,5},{5,4},{6,7},{7,6},{8,9},{9,8},{10,11... | collective-permute-start | bytes 147464 | tf_op jit(solution)/shard_map/ppermute | solution.py:26
  51.0 2.4 %collective-permute-start.20 = (bf16[64,384]{1,0:T(8,128)(2,1)S(1)}, bf16[64,384]{1,0:T(8,128)(2,1)S(1)}, u32[]{:S(2)}, u32[]{:S(2)}) collective-permute-start(bf16[64,384]{1,0:T(8,128)(2,1)S(1)} %collective-permute-done.16.refs_2_), channel_id=1, source_target_pairs={{0,1},{1,0},{2,3},{3,2},{4,5},{5,4},{6,7},{7,6},{8,9},{9,8},{10,11... | collective-permute-start | bytes 147464 | tf_op jit(solution)/shard_map/ppermute | solution.py:26
  51.0 2.3 %collective-permute-start.21 = (bf16[64,384]{1,0:T(8,128)(2,1)S(1)}, bf16[64,384]{1,0:T(8,128)(2,1)S(1)}, u32[]{:S(2)}, u32[]{:S(2)}) collective-permute-start(bf16[64,384]{1,0:T(8,128)(2,1)S(1)} %collective-permute-done.17.refs_3_), channel_id=1, source_target_pairs={{0,1},{1,0},{2,3},{3,2},{4,5},{5,4},{6,7},{7,6},{8,9},{9,8},{10,11... | collective-permute-start | bytes 147464 | tf_op jit(solution)/shard_map/ppermute | solution.py:26

commit v3 on v2

--- a/solution.py
+++ b/solution.py
@@ -26,7 +26,14 @@
     return lax.ppermute(block, AXES, route)
 
 
+COST = {}
+
+
 def call(body, outs, smem, vmem, scratch=(), limit=24):
+    title = getattr(body, "func", body).__name__
+    cost = None
+    if COST.get(title, 1):
+        cost = pl.CostEstimate(flops=10**9, bytes_accessed=0, transcendentals=0)
     specs = [pl.BlockSpec(memory_space=pltpu.SMEM)] * len(smem)
     specs += [pl.BlockSpec(memory_space=pltpu.VMEM)] * len(vmem)
     return pl.pallas_call(
@@ -37,7 +44,7 @@
         scratch_shapes=scratch,
         compiler_params=pltpu.CompilerParams(vmem_limit_bytes=limit << 20),
         cost_estimate=pl.CostEstimate(flops=5 * 10**9, bytes_accessed=0, transcendentals=0),
-        name=getattr(body, "func", body).__name__,
+        name=title,
     )(*smem, *vmem)
 
 
@@ -80,80 +87,62 @@
         right[k] = jnp.where(side == 0, part[:share], part[share:])
 
 
-def leaf_products(ids, inverse, rhs, keep, turned, *sends):
+def leaf_products(ids, inverse, rhs, keep, *refs):
+    *sends, order = refs
     column = ids[0]
-    rows = rhs.shape[0]
-    half = len(sends) + 1
-    turned[...] = rhs[...].T
-    for j in range(half):
-        for top in range(2):
-            block = ((column ^ j) & (half - 1)) + top * half
-            value = dot(inverse[rows_at(block * rows, rows), :], rhs[...], NN)
-            if j == 0:
-                keep[top] = value
-            else:
-                sends[j - 1][top] = value.astype(BF16)
-
-
-def add_products(count, ids, keep, *refs):
-    low, high, high_own = refs[count:]
-    value = keep[0]
-    for r in refs[:count]:
-        value += r[0].astype(F32)
-    low[...] = value.astype(BF16)
-    value = keep[1]
-    for r in refs[:count]:
-        value += r[1].astype(F32)
-    high[...] = value.astype(BF16)
-    high_own[...] = value
-
-
-def panel_products(masks, ids, inverse, *refs):
-    panels, out = refs[: len(masks)], refs[-1]
+    groups, wide, rows = inverse.shape[0] // rhs.shape[0], keep.shape[1] // 2, rhs.shape[0]
+    half = groups // 2
+    order[...] = rhs[...].T
+    turned = jnp.concatenate(
+        [
+            order[rows_at((((column ^ j) & (half - 1)) + top * half) * wide, wide), :]
+            for j in range(half)
+            for top in range(2)
+        ],
+        axis=0,
+    )
+    for block in range(groups):
+        value = dot(turned, inverse[block * rows : (block + 1) * rows, :], NT)
+        keep[block] = value[: 2 * wide]
+        for j in range(1, half):
+            part = value[2 * wide * j : 2 * wide * (j + 1)]
+            sends[(j - 1) * groups + block][...] = part.astype(BF16)
+
+
+def own_partials(masks, ids, keep, *refs):
+    panels, received = refs[: len(masks)], refs[len(masks) : -5]
+    mine, low, high, high_own, out = refs[-5:]
     column = ids[0]
-    rows = inverse.shape[1]
+    half = low.shape[0]
+    for block in range(2 * half):
+        value = keep[block]
+        for r in received[block :: 2 * half]:
+            value += r[...].astype(F32)
+        mine[block] = value.astype(BF16)
+        if block < half:
+            low[block] = value.astype(BF16)
+        else:
+            high[block - half] = value.astype(BF16)
+            high_own[block - half] = value
     total = None
     for mask, panel in zip(masks, panels):
-        value = dot(panel[...], inverse[rows_at((column ^ mask) * rows, rows), :], NN)
+        value = dot(mine[column ^ mask], panel[...], NT)
         total = value if total is None else total + value
     out[...] = total
 
 
-def partials(masks, ids, inverse, early, turned, *refs):
+def partials(masks, ids, mine, early, *refs):
     panels = refs[: len(masks)]
-    weight, keep, *sends = refs[len(masks) :]
-    scratch = sends.pop()
-    column = ids[0]
-    rows = inverse.shape[1]
+    own, same, other, cross, scratch = refs[len(masks) :]
+    column, side, top = ids[0], ids[1], ids[2]
+    share = own.shape[0]
     total = early[...]
     for mask, panel in zip(masks, panels):
-        total += dot(panel[...], inverse[rows_at((column ^ mask) * rows, rows), :], NN)
-    weight[...] = total.astype(BF16)
-    scratch[...] = dot(turned[...], weight[...], NT)
-    half = len(sends) + 1
-    wide = keep.shape[0] // 2
-    for j in range(half):
-        for top in range(2):
-            block = ((column ^ j) & (half - 1)) + top * half
-            value = scratch[rows_at(block * wide, wide), :]
-            if j == 0:
-                keep[top * wide : (top + 1) * wide] = value
-            else:
-                sends[j - 1][top * wide : (top + 1) * wide] = value.astype(BF16)
-
-
-def spread(count, ids, keep, *refs):
-    received = refs[:count]
-    own, same, other, cross = refs[count:]
-    top, side = ids[2], ids[1]
-    share = own.shape[0]
+        total += dot(mine[column ^ mask], panel[...], NT)
+    scratch[...] = total
 
     def piece(which_top, which_side):
-        at = rows_at((which_top * 2 + which_side) * share, share)
-        value = keep[at, :]
-        for r in received:
-            value += r[at, :].astype(F32)
-        return value
+        return scratch[rows_at((which_top * 2 + which_side) * share, share), :]
 
     own[...] = piece(top, side)
     same[...] = piece(1 - top, side).astype(BF16)
@@ -207,20 +196,29 @@
             out[:, k * touched : (k + 1) * touched] = piece.astype(BF16)
 
 
-def leaf_transposed(count, ids, inverse, weight, *refs):
+def leaf_transposed(masks, half, ids, inverse, *refs):
+    panels, blocks = refs[: len(masks)], refs[len(masks) : -2]
     out, weight_turned = refs[-2:]
-    blocks = refs[:-2]
     column = ids[0]
     rows = inverse.shape[1]
-    half = count
-    weight_turned[...] = weight[...].T
+    weight = None
+    for mask, panel in zip(masks, panels):
+        value = dot(panel[...], inverse[rows_at((column ^ mask) * rows, rows), :], NN)
+        weight = value if weight is None else weight + value
+    weight_turned[...] = weight.T.astype(BF16)
     total = None
+    for block in range(2 * half):
+        left = jnp.concatenate(
+            [blocks[2 * j + block // half][block % half] for j in range(half)], axis=0
+        )
+        value = dot(left, inverse[block * rows : (block + 1) * rows, :], NN)
+        total = value if total is None else total + value
+    wide = total.shape[0] // (2 * half)
     for j in range(half):
         for top in range(2):
-            block = ((column ^ j) & (half - 1)) + top * half
-            value = dot(inverse[rows_at(block * rows, rows), :], blocks[2 * j + top][...], TN)
-            total = value if total is None else total + value
-    out[...] = total
+            source = ((column ^ j) & (half - 1)) + top * half
+            at = (2 * j + top) * wide
+            out[:, rows_at(source * wide, wide)] = total[at : at + wide].T
 
 
 def finish(half, ids, base, weight_turned, *refs):
@@ -262,75 +260,57 @@
     def shape(dims, dtype=F32):
         return jax.ShapeDtypeStruct(dims, dtype)
 
-    held = {0: panel}
-    for bit in reversed(range(groups.bit_length() - 1)):
-        for mask in list(held):
-            held[mask | 1 << bit] = moved(held[mask], 0, 1 << bit)
+    held = {0: panel, half: moved(panel, 0, half)}
+    for mask in range(1, half):
+        held[mask] = moved(panel, 0, mask)
     spots = jnp.concatenate([offsets, pattern], axis=0)
     spots = jnp.concatenate([spots, moved(spots, 1, 0)], axis=0)
 
-    keep, turned, *sends = call(
+    mine_rows = (groups, sources // half, rows)
+    upper_rows = (half, sources // half, rows)
+    keep, *sends = call(
         leaf_products,
-        [shape((2, rows, sources)), shape((sources, rows), BF16)]
-        + [shape((2, rows, sources), BF16)] * (half - 1),
+        [shape(mine_rows)] + [shape(mine_rows[1:], BF16)] * ((half - 1) * groups),
         [ids],
         [inverse, rhs],
-    )
+        [pltpu.VMEM((sources, rows), BF16)],
+    )
+    received = [moved(block, 0, n // groups + 1) for n, block in enumerate(sends)]
+
+    near, far = list(range(half)), list(range(half, groups))
+    partial_shape = (sources // half, levels * touched)
+    keep, held[half] = lax.optimization_barrier((keep, held[half]))
+    mine, low, high, high_own, early = call(
+        functools.partial(own_partials, near),
+        [shape(mine_rows, BF16)]
+        + [shape(upper_rows, BF16)] * 2
+        + [shape(upper_rows), shape(partial_shape)],
+        [ids],
+        [keep] + [held[mask] for mask in near] + received,
+    )
+    for mask in range(1, half):
+        held[half | mask] = moved(held[half], 0, mask)
+    piece = (share, levels * touched)
+    own, same, other, cross = call(
+        functools.partial(partials, far),
+        [shape(piece)] + [shape(piece, BF16)] * 3,
+        [ids],
+        [mine, early] + [held[mask] for mask in far],
+        [pltpu.VMEM(partial_shape, F32)],
+    )
+    high, own, inverses = lax.optimization_barrier((high, own, sep_inverse[0]))
+    same, other, cross = moved(same, 0, half), moved(other, 1, 0), moved(cross, 1, half)
+
+    high = moved(high, 0, half)
+
     q_high, q_low, k_high, k_low, right = call(
         prepare,
         [shape((levels, sep_rows, sep_rows), BF16)] * 2
         + [shape((levels - 1, sep_rows, sep_rows), BF16)] * 2
         + [shape((levels, share, sep_rows))],
         [ids],
-        [sep_inverse[0], sep_link[0], sep_rhs[0]],
-    )
-    received = [moved(block, 0, j + 1) for j, block in enumerate(sends)]
-    low, high, high_own = call(
-        functools.partial(add_products, half - 1),
-        [shape((rows, sources), BF16)] * 2 + [shape((rows, sources))],
-        [ids],
-        [keep, *received],
-    )
-
-    near = [mask for mask in held if mask < half]
-    far = [mask for mask in held if mask >= half]
-    early = call(
-        functools.partial(panel_products, near),
-        [shape(panel.shape)],
-        [ids],
-        [inverse] + [held[mask] for mask in near],
-    )[0]
-    names = [shape(panel.shape, BF16), shape((sources // half, levels * touched))]
-    names += [shape((sources // half, levels * touched), BF16)] * (half - 1)
-    weight, part_keep, *part_sends = call(
-        functools.partial(partials, far),
-        names,
-        [ids],
-        [inverse, early, turned] + [held[mask] for mask in far],
-        [pltpu.VMEM((sources, levels * touched), F32)],
-    )
-    part_received = [moved(block, 0, j + 1) for j, block in enumerate(part_sends)]
-    piece = (share, levels * touched)
-    own, same, other, cross = call(
-        functools.partial(spread, half - 1),
-        [shape(piece)] + [shape(piece, BF16)] * 3,
-        [ids],
-        [part_keep, *part_received],
-    )
-    same, other, cross = moved(same, 0, half), moved(other, 1, 0), moved(cross, 1, half)
-
-    high, own = lax.optimization_barrier((high, own))
-    solved_high = (high_own + moved(high, 0, half).astype(F32)).astype(BF16)
-    solved = [low, solved_high]
-    for j in range(1, half):
-        solved += [moved(low, 0, j), moved(solved_high, 0, j)]
-    base, weight_turned = call(
-        functools.partial(leaf_transposed, half),
-        [shape((rows, sources)), shape((rows, levels * touched), BF16)],
-        [ids],
-        [inverse, weight, *solved],
-    )
-
+        [inverses, sep_link[0], sep_rhs[0]],
+    )
     kept, *up_sends = call(
         functools.partial(upward, touched),
         [shape((levels, share, sep_rows))]
@@ -342,6 +322,19 @@
     for delta in range(1, leaves // 2):
         lengths.append(delta.bit_length())
         up_received.append(moved(up_sends[delta.bit_length() - 1], 2 * delta, 0))
+    high, *up_received = lax.optimization_barrier((high, *up_received))
+    solved_high = (high_own + high.astype(F32)).astype(BF16)
+    solved = [low, solved_high]
+    for j in range(1, half):
+        solved += [moved(low, 0, j), moved(solved_high, 0, j)]
+    masks = near + far
+    base, weight_turned = call(
+        functools.partial(leaf_transposed, masks, half),
+        [shape((rows, sources)), shape((rows, levels * touched), BF16)],
+        [ids],
+        [inverse] + [held[mask] for mask in masks] + solved,
+    )
+
     answer, passed, mine, theirs = call(
         functools.partial(downward, touched, lengths),
         [shape((levels, share, sep_rows))] * 2 + [shape(piece, BF16)] * 2,
@@ -351,6 +344,7 @@
 
     blocks = [mine, moved(mine, 0, half), moved(theirs, 1, 0), moved(theirs, 1, half)]
     passed = moved(passed, 1, 0)
+    *blocks, base = lax.optimization_barrier((*blocks, base))
     for j in range(1, half):
         blocks += [moved(block, 0, j) for block in blocks[:4]]
     final = call(

time: 55.4 us -> 50.4 us (0.910)
  waiting for transfers between devices: 16.6 us -> 10.2 us
  starting transfers between devices: 19.6 us -> 21.6 us
  Pallas kernels: 15.3 us -> 14.7 us
    ppermute x23 -> x25, waiting for transfers between devices: 16.6 us -> 10.2 us  [moved(): return lax.ppermute(block, AXES, route)]
    ppermute x23 -> x25, starting transfers between devices: 19.6 us -> 21.6 us  [moved(): return lax.ppermute(block, AXES, route)]
    pallas_call x11 -> x9, Pallas kernels: 15.3 us -> 14.7 us  [call(): pl.pallas_call(body, out_shape=outs, in_specs=specs, out_specs=[pl.BlockS...]
  transfers between devices with their start and end apart: 23 -> 25, of which waited for: 9 -> 8; matrix products, arithmetic and copies ran while one was open for 0% -> 1% of each run, Pallas kernels for 22% -> 24%
where the time goes in v3:
time: 50.4 us; the launch traced here: 50.2 us
  starting transfers between devices  21.6 us (43%)
  Pallas kernels  14.7 us (29%)
  waiting for transfers between devices  10.2 us (20%)
  local copies, waits for them, and re-layouts  2.67 us (5%)
  between operations  0.83 us (2%)
    ppermute x25, starting transfers between devices, moved(): return lax.ppermute(block, AXES, route)  21.6 us
    pallas_call x9, Pallas kernels, call(): pl.pallas_call(body, out_shape=outs, in_specs=specs, out_specs=[pl.BlockS...  14.7 us
    ppermute x25, waiting for transfers between devices, moved(): return lax.ppermute(block, AXES, route)  10.2 us
    unnamed x18, local copies, waits for them, and re-layouts  2.67 us
  transfers between devices with their start and end apart: 25, of which 8 were waited for; matrix products, arithmetic and copies ran while one was open for 1% of the time, Pallas kernels for 24%

profile of v3, /device:TPU:0, one launch (start us, length us, event | category | flops | bytes accessed | tf_op | source)
XLA Modules:
  0.0 50.2 jit_solution(18141045835923513935)
XLA Ops:
  0.6 3.0 %collective-permute-start.1 = (bf16[384,512]{1,0:T(8,128)(2,1)}, bf16[384,512]{1,0:T(8,128)(2,1)S(1)}, u32[]{:S(2)}, u32[]{:S(2)}) collective-permute-start(bf16[384,512]{1,0:T(8,128)(2,1)} %bitcast.17), channel_id=1, source_target_pairs={{0,2},{1,3},{2,0},{3,1},{4,6},{5,7},{6,4},{7,5},{8,10},{9,11},{10,... | collective-permute-start | bytes 1179656 | tf_op jit(solution)/shard_map/ppermute | solution.py:26
  3.7 1.6 %copy-done = bf16[1,2048,512]{2,1,0:T(8,128)(2,1)S(1)} copy-done((bf16[1,2048,512]{2,1,0:T(8,128)(2,1)S(1)}, bf16[1,2048,512]{2,1,0:T(8,128)(2,1)}, u32[]{:S(2)}) %copy-start) | copy-done | bytes 2097176
  5.3 1.0 %copy-done.4 = bf16[1,512,512]{2,1,0:T(8,128)(2,1)S(1)} copy-done((bf16[1,512,512]{2,1,0:T(8,128)(2,1)S(1)}, bf16[1,512,512]{2,1,0:T(8,128)(2,1)}, u32[]{:S(2)}) %copy-start.4) | copy-done | bytes 524312
  6.4 1.9 %leaf_products.1 = (f32[4,256,512]{2,1,0:T(8,128)S(1)}, bf16[256,512]{1,0:T(8,128)(2,1)S(1)}, bf16[256,512]{1,0:T(8,128)(2,1)S(1)}, bf16[256,512]{1,0:T(8,128)(2,1)S(1)}, bf16[256,512]{1,0:T(8,128)(2,1)S(1)}) custom-call(s32[3]{0:T(128)S(1)} %pad_add_fusion.2.ids, bf16[2048,512]{1,0:T(8,128)(2,1)S(1)} %bitcast.11, bf16[512,512]{1,0:T(8,128)(2,1)S(1)} %bitcast.15), custom_call_target="tpu_custom_call" | custom-call | flops 5000000000 | tf_op jit(solution)/shard_map/leaf_products/pallas_call | solution.py:39
  8.2 0.6 %collective-permute-start.3 = (bf16[256,512]{1,0:T(8,128)(2,1)S(1)}, bf16[256,512]{1,0:T(8,128)(2,1)S(1)}, u32[]{:S(2)}, u32[]{:S(2)}) collective-permute-start(bf16[256,512]{1,0:T(8,128)(2,1)S(1)} %get-tuple-element.46), channel_id=1, source_target_pairs={{0,1},{1,0},{2,3},{3,2},{4,5},{5,4},{6,7},{7,6},{8,9},{9,8},{10,11... | collective-permute-start | bytes 786440 | tf_op jit(solution)/shard_map/ppermute | solution.py:26
  8.9 1.6 %collective-permute-start = (s32[2,3]{1,0:T(2,128)S(1)}, s32[2,3]{1,0:T(2,128)S(1)}, u32[]{:S(2)}, u32[]{:S(2)}) collective-permute-start(s32[2,3]{1,0:T(2,128)S(1)} %pad_add_fusion.1), channel_id=1, source_target_pairs={{0,4},{1,5},{2,6},{3,7},{4,0},{5,1},{6,2},{7,3},{8,12},{9,13},{10,... | collective-permute-start | bytes 80 | tf_op jit(solution)/shard_map/ppermute | solution.py:26
  10.5 2.1 %collective-permute-done = s32[2,3]{1,0:T(2,128)S(1)} collective-permute-done((s32[2,3]{1,0:T(2,128)S(1)}, s32[2,3]{1,0:T(2,128)S(1)}, u32[]{:S(2)}, u32[]{:S(2)}) %collective-permute-start) | collective-permute-done | bytes 56 | tf_op jit(solution)/shard_map/ppermute | solution.py:26
  12.5 0.4 collective-permute-done.1.refs_0_.refs_2_
  13.1 0.5 %collective-permute-start.7 = (bf16[384,512]{1,0:T(8,128)(2,1)S(1)}, bf16[384,512]{1,0:T(8,128)(2,1)S(1)}, u32[]{:S(2)}, u32[]{:S(2)}) collective-permute-start(bf16[384,512]{1,0:T(8,128)(2,1)S(1)} %collective-permute-done.1.refs_0_.refs_2_), channel_id=1, source_target_pairs={{0,1},{1,0},{2,3},{3,2},{4,5},{5,4},{6,7},{7,6},{8,9},{9,8},{10,11... | collective-permute-start | bytes 1179656 | tf_op jit(solution)/shard_map/ppermute | solution.py:26
  13.6 0.5 collective-permute-done.5.refs_4_
  14.1 0.4 collective-permute-done.6.refs_5_
  14.5 1.4 %own_partials.1 = (bf16[4,256,512]{2,1,0:T(8,128)(2,1)S(1)}, bf16[2,256,512]{2,1,0:T(8,128)(2,1)S(1)}, bf16[2,256,512]{2,1,0:T(8,128)(2,1)S(1)}, f32[2,256,512]{2,1,0:T(8,128)S(1)}, f32[256,384]{1,0:T(8,128)S(1)}) custom-call(s32[3]{0:T(128)S(1)} %pad_add_fusion.2.ids, f32[4,256,512]{2,1,0:T(8,128)S(1)} %get-tuple-element.45.keep, ...), custom_call_target="tpu_custom_call" | custom-call | flops 5000000000 | tf_op jit(solution)/shard_map/own_partials/pallas_call | solution.py:39
  15.9 1.0 %partials.1 = (f32[64,384]{1,0:T(8,128)S(1)}, bf16[64,384]{1,0:T(8,128)(2,1)S(1)}, bf16[64,384]{1,0:T(8,128)(2,1)S(1)}, bf16[64,384]{1,0:T(8,128)(2,1)S(1)}) custom-call(s32[3]{0:T(128)S(1)} %pad_add_fusion.2.ids, bf16[4,256,512]{2,1,0:T(8,128)(2,1)S(1)} %get-tuple-element.51.mine, f32[256,384]{1,0:T(8,128)S(1)} %get-tuple-element.52.early, ...), custom_call_target="tpu_custom_call" | custom-call | flops 5000000000 | tf_op jit(solution)/shard_map/partials/pallas_call | solution.py:39
  17.0 2.7 %collective-permute-start.10 = (bf16[64,384]{1,0:T(8,128)(2,1)S(1)}, bf16[64,384]{1,0:T(8,128)(2,1)S(1)}, u32[]{:S(2)}, u32[]{:S(2)}) collective-permute-start(bf16[64,384]{1,0:T(8,128)(2,1)S(1)} %get-tuple-element.58), channel_id=1, source_target_pairs={{0,6},{1,7},{2,4},{3,5},{4,2},{5,3},{6,0},{7,1},{8,14},{9,15},{10,... | collective-permute-start | bytes 147464 | tf_op jit(solution)/shard_map/ppermute | solution.py:26
  19.7 0.5 %collective-permute-start.8 = (bf16[64,384]{1,0:T(8,128)(2,1)S(1)}, bf16[64,384]{1,0:T(8,128)(2,1)S(1)}, u32[]{:S(2)}, u32[]{:S(2)}) collective-permute-start(bf16[64,384]{1,0:T(8,128)(2,1)S(1)} %get-tuple-element.56), channel_id=1, source_target_pairs={{0,2},{1,3},{2,0},{3,1},{4,6},{5,7},{6,4},{7,5},{8,10},{9,11},{10,... | collective-permute-start | bytes 147464 | tf_op jit(solution)/shard_map/ppermute | solution.py:26
  20.5 1.7 %collective-permute-start.11 = (bf16[2,256,512]{2,1,0:T(8,128)(2,1)S(1)}, bf16[2,256,512]{2,1,0:T(8,128)(2,1)S(1)}, u32[]{:S(2)}, u32[]{:S(2)}) collective-permute-start(bf16[2,256,512]{2,1,0:T(8,128)(2,1)S(1)} %get-tuple-element.66), channel_id=1, source_target_pairs={{0,2},{1,3},{2,0},{3,1},{4,6},{5,7},{6,4},{7,5},{8,10},{9,11},{10,... | collective-permute-start | bytes 1572872 | tf_op jit(solution)/shard_map/ppermute | solution.py:26
  22.3 1.9 %prepare.1 = (bf16[3,256,256]{2,1,0:T(8,128)(2,1)S(1)}, bf16[3,256,256]{2,1,0:T(8,128)(2,1)S(1)}, bf16[2,256,256]{2,1,0:T(8,128)(2,1)S(1)}, bf16[2,256,256]{2,1,0:T(8,128)(2,1)S(1)}, f32[3,64,256]{2,1,0:T(8,128)S(1)}) custom-call(s32[3]{0:T(128)S(1)} %pad_add_fusion.2.ids, f32[3,256,256]{2,1,0:T(8,128)S(1)} %bitcast.14, f32[2,256,256]{2,1,0:T(8,128)S(1)} %bitcast.16, ...), custom_call_target="tpu_custom_call" | custom-call | flops 5000000000 | tf_op jit(solution)/shard_map/prepare/pallas_call | solution.py:39
  24.3 1.2 %upward.1 = (f32[3,64,256]{2,1,0:T(8,128)S(1)}, bf16[2,64,256]{2,1,0:T(8,128)(2,1)S(1)}, bf16[1,64,256]{2,1,0:T(8,128)(2,1)S(1)}) custom-call(s32[3]{0:T(128)S(1)} %pad_add_fusion.2.ids, s32[4,3]{1,0:T(4,128)S(1)} %pad_add_fusion.spots, f32[64,384]{1,0:T(8,128)S(1)} %get-tuple-element.55.own, bf16[64,384]{1,0:T(8,128)(2,1)S(1)} %collective-permute-done.8.same, ...), custom_call_target="tpu_custom_call" | custom-call | flops 5000000000 | tf_op jit(solution)/shard_map/upward/pallas_call | solution.py:39
  25.5 1.6 %collective-permute-start.12 = (bf16[2,64,256]{2,1,0:T(8,128)(2,1)S(1)}, bf16[2,64,256]{2,1,0:T(8,128)(2,1)S(1)}, u32[]{:S(2)}, u32[]{:S(2)}) collective-permute-start(bf16[2,64,256]{2,1,0:T(8,128)(2,1)S(1)} %get-tuple-element.67), channel_id=1, source_target_pairs={{0,8},{1,9},{2,10},{3,11},{4,12},{5,13},{6,14},{7,15},{8,0},{9,1},... | collective-permute-start | bytes 196616 | tf_op jit(solution)/shard_map/ppermute | solution.py:26
  27.2 2.6 %collective-permute-start.13 = (bf16[1,64,256]{2,1,0:T(8,128)(2,1)S(1)}, bf16[1,64,256]{2,1,0:T(8,128)(2,1)S(1)}, u32[]{:S(2)}, u32[]{:S(2)}) collective-permute-start(bf16[1,64,256]{2,1,0:T(8,128)(2,1)S(1)} %get-tuple-element.68), channel_id=1, source_target_pairs={{0,16},{1,17},{2,18},{3,19},{4,20},{5,21},{6,22},{7,23},{8,24},{9,... | collective-permute-start | bytes 98312 | tf_op jit(solution)/shard_map/ppermute | solution.py:26
  30.0 2.0 %collective-permute-done.13.refs_1_ = bf16[1,64,256]{2,1,0:T(8,128)(2,1)S(1)} collective-permute-done((bf16[1,64,256]{2,1,0:T(8,128)(2,1)S(1)}, bf16[1,64,256]{2,1,0:T(8,128)(2,1)S(1)}, u32[]{:S(2)}, u32[]{:S(2)}) %collective-permute-start.13) | collective-permute-done | bytes 32800 | tf_op jit(solution)/shard_map/ppermute | solution.py:26
  32.0 3.5 %collective-permute-done.14.refs_2_ = bf16[1,64,256]{2,1,0:T(8,128)(2,1)S(1)} collective-permute-done((bf16[1,64,256]{2,1,0:T(8,128)(2,1)S(1)}, bf16[1,64,256]{2,1,0:T(8,128)(2,1)S(1)}, u32[]{:S(2)}, u32[]{:S(2)}) %collective-permute-start.14) | collective-permute-done | bytes 32800 | tf_op jit(solution)/shard_map/ppermute | solution.py:26
  35.8 1.3 %downward.1 = (f32[3,64,256]{2,1,0:T(8,128)S(1)}, f32[3,64,256]{2,1,0:T(8,128)S(1)}, bf16[64,384]{1,0:T(8,128)(2,1)S(1)}, bf16[64,384]{1,0:T(8,128)(2,1)S(1)}) custom-call(s32[3]{0:T(128)S(1)} %pad_add_fusion.2.ids, s32[4,3]{1,0:T(4,128)S(1)} %pad_add_fusion.spots, f32[3,64,256]{2,1,0:T(8,128)S(1)} %get-tuple-element.63.kept, ...), custom_call_target="tpu_custom_call" | custom-call | flops 5000000000 | tf_op jit(solution)/shard_map/downward/pallas_call | solution.py:39
  37.0 1.4 %collective-permute-start.16 = (bf16[64,384]{1,0:T(8,128)(2,1)S(1)}, bf16[64,384]{1,0:T(8,128)(2,1)S(1)}, u32[]{:S(2)}, u32[]{:S(2)}) collective-permute-start(bf16[64,384]{1,0:T(8,128)(2,1)S(1)} %get-tuple-element.73), channel_id=1, source_target_pairs={{0,4},{1,5},{2,6},{3,7},{4,0},{5,1},{6,2},{7,3},{8,12},{9,13},{10,... | collective-permute-start | bytes 147464 | tf_op jit(solution)/shard_map/ppermute | solution.py:26
  38.4 1.6 %collective-permute-start.17 = (bf16[64,384]{1,0:T(8,128)(2,1)S(1)}, bf16[64,384]{1,0:T(8,128)(2,1)S(1)}, u32[]{:S(2)}, u32[]{:S(2)}) collective-permute-start(bf16[64,384]{1,0:T(8,128)(2,1)S(1)} %get-tuple-element.73), channel_id=1, source_target_pairs={{0,6},{1,7},{2,4},{3,5},{4,2},{5,3},{6,0},{7,1},{8,14},{9,15},{10,... | collective-permute-start | bytes 147464 | tf_op jit(solution)/shard_map/ppermute | solution.py:26
  40.0 0.5 %collective-permute-start.24 = (f32[3,64,256]{2,1,0:T(8,128)S(1)}, f32[3,64,256]{2,1,0:T(8,128)S(1)}, u32[]{:S(2)}, u32[]{:S(2)}) collective-permute-start(f32[3,64,256]{2,1,0:T(8,128)S(1)} %get-tuple-element.85), channel_id=1, source_target_pairs={{0,4},{1,5},{2,6},{3,7},{4,0},{5,1},{6,2},{7,3},{8,12},{9,13},{10,... | collective-permute-start | bytes 589832 | tf_op jit(solution)/shard_map/ppermute | solution.py:26
  40.6 1.3 %collective-permute-start.15 = (bf16[64,384]{1,0:T(8,128)(2,1)S(1)}, bf16[64,384]{1,0:T(8,128)(2,1)S(1)}, u32[]{:S(2)}, u32[]{:S(2)}) collective-permute-start(bf16[64,384]{1,0:T(8,128)(2,1)S(1)} %get-tuple-element.80.refs_0_), channel_id=1, source_target_pairs={{0,2},{1,3},{2,0},{3,1},{4,6},{5,7},{6,4},{7,5},{8,10},{9,11},{10,... | collective-permute-start | bytes 147464 | tf_op jit(solution)/shard_map/ppermute | solution.py:26
  41.9 2.8 %leaf_transposed.1 = (f32[512,512]{1,0:T(8,128)S(1)}, bf16[512,384]{1,0:T(8,128)(2,1)S(1)}) custom-call(s32[3]{0:T(128)S(1)} %pad_add_fusion.2.ids, bf16[2048,512]{1,0:T(8,128)(2,1)S(1)} %bitcast.12, bf16[384,512]{1,0:T(8,128)(2,1)S(1)} %bitcast.20, bf16[384,512]{1,0:T(8,128)(2,1)S(1)} %collective-permute-done.2.refs_1_, ...), custom_call_target="tpu_custom_call" | custom-call | flops 5000000000 | tf_op jit(solution)/shard_map/leaf_transposed/pallas_call | solution.py:39
  44.9 0.5 collective-permute-start.21
  45.9 1.0 %collective-permute-done.24.theirs = f32[3,64,256]{2,1,0:T(8,128)S(1)} collective-permute-done((f32[3,64,256]{2,1,0:T(8,128)S(1)}, f32[3,64,256]{2,1,0:T(8,128)S(1)}, u32[]{:S(2)}, u32[]{:S(2)}) %collective-permute-start.24) | collective-permute-done | bytes 196640 | tf_op jit(solution)/shard_map/ppermute | solution.py:26
  46.9 1.5 %assemble.1 = f32[3,256,128]{2,1,0:T(8,128)} custom-call(s32[3]{0:T(128)S(1)} %pad_add_fusion.2.ids, f32[3,64,256]{2,1,0:T(8,128)S(1)} %get-tuple-element.84.mine, f32[3,64,256]{2,1,0:T(8,128)S(1)} %collective-permute-done.24.theirs), custom_call_target="tpu_custom_call" | custom-call | flops 5000000000 | tf_op jit(solution)/shard_map/assemble/pallas_call | solution.py:39
  48.3 1.8 %finish.1 = bf16[512,512]{1,0:T(8,128)(2,1)} custom-call(s32[3]{0:T(128)S(1)} %pad_add_fusion.2.ids, f32[512,512]{1,0:T(8,128)S(1)} %get-tuple-element.78.base, bf16[512,384]{1,0:T(8,128)(2,1)S(1)} %get-tuple-element.79.weight_turned, bf16[64,384]{1,0:T(8,128)(2,1)S(1)} %get-tuple-element.80.refs_0_, bf16[64,384]{1,0:T(8,128)(2,1)S(1)} %collective-permute-done.15.refs_1_, ...), custom_call_target="tpu_custom_call" | custom-call | flops 5000000000 | tf_op jit(solution)/shard_map/finish/pallas_call | solution.py:39
  (49 shorter events, 1.9 us)
Async XLA Ops:
  0.6 12.4 %collective-permute-start.1 = (bf16[384,512]{1,0:T(8,128)(2,1)}, bf16[384,512]{1,0:T(8,128)(2,1)S(1)}, u32[]{:S(2)}, u32[]{:S(2)}) collective-permute-start(bf16[384,512]{1,0:T(8,128)(2,1)} %bitcast.17), channel_id=1, source_target_pairs={{0,2},{1,3},{2,0},{3,1},{4,6},{5,7},{6,4},{7,5},{8,10},{9,11},{10,... | collective-permute-start | bytes 1179656 | tf_op jit(solution)/shard_map/ppermute | solution.py:26
  3.7 10.9 %collective-permute-start.2 = (bf16[384,512]{1,0:T(8,128)(2,1)}, bf16[384,512]{1,0:T(8,128)(2,1)S(1)}, u32[]{:S(2)}, u32[]{:S(2)}) collective-permute-start(bf16[384,512]{1,0:T(8,128)(2,1)} %bitcast.18), channel_id=1, source_target_pairs={{0,1},{1,0},{2,3},{3,2},{4,5},{5,4},{6,7},{7,6},{8,9},{9,8},{10,11... | collective-permute-start | bytes 1179656 | tf_op jit(solution)/shard_map/ppermute | solution.py:26
  6.4 2.5 %copy-start.7 = (s32[1,3]{1,0:T(1,128)S(1)}, s32[1,3]{1,0:T(1,128)}, u32[]{:S(2)}) copy-start(s32[1,3]{1,0:T(1,128)} %param.11) | copy-start | bytes 40
  6.4 2.5 %copy-start.8 = (s32[1,3]{1,0:T(1,128)S(1)}, s32[1,3]{1,0:T(1,128)}, u32[]{:S(2)}) copy-start(s32[1,3]{1,0:T(1,128)} %param.12) | copy-start | bytes 40
  6.4 8.2 %copy-start.6 = (bf16[1,3,128,512]{3,2,1,0:T(8,128)(2,1)S(1)}, bf16[1,3,128,512]{3,2,1,0:T(8,128)(2,1)}, u32[]{:S(2)}) copy-start(bf16[1,3,128,512]{3,2,1,0:T(8,128)(2,1)} %param.10) | copy-start | bytes 1179652
  8.2 4.8 %collective-permute-start.3 = (bf16[256,512]{1,0:T(8,128)(2,1)S(1)}, bf16[256,512]{1,0:T(8,128)(2,1)S(1)}, u32[]{:S(2)}, u32[]{:S(2)}) collective-permute-start(bf16[256,512]{1,0:T(8,128)(2,1)S(1)} %get-tuple-element.46), channel_id=1, source_target_pairs={{0,1},{1,0},{2,3},{3,2},{4,5},{5,4},{6,7},{7,6},{8,9},{9,8},{10,11... | collective-permute-start | bytes 786440 | tf_op jit(solution)/shard_map/ppermute | solution.py:26
  8.8 4.8 %collective-permute-start.4 = (bf16[256,512]{1,0:T(8,128)(2,1)S(1)}, bf16[256,512]{1,0:T(8,128)(2,1)S(1)}, u32[]{:S(2)}, u32[]{:S(2)}) collective-permute-start(bf16[256,512]{1,0:T(8,128)(2,1)S(1)} %get-tuple-element.47), channel_id=1, source_target_pairs={{0,1},{1,0},{2,3},{3,2},{4,5},{5,4},{6,7},{7,6},{8,9},{9,8},{10,11... | collective-permute-start | bytes 786440 | tf_op jit(solution)/shard_map/ppermute | solution.py:26
  8.9 3.6 %collective-permute-start = (s32[2,3]{1,0:T(2,128)S(1)}, s32[2,3]{1,0:T(2,128)S(1)}, u32[]{:S(2)}, u32[]{:S(2)}) collective-permute-start(s32[2,3]{1,0:T(2,128)S(1)} %pad_add_fusion.1), channel_id=1, source_target_pairs={{0,4},{1,5},{2,6},{3,7},{4,0},{5,1},{6,2},{7,3},{8,12},{9,13},{10,... | collective-permute-start | bytes 80 | tf_op jit(solution)/shard_map/ppermute | solution.py:26
  12.5 1.5 %collective-permute-start.5 = (bf16[256,512]{1,0:T(8,128)(2,1)S(1)}, bf16[256,512]{1,0:T(8,128)(2,1)S(1)}, u32[]{:S(2)}, u32[]{:S(2)}) collective-permute-start(bf16[256,512]{1,0:T(8,128)(2,1)S(1)} %get-tuple-element.48), channel_id=1, source_target_pairs={{0,1},{1,0},{2,3},{3,2},{4,5},{5,4},{6,7},{7,6},{8,9},{9,8},{10,11... | collective-permute-start | bytes 786440 | tf_op jit(solution)/shard_map/ppermute | solution.py:26
  13.0 1.5 %collective-permute-start.6 = (bf16[256,512]{1,0:T(8,128)(2,1)S(1)}, bf16[256,512]{1,0:T(8,128)(2,1)S(1)}, u32[]{:S(2)}, u32[]{:S(2)}) collective-permute-start(bf16[256,512]{1,0:T(8,128)(2,1)S(1)} %get-tuple-element.49), channel_id=1, source_target_pairs={{0,1},{1,0},{2,3},{3,2},{4,5},{5,4},{6,7},{7,6},{8,9},{9,8},{10,11... | collective-permute-start | bytes 786440 | tf_op jit(solution)/shard_map/ppermute | solution.py:26
  13.1 2.8 %collective-permute-start.7 = (bf16[384,512]{1,0:T(8,128)(2,1)S(1)}, bf16[384,512]{1,0:T(8,128)(2,1)S(1)}, u32[]{:S(2)}, u32[]{:S(2)}) collective-permute-start(bf16[384,512]{1,0:T(8,128)(2,1)S(1)} %collective-permute-done.1.refs_0_.refs_2_), channel_id=1, source_target_pairs={{0,1},{1,0},{2,3},{3,2},{4,5},{5,4},{6,7},{7,6},{8,9},{9,8},{10,11... | collective-permute-start | bytes 1179656 | tf_op jit(solution)/shard_map/ppermute | solution.py:26
  15.9 6.4 %copy-start.2 = (f32[1,3,256,512]{3,2,1,0:T(8,128)S(1)}, f32[1,3,256,512]{3,2,1,0:T(8,128)}, u32[]{:S(2)}) copy-start(f32[1,3,256,512]{3,2,1,0:T(8,128)} %param.15) | copy-start | bytes 4718596
  15.9 6.3 %copy-start.3 = (f32[1,3,256,256]{3,2,1,0:T(8,128)S(1)}, f32[1,3,256,256]{3,2,1,0:T(8,128)}, u32[]{:S(2)}) copy-start(f32[1,3,256,256]{3,2,1,0:T(8,128)} %param.13) | copy-start | bytes 2359300
  15.9 6.3 %copy-start.5 = (f32[1,2,256,256]{3,2,1,0:T(8,128)S(1)}, f32[1,2,256,256]{3,2,1,0:T(8,128)}, u32[]{:S(2)}) copy-start(f32[1,2,256,256]{3,2,1,0:T(8,128)} %param.14) | copy-start | bytes 1572868
  17.0 7.2 %collective-permute-start.10 = (bf16[64,384]{1,0:T(8,128)(2,1)S(1)}, bf16[64,384]{1,0:T(8,128)(2,1)S(1)}, u32[]{:S(2)}, u32[]{:S(2)}) collective-permute-start(bf16[64,384]{1,0:T(8,128)(2,1)S(1)} %get-tuple-element.58), channel_id=1, source_target_pairs={{0,6},{1,7},{2,4},{3,5},{4,2},{5,3},{6,0},{7,1},{8,14},{9,15},{10,... | collective-permute-start | bytes 147464 | tf_op jit(solution)/shard_map/ppermute | solution.py:26
  19.7 4.6 %collective-permute-start.8 = (bf16[64,384]{1,0:T(8,128)(2,1)S(1)}, bf16[64,384]{1,0:T(8,128)(2,1)S(1)}, u32[]{:S(2)}, u32[]{:S(2)}) collective-permute-start(bf16[64,384]{1,0:T(8,128)(2,1)S(1)} %get-tuple-element.56), channel_id=1, source_target_pairs={{0,2},{1,3},{2,0},{3,1},{4,6},{5,7},{6,4},{7,5},{8,10},{9,11},{10,... | collective-permute-start | bytes 147464 | tf_op jit(solution)/shard_map/ppermute | solution.py:26
  20.2 4.1 %collective-permute-start.9 = (bf16[64,384]{1,0:T(8,128)(2,1)S(1)}, bf16[64,384]{1,0:T(8,128)(2,1)S(1)}, u32[]{:S(2)}, u32[]{:S(2)}) collective-permute-start(bf16[64,384]{1,0:T(8,128)(2,1)S(1)} %get-tuple-element.57), channel_id=1, source_target_pairs={{0,4},{1,5},{2,6},{3,7},{4,0},{5,1},{6,2},{7,3},{8,12},{9,13},{10,... | collective-permute-start | bytes 147464 | tf_op jit(solution)/shard_map/ppermute | solution.py:26
  20.5 15.0 %collective-permute-start.11 = (bf16[2,256,512]{2,1,0:T(8,128)(2,1)S(1)}, bf16[2,256,512]{2,1,0:T(8,128)(2,1)S(1)}, u32[]{:S(2)}, u32[]{:S(2)}) collective-permute-start(bf16[2,256,512]{2,1,0:T(8,128)(2,1)S(1)} %get-tuple-element.66), channel_id=1, source_target_pairs={{0,2},{1,3},{2,0},{3,1},{4,6},{5,7},{6,4},{7,5},{8,10},{9,11},{10,... | collective-permute-start | bytes 1572872 | tf_op jit(solution)/shard_map/ppermute | solution.py:26
  25.5 10.0 %collective-permute-start.12 = (bf16[2,64,256]{2,1,0:T(8,128)(2,1)S(1)}, bf16[2,64,256]{2,1,0:T(8,128)(2,1)S(1)}, u32[]{:S(2)}, u32[]{:S(2)}) collective-permute-start(bf16[2,64,256]{2,1,0:T(8,128)(2,1)S(1)} %get-tuple-element.67), channel_id=1, source_target_pairs={{0,8},{1,9},{2,10},{3,11},{4,12},{5,13},{6,14},{7,15},{8,0},{9,1},... | collective-permute-start | bytes 196616 | tf_op jit(solution)/shard_map/ppermute | solution.py:26
  27.2 4.8 %collective-permute-start.13 = (bf16[1,64,256]{2,1,0:T(8,128)(2,1)S(1)}, bf16[1,64,256]{2,1,0:T(8,128)(2,1)S(1)}, u32[]{:S(2)}, u32[]{:S(2)}) collective-permute-start(bf16[1,64,256]{2,1,0:T(8,128)(2,1)S(1)} %get-tuple-element.68), channel_id=1, source_target_pairs={{0,16},{1,17},{2,18},{3,19},{4,20},{5,21},{6,22},{7,23},{8,24},{9,... | collective-permute-start | bytes 98312 | tf_op jit(solution)/shard_map/ppermute | solution.py:26
  29.8 5.7 %collective-permute-start.14 = (bf16[1,64,256]{2,1,0:T(8,128)(2,1)S(1)}, bf16[1,64,256]{2,1,0:T(8,128)(2,1)S(1)}, u32[]{:S(2)}, u32[]{:S(2)}) collective-permute-start(bf16[1,64,256]{2,1,0:T(8,128)(2,1)S(1)} %get-tuple-element.68), channel_id=1, source_target_pairs={{0,24},{1,25},{2,26},{3,27},{4,28},{5,29},{6,30},{7,31},{8,16},{9,... | collective-permute-start | bytes 98312 | tf_op jit(solution)/shard_map/ppermute | solution.py:26
  30.0 10.6 %collective-permute-start.18 = (bf16[2,256,512]{2,1,0:T(8,128)(2,1)S(1)}, bf16[2,256,512]{2,1,0:T(8,128)(2,1)S(1)}, u32[]{:S(2)}, u32[]{:S(2)}) collective-permute-start(bf16[2,256,512]{2,1,0:T(8,128)(2,1)S(1)} %get-tuple-element.74.refs_4_), channel_id=1, source_target_pairs={{0,1},{1,0},{2,3},{3,2},{4,5},{5,4},{6,7},{7,6},{8,9},{9,8},{10,11... | collective-permute-start | bytes 1572872 | tf_op jit(solution)/shard_map/ppermute | solution.py:26
  35.7 6.3 %collective-permute-start.19 = (bf16[2,256,512]{2,1,0:T(8,128)(2,1)S(1)}, bf16[2,256,512]{2,1,0:T(8,128)(2,1)S(1)}, u32[]{:S(2)}, u32[]{:S(2)}) collective-permute-start(bf16[2,256,512]{2,1,0:T(8,128)(2,1)S(1)} %add_convert_fusion.refs_5_), channel_id=1, source_target_pairs={{0,1},{1,0},{2,3},{3,2},{4,5},{5,4},{6,7},{7,6},{8,9},{9,8},{10,11... | collective-permute-start | bytes 1572872 | tf_op jit(solution)/shard_map/ppermute | solution.py:26
  35.7 6.2 %copy-start.1 = (bf16[1,2048,512]{2,1,0:T(8,128)(2,1)S(1)}, bf16[1,2048,512]{2,1,0:T(8,128)(2,1)}, u32[]{:S(2)}) copy-start(bf16[1,2048,512]{2,1,0:T(8,128)(2,1)} %param.9) | copy-start | bytes 6291460
  37.0 7.7 %collective-permute-start.16 = (bf16[64,384]{1,0:T(8,128)(2,1)S(1)}, bf16[64,384]{1,0:T(8,128)(2,1)S(1)}, u32[]{:S(2)}, u32[]{:S(2)}) collective-permute-start(bf16[64,384]{1,0:T(8,128)(2,1)S(1)} %get-tuple-element.73), channel_id=1, source_target_pairs={{0,4},{1,5},{2,6},{3,7},{4,0},{5,1},{6,2},{7,3},{8,12},{9,13},{10,... | collective-permute-start | bytes 147464 | tf_op jit(solution)/shard_map/ppermute | solution.py:26
  38.4 6.3 %collective-permute-start.17 = (bf16[64,384]{1,0:T(8,128)(2,1)S(1)}, bf16[64,384]{1,0:T(8,128)(2,1)S(1)}, u32[]{:S(2)}, u32[]{:S(2)}) collective-permute-start(bf16[64,384]{1,0:T(8,128)(2,1)S(1)} %get-tuple-element.73), channel_id=1, source_target_pairs={{0,6},{1,7},{2,4},{3,5},{4,2},{5,3},{6,0},{7,1},{8,14},{9,15},{10,... | collective-permute-start | bytes 147464 | tf_op jit(solution)/shard_map/ppermute | solution.py:26
  40.0 6.8 %collective-permute-start.24 = (f32[3,64,256]{2,1,0:T(8,128)S(1)}, f32[3,64,256]{2,1,0:T(8,128)S(1)}, u32[]{:S(2)}, u32[]{:S(2)}) collective-permute-start(f32[3,64,256]{2,1,0:T(8,128)S(1)} %get-tuple-element.85), channel_id=1, source_target_pairs={{0,4},{1,5},{2,6},{3,7},{4,0},{5,1},{6,2},{7,3},{8,12},{9,13},{10,... | collective-permute-start | bytes 589832 | tf_op jit(solution)/shard_map/ppermute | solution.py:26
  40.6 4.2 %collective-permute-start.15 = (bf16[64,384]{1,0:T(8,128)(2,1)S(1)}, bf16[64,384]{1,0:T(8,128)(2,1)S(1)}, u32[]{:S(2)}, u32[]{:S(2)}) collective-permute-start(bf16[64,384]{1,0:T(8,128)(2,1)S(1)} %get-tuple-element.80.refs_0_), channel_id=1, source_target_pairs={{0,2},{1,3},{2,0},{3,1},{4,6},{5,7},{6,4},{7,5},{8,10},{9,11},{10,... | collective-permute-start | bytes 147464 | tf_op jit(solution)/shard_map/ppermute | solution.py:26
  44.8 3.5 %collective-permute-start.20 = (bf16[64,384]{1,0:T(8,128)(2,1)S(1)}, bf16[64,384]{1,0:T(8,128)(2,1)S(1)}, u32[]{:S(2)}, u32[]{:S(2)}) collective-permute-start(bf16[64,384]{1,0:T(8,128)(2,1)S(1)} %get-tuple-element.80.refs_0_), channel_id=1, source_target_pairs={{0,1},{1,0},{2,3},{3,2},{4,5},{5,4},{6,7},{7,6},{8,9},{9,8},{10,11... | collective-permute-start | bytes 147464 | tf_op jit(solution)/shard_map/ppermute | solution.py:26
  44.9 3.5 %collective-permute-start.21 = (bf16[64,384]{1,0:T(8,128)(2,1)S(1)}, bf16[64,384]{1,0:T(8,128)(2,1)S(1)}, u32[]{:S(2)}, u32[]{:S(2)}) collective-permute-start(bf16[64,384]{1,0:T(8,128)(2,1)S(1)} %collective-permute-done.15.refs_1_), channel_id=1, source_target_pairs={{0,1},{1,0},{2,3},{3,2},{4,5},{5,4},{6,7},{7,6},{8,9},{9,8},{10,11... | collective-permute-start | bytes 147464 | tf_op jit(solution)/shard_map/ppermute | solution.py:26
  45.4 3.0 %collective-permute-start.22 = (bf16[64,384]{1,0:T(8,128)(2,1)S(1)}, bf16[64,384]{1,0:T(8,128)(2,1)S(1)}, u32[]{:S(2)}, u32[]{:S(2)}) collective-permute-start(bf16[64,384]{1,0:T(8,128)(2,1)S(1)} %collective-permute-done.16.refs_2_), channel_id=1, source_target_pairs={{0,1},{1,0},{2,3},{3,2},{4,5},{5,4},{6,7},{7,6},{8,9},{9,8},{10,11... | collective-permute-start | bytes 147464 | tf_op jit(solution)/shard_map/ppermute | solution.py:26
  45.4 2.9 %collective-permute-start.23 = (bf16[64,384]{1,0:T(8,128)(2,1)S(1)}, bf16[64,384]{1,0:T(8,128)(2,1)S(1)}, u32[]{:S(2)}, u32[]{:S(2)}) collective-permute-start(bf16[64,384]{1,0:T(8,128)(2,1)S(1)} %collective-permute-done.17.refs_3_), channel_id=1, source_target_pairs={{0,1},{1,0},{2,3},{3,2},{4,5},{5,4},{6,7},{7,6},{8,9},{9,8},{10,11... | collective-permute-start | bytes 147464 | tf_op jit(solution)/shard_map/ppermute | solution.py:26
  (2 other events, 2.6 us)

commit v4 on v3

v4 whole, which is shorter than its diff:
```python
import functools

import jax
import jax.numpy as jnp
from jax import lax
from jax.experimental import pallas as pl
from jax.experimental.pallas import tpu as pltpu
from jax.sharding import PartitionSpec as P

F32 = jnp.float32
BF16 = jnp.bfloat16
HIGHEST = lax.Precision.HIGHEST
NN = (((1,), (0,)), ((), ()))
NT = (((1,), (1,)), ((), ()))
TN = (((0,), (0,)), ((), ()))
AXES = ("leaf", "col")


def moved(block, leaf_flip, col_flip):
    leaves, groups = lax.axis_size("leaf"), lax.axis_size("col")
    route = [
        (leaf * groups + col, (leaf ^ leaf_flip) * groups + (col ^ col_flip))
        for leaf in range(leaves)
        for col in range(groups)
    ]
    return lax.ppermute(block, AXES, route)


COST = {}


def call(body, outs, smem, vmem, scratch=(), limit=24, space=pltpu.VMEM):
    title = getattr(body, "func", body).__name__
    cost = None
    if COST.get(title, 1):
        cost = pl.CostEstimate(flops=10**9, bytes_accessed=0, transcendentals=0)
    specs = [pl.BlockSpec(memory_space=pltpu.SMEM)] * len(smem)
    specs += [pl.BlockSpec(memory_space=pltpu.VMEM)] * len(vmem)
    return pl.pallas_call(
        body,
        out_shape=outs,
        in_specs=specs,
        out_specs=[pl.BlockSpec(memory_space=space)] * len(outs),
        scratch_shapes=scratch,
        compiler_params=pltpu.CompilerParams(vmem_limit_bytes=limit << 20),
        cost_estimate=pl.CostEstimate(flops=5 * 10**9, bytes_accessed=0, transcendentals=0),
        name=title,
    )(*smem, *vmem)


def position():
    column = lax.axis_index("col")
    return column, lax.axis_index("leaf") & 1, column // (lax.axis_size("col") // 2)


def dot(a, b, dims):
    return lax.dot_general(a, b, dims, preferred_element_type=F32)


def split(value):
    high = value.astype(BF16)
    return high, (value - high.astype(F32)).astype(BF16)


def dot_split(value, high, low, dims):
    first, second = split(value)
    return dot(first, high, dims) + (dot(first, low, dims) + dot(second, high, dims))


def rows_at(start, size):
    return pl.ds(pl.multiple_of(start, size), size)


def prepare(spots, inverse, link, rhs, k_high, k_low, right, place):
    column, side, _ = position()
    levels, share, sep_rows = right.shape
    touched = place.shape[1] // 2
    wide = 2 * share
    shift = lax.broadcasted_iota(jnp.int32, (touched, sep_rows), 1) - lax.broadcasted_iota(
        jnp.int32, (touched, sep_rows), 0
    )
    for k in range(levels):
        for n in range(2):
            chosen = jnp.where(shift == spots[2 * n, k], spots[2 * n + 1, k].astype(F32), 0.0)
            place[k, n * touched : (n + 1) * touched] = chosen.astype(BF16)
        if k + 1 < levels:
            high, low = split(
                lax.dot_general(
                    link[k], inverse[k], NN, precision=HIGHEST, preferred_element_type=F32
                )
            )
            k_high[k] = high
            k_low[k] = low
        part = rhs[k, :, rows_at(column * wide, wide)].T
        right[k] = jnp.where(side == 0, part[:share], part[share:])


def squares(inverse, q_high, q_low):
    for k in range(inverse.shape[0]):
        block = inverse[k]
        high, low = split(
            lax.dot_general(block, block, TN, precision=HIGHEST, preferred_element_type=F32)
        )
        q_high[k] = high
        q_low[k] = low


def leaf_products(inverse, rhs, keep, *refs):
    *sends, order = refs
    column, _, _ = position()
    groups, wide, rows = inverse.shape[0] // rhs.shape[0], keep.shape[1] // 2, rhs.shape[0]
    half = groups // 2
    order[...] = rhs[...].T
    turned = jnp.concatenate(
        [
            order[rows_at((((column ^ j) & (half - 1)) + top * half) * wide, wide), :]
            for j in range(half)
            for top in range(2)
        ],
        axis=0,
    )
    for block in range(groups):
        value = dot(turned, inverse[block * rows : (block + 1) * rows, :], NT)
        keep[block] = value[: 2 * wide]
        for j in range(1, half):
            part = value[2 * wide * j : 2 * wide * (j + 1)]
            sends[(j - 1) * groups + block][...] = part.astype(BF16)


def own_partials(masks, keep, *refs):
    panels, received = refs[: len(masks)], refs[len(masks) : -3]
    low, high, out = refs[-3:]
    column, _, top = position()
    half = low.shape[0]
    for block in range(2 * half):
        value = keep[block]
        for r in received[block :: 2 * half]:
            value += r[...].astype(F32)
        if block < half:
            low[block] = value.astype(BF16)
        else:
            high[block - half] = value.astype(BF16)
    out[...] = panel_products(top, column, masks, panels, low, high)


def panel_products(top, column, masks, panels, low, high):
    half = low.shape[0]
    total = None
    for mask, panel in zip(masks, panels):
        block = (column ^ mask) & (half - 1)
        value = dot(jnp.where(top == 0, low[block], high[block]), panel[...], NT)
        total = value if total is None else total + value
    return total


def partials(masks, low, high, early, *refs):
    panels = refs[: len(masks)]
    own, same, other, cross, scratch = refs[len(masks) :]
    column, side, top = position()
    share = own.shape[0]
    scratch[...] = early[...] + panel_products(1 - top, column, masks, panels, low, high)

    def piece(which_top, which_side):
        return scratch[rows_at((which_top * 2 + which_side) * share, share), :]

    own[...] = piece(top, side)
    same[...] = piece(1 - top, side).astype(BF16)
    other[...] = piece(top, 1 - side).astype(BF16)
    cross[...] = piece(1 - top, 1 - side).astype(BF16)


def upward(own, cross, same, other, right, k_high, k_low, place, kept, *sends):
    levels = right.shape[0]
    touched = place.shape[1] // 2
    mine = own[...] + same[...].astype(F32)
    theirs = other[...].astype(F32) + cross[...].astype(F32)
    carried = None
    for k in range(levels):
        at = slice(k * touched, (k + 1) * touched)
        high, low = split(jnp.concatenate([mine[:, at], theirs[:, at]], axis=1))
        value = dot(high, place[k], NN) + dot(low, place[k], NN)
        if k > 0:
            value += carried
        kept[k] = value
        for j in range(min(k, len(sends))):
            sends[j][k - 1 - j] = value.astype(BF16)
        if k + 1 < levels:
            rest = right[k] * (0.5**k) - value
            carried = dot_split(rest, k_high[k], k_low[k], NT)


def downward(lengths, kept, right, q_high, q_low, k_high, k_low, place, *refs):
    received = refs[: len(lengths)]
    solution, mine, theirs, passed = refs[len(lengths) :]
    levels = right.shape[0]
    touched = place.shape[1] // 2
    parent = None
    for k in reversed(range(levels)):
        value = right[k] - kept[k]
        for length, block in zip(lengths, received):
            if length <= k:
                value -= block[k - length].astype(F32)
        answer = dot_split(value, q_high[k], q_low[k], NN)
        if parent is not None:
            answer -= dot_split(parent, k_high[k], k_low[k], NN)
        parent = answer
        solution[k] = answer
        rounded = answer.astype(BF16)
        pieces = dot(rounded, place[k], NT).astype(BF16)
        at = slice(k * touched, (k + 1) * touched)
        mine[:, at] = pieces[:, :touched]
        theirs[:, at] = pieces[:, touched:]
        passed[k] = rounded


def lower_transposed(masks, half, inverse, *refs):
    panels, blocks = refs[: len(masks)], refs[len(masks) : -2]
    out, weight_turned = refs[-2:]
    column, _, _ = position()
    rows = inverse.shape[1]
    weight = None
    for mask, panel in zip(masks, panels):
        value = dot(panel[...], inverse[rows_at((column ^ mask) * rows, rows), :], NN)
        weight = value if weight is None else weight + value
    weight_turned[...] = weight.T.astype(BF16)
    total = None
    for block in range(half):
        left = jnp.concatenate([piece[block] for piece in blocks], axis=0)
        value = dot(left, inverse[block * rows : (block + 1) * rows, :], NN)
        total = value if total is None else total + value
    out[...] = total


def upper_transposed(half, inverse, lower, *refs):
    blocks, out = refs[:-1], refs[-1]
    column, _, _ = position()
    rows = inverse.shape[1]
    total = lower[...]
    for block in range(half):
        left = jnp.concatenate([piece[block] for piece in blocks], axis=0)
        at = (half + block) * rows
        total += dot(left, inverse[at : at + rows, :], NN)
    wide = total.shape[0] // (2 * half)
    for j in range(half):
        for top in range(2):
            source = ((column ^ j) & (half - 1)) + top * half
            at = (2 * j + top) * wide
            out[:, rows_at(source * wide, wide)] = total[at : at + wide].T


def finish(half, base, weight_turned, *refs):
    out, gathered, staged, sems = refs[-4:]
    blocks = refs[:-4]
    column, side, top = position()
    share = blocks[0].shape[0]
    for j in range(half):
        inner = (column ^ j) & (half - 1)
        for n, (flip_side, flip_top) in enumerate(((0, 0), (0, 1), (1, 0), (1, 1))):
            which_top = top ^ flip_top
            which_side = side ^ flip_side
            at = ((which_top * half + inner) * 2 + which_side) * share
            gathered[rows_at(at, share), :] = blocks[4 * j + n][...]
    pieces = sems.shape[0]
    size = out.shape[1] // pieces
    copies = []
    for n in range(pieces):
        part = pl.ds(n * size, size)
        value = base[:, part] - dot(weight_turned[...], gathered[part, :], NT)
        staged[:, part] = value.astype(BF16)
        copy = pltpu.make_async_copy(staged.at[:, part], out.at[:, part], sems.at[n])
        copy.start()
        copies.append(copy)
    for copy in copies:
        copy.wait()


def assemble(mine, passed, out, staged, sems):
    _, side, _ = position()
    copies = []
    for k in range(mine.shape[0]):
        other = passed[k].astype(F32)
        left = jnp.where(side == 0, mine[k], other)
        right = jnp.where(side == 0, other, mine[k])
        staged[k] = jnp.concatenate([left, right], axis=0).T
        copy = pltpu.make_async_copy(staged.at[k], out.at[k], sems.at[k])
        copy.start()
        copies.append(copy)
    for copy in copies:
        copy.wait()


def on_device(leaf_rhs, leaf_inverse, panels, pattern, offsets, sep_inverse, sep_link, sep_rhs):
    rhs, inverse = leaf_rhs[0], leaf_inverse[0]
    rows, sources = rhs.shape
    leaves, groups = lax.axis_size("leaf"), lax.axis_size("col")
    levels = leaves.bit_length() - 1
    half = groups // 2
    touched, sep_rows = panels.shape[2], sep_inverse.shape[2]
    share = sources // groups // 2
    panel = panels[0].reshape(levels * touched, rows)
    def shape(dims, dtype=F32):
        return jax.ShapeDtypeStruct(dims, dtype)

    held = {0: panel, half: moved(panel, 0, half)}
    for mask in range(1, half):
        held[mask] = moved(panel, 0, mask)

    mine_rows = (groups, sources // half, rows)
    upper_rows = (half, sources // half, rows)
    keep, *sends = call(
        leaf_products,
        [shape(mine_rows)] + [shape(mine_rows[1:], BF16)] * ((half - 1) * groups),
        [],
        [inverse, rhs],
        [pltpu.VMEM((sources, rows), BF16)],
    )
    keep, offsets, pattern = lax.optimization_barrier((keep, offsets, pattern))
    spots = jnp.concatenate([offsets, pattern], axis=0)
    spots = jnp.concatenate([spots, moved(spots, 1, 0)], axis=0)
    received = [moved(block, 0, n // groups + 1) for n, block in enumerate(sends)]

    near, far = list(range(half)), list(range(half, groups))
    partial_shape = (sources // half, levels * touched)
    keep, held[half] = lax.optimization_barrier((keep, held[half]))
    low, high, early = call(
        functools.partial(own_partials, near),
        [shape(upper_rows, BF16)] * 2 + [shape(partial_shape)],
        [],
        [keep] + [held[mask] for mask in near] + received,
    )
    for mask in range(1, half):
        held[half | mask] = moved(held[half], 0, mask)
    piece = (share, levels * touched)
    own, same, other, cross = call(
        functools.partial(partials, far),
        [shape(piece)] + [shape(piece, BF16)] * 3,
        [],
        [low, high, early] + [held[mask] for mask in far],
        [pltpu.VMEM(partial_shape, F32)],
    )
    high, own, inverses = lax.optimization_barrier((high, own, sep_inverse[0]))
    cross = moved(cross, 1, half)
    same, other = moved(same, 0, half), moved(other, 1, 0)

    high = moved(high, 0, half)

    k_high, k_low, right, place = call(
        prepare,
        [shape((levels - 1, sep_rows, sep_rows), BF16)] * 2
        + [shape((levels, share, sep_rows)), shape((levels, 2 * touched, sep_rows), BF16)],
        [spots],
        [inverses, sep_link[0], sep_rhs[0]],
    )
    kept, *up_sends = call(
        upward,
        [shape((levels, share, sep_rows))]
        + [shape((levels - length, share, sep_rows), BF16) for length in range(1, levels)],
        [],
        [own, cross, same, other, right, k_high, k_low, place],
    )
    lengths, up_received = [], []
    for delta in range(1, leaves // 2):
        lengths.append(delta.bit_length())
        up_received.append(moved(up_sends[delta.bit_length() - 1], 2 * delta, 0))
    kept, inverse, inverses = lax.optimization_barrier((kept, inverse, inverses))
    masks = near + far
    lower, weight_turned = call(
        functools.partial(lower_transposed, masks, half),
        [shape((sources, rows)), shape((rows, levels * touched), BF16)],
        [],
        [inverse] + [held[mask] for mask in masks] + [low] + [moved(low, 0, j) for j in range(1, half)],
    )
    lower, inverses = lax.optimization_barrier((lower, inverses))
    q_high, q_low = call(
        squares, [shape((levels, sep_rows, sep_rows), BF16)] * 2, [], [inverses]
    )

    answer, mine, theirs, passed = call(
        functools.partial(downward, lengths),
        [shape((levels, share, sep_rows))]
        + [shape(piece, BF16)] * 2
        + [shape((levels, share, sep_rows), BF16)],
        [],
        [kept, right, q_high, q_low, k_high, k_low, place, *up_received],
    )

    high, mine = lax.optimization_barrier((high, mine))
    solved = keep[half:] + high.astype(F32)
    for n, block in enumerate(received):
        if n % groups >= half:
            solved = solved.at[n % groups - half].add(block.astype(F32))
    solved = solved.astype(BF16)
    solved = [solved] + [moved(solved, 0, j) for j in range(1, half)]
    *solved, passed = lax.optimization_barrier((*solved, passed))
    base = call(
        functools.partial(upper_transposed, half),
        [shape((rows, sources))],
        [],
        [inverse, lower, *solved],
    )[0]

    cross = moved(theirs, 1, half)
    blocks = [mine, moved(mine, 0, half), moved(theirs, 1, 0), cross]
    passed = moved(passed, 1, 0)
    *blocks, base = lax.optimization_barrier((*blocks, base))
    weight_turned, passed = lax.optimization_barrier((weight_turned, passed))
    for j in range(1, half):
        blocks += [moved(block, 0, j) for block in blocks[:4]]
    final = call(
        functools.partial(finish, half),
        [shape((rows, sources), BF16)],
        [],
        [base, weight_turned, *blocks],
        [
            pltpu.VMEM((sources, levels * touched), BF16),
            pltpu.VMEM((rows, sources), BF16),
            pltpu.SemaphoreType.DMA((half,)),
        ],
        space=pl.ANY,
    )[0]
    solution_rows = call(
        assemble,
        [shape((levels, sep_rows, 2 * share))],
        [],
        [answer, passed],
        [pltpu.VMEM((levels, sep_rows, 2 * share), F32), pltpu.SemaphoreType.DMA((levels,))],
        space=pl.ANY,
    )[0]
    return final[None], solution_rows[None]


def solution(mesh):
    in_specs = (
        P("leaf", "col", None),
        P("leaf", None, "col"),
        P("leaf", None, None, "col"),
        P("leaf", None),
        P("leaf", None),
        P("leaf", None, None, None),
        P("leaf", None, None, None),
        P("leaf", None, None, None),
    )
    out_specs = (P("leaf", "col", None), P("leaf", None, None, "col"))
    return jax.shard_map(
        on_device, mesh=mesh, in_specs=in_specs, out_specs=out_specs, check_vma=False
    )
```

time: 50.4 us -> 45.4 us (0.901)
  Pallas kernels: 14.7 us -> 10.9 us
  waiting for transfers between devices: 10.2 us -> 8.72 us
    pallas_call x9 -> x11, Pallas kernels: 14.7 us -> 10.9 us  [call(): pl.pallas_call(body, out_shape=outs, in_specs=specs, out_specs=[pl.BlockS...]
    ppermute x25, waiting for transfers between devices: 10.2 us -> 8.72 us  [moved(): return lax.ppermute(block, AXES, route)]
  transfers between devices with their start and end apart: 25 -> 25, of which waited for: 8 -> 9; matrix products, arithmetic and copies ran while one was open for 1% -> 0% of each run, Pallas kernels for 24% -> 21%
where the time goes in v4:
time: 45.4 us; the launch traced here: 45.3 us
  starting transfers between devices  21.7 us (48%)
  Pallas kernels  10.9 us (24%)
  waiting for transfers between devices  8.72 us (19%)
  local copies, waits for them, and re-layouts  2.66 us (6%)
  between operations  0.85 us (2%)
  other arithmetic  0.51 us (1%)
    ppermute x25, starting transfers between devices, moved(): return lax.ppermute(block, AXES, route)  21.7 us
    pallas_call x11, Pallas kernels, call(): pl.pallas_call(body, out_shape=outs, in_specs=specs, out_specs=[pl.BlockS...  10.9 us
    ppermute x25, waiting for transfers between devices, moved(): return lax.ppermute(block, AXES, route)  8.72 us
    unnamed x18, local copies, waits for them, and re-layouts  2.66 us
  transfers between devices with their start and end apart: 25, of which 9 were waited for; matrix products, arithmetic and copies ran while one was open for 0% of the time, Pallas kernels for 21%

profile of v4, /device:TPU:0, one launch (start us, length us, event | category | flops | bytes accessed | tf_op | source)
XLA Modules:
  0.0 45.3 jit_solution(14750051468222786186)
XLA Ops:
  0.6 0.5 %collective-permute-start.1 = (bf16[384,512]{1,0:T(8,128)(2,1)}, bf16[384,512]{1,0:T(8,128)(2,1)S(1)}, u32[]{:S(2)}, u32[]{:S(2)}) collective-permute-start(bf16[384,512]{1,0:T(8,128)(2,1)} %bitcast.22), channel_id=1, source_target_pairs={{0,1},{1,0},{2,3},{3,2},{4,5},{5,4},{6,7},{7,6},{8,9},{9,8},{10,11... | collective-permute-start | bytes 1179656 | tf_op jit(solution)/shard_map/ppermute | solution.py:26
  1.1 2.6 %collective-permute-start = (bf16[384,512]{1,0:T(8,128)(2,1)}, bf16[384,512]{1,0:T(8,128)(2,1)S(1)}, u32[]{:S(2)}, u32[]{:S(2)}) collective-permute-start(bf16[384,512]{1,0:T(8,128)(2,1)} %bitcast.23), channel_id=1, source_target_pairs={{0,2},{1,3},{2,0},{3,1},{4,6},{5,7},{6,4},{7,5},{8,10},{9,11},{10,... | collective-permute-start | bytes 1179656 | tf_op jit(solution)/shard_map/ppermute | solution.py:26
  3.7 1.6 %copy-done = bf16[1,2048,512]{2,1,0:T(8,128)(2,1)S(1)} copy-done((bf16[1,2048,512]{2,1,0:T(8,128)(2,1)S(1)}, bf16[1,2048,512]{2,1,0:T(8,128)(2,1)}, u32[]{:S(2)}) %copy-start) | copy-done | bytes 2097176
  5.3 1.0 %copy-done.4 = bf16[1,512,512]{2,1,0:T(8,128)(2,1)S(1)} copy-done((bf16[1,512,512]{2,1,0:T(8,128)(2,1)S(1)}, bf16[1,512,512]{2,1,0:T(8,128)(2,1)}, u32[]{:S(2)}) %copy-start.4) | copy-done | bytes 524312
  6.4 1.3 %leaf_products.1 = (f32[4,256,512]{2,1,0:T(8,128)S(1)}, bf16[256,512]{1,0:T(8,128)(2,1)S(1)}, bf16[256,512]{1,0:T(8,128)(2,1)S(1)}, bf16[256,512]{1,0:T(8,128)(2,1)S(1)}, bf16[256,512]{1,0:T(8,128)(2,1)S(1)}) custom-call(bf16[2048,512]{1,0:T(8,128)(2,1)S(1)} %bitcast.14, bf16[512,512]{1,0:T(8,128)(2,1)S(1)} %bitcast.20), custom_call_target="tpu_custom_call" | custom-call | flops 5000000000 | tf_op jit(solution)/shard_map/leaf_products/pallas_call | solution.py:39
  7.7 1.6 %collective-permute-start.11 = (s32[2,3]{1,0:T(2,128)S(1)}, s32[2,3]{1,0:T(2,128)S(1)}, u32[]{:S(2)}, u32[]{:S(2)}) collective-permute-start(s32[2,3]{1,0:T(2,128)S(1)} %pad_add_fusion.1), channel_id=1, source_target_pairs={{0,4},{1,5},{2,6},{3,7},{4,0},{5,1},{6,2},{7,3},{8,12},{9,13},{10,... | collective-permute-start | bytes 80 | tf_op jit(solution)/shard_map/ppermute | solution.py:26
  9.3 0.5 %collective-permute-start.3 = (bf16[256,512]{1,0:T(8,128)(2,1)S(1)}, bf16[256,512]{1,0:T(8,128)(2,1)S(1)}, u32[]{:S(2)}, u32[]{:S(2)}) collective-permute-start(bf16[256,512]{1,0:T(8,128)(2,1)S(1)} %get-tuple-element.82), channel_id=1, source_target_pairs={{0,1},{1,0},{2,3},{3,2},{4,5},{5,4},{6,7},{7,6},{8,9},{9,8},{10,11... | collective-permute-start | bytes 786440 | tf_op jit(solution)/shard_map/ppermute | solution.py:26
  9.8 1.6 %collective-permute-done.11 = s32[2,3]{1,0:T(2,128)S(1)} collective-permute-done((s32[2,3]{1,0:T(2,128)S(1)}, s32[2,3]{1,0:T(2,128)S(1)}, u32[]{:S(2)}, u32[]{:S(2)}) %collective-permute-start.11) | collective-permute-done | bytes 56 | tf_op jit(solution)/shard_map/ppermute | solution.py:26
  11.4 2.3 %collective-permute-done.refs_0_.refs_2_ = bf16[384,512]{1,0:T(8,128)(2,1)S(1)} collective-permute-done((bf16[384,512]{1,0:T(8,128)(2,1)}, bf16[384,512]{1,0:T(8,128)(2,1)S(1)}, u32[]{:S(2)}, u32[]{:S(2)}) %collective-permute-start) | collective-permute-done | bytes 393248 | tf_op jit(solution)/shard_map/ppermute | solution.py:26
  13.7 0.6 %collective-permute-start.6 = (bf16[384,512]{1,0:T(8,128)(2,1)S(1)}, bf16[384,512]{1,0:T(8,128)(2,1)S(1)}, u32[]{:S(2)}, u32[]{:S(2)}) collective-permute-start(bf16[384,512]{1,0:T(8,128)(2,1)S(1)} %collective-permute-done.refs_0_.refs_2_), channel_id=1, source_target_pairs={{0,1},{1,0},{2,3},{3,2},{4,5},{5,4},{6,7},{7,6},{8,9},{9,8},{10,11... | collective-permute-start | bytes 1179656 | tf_op jit(solution)/shard_map/ppermute | solution.py:26
  14.3 0.9 %collective-permute-done.5.refs_5_ = bf16[256,512]{1,0:T(8,128)(2,1)S(1)} collective-permute-done((bf16[256,512]{1,0:T(8,128)(2,1)S(1)}, bf16[256,512]{1,0:T(8,128)(2,1)S(1)}, u32[]{:S(2)}, u32[]{:S(2)}) %collective-permute-start.5) | collective-permute-done | bytes 262176 | tf_op jit(solution)/shard_map/ppermute | solution.py:26
  15.2 0.6 %own_partials.1 = (bf16[2,256,512]{2,1,0:T(8,128)(2,1)S(1)}, bf16[2,256,512]{2,1,0:T(8,128)(2,1)S(1)}, f32[256,384]{1,0:T(8,128)S(1)}) custom-call(f32[4,256,512]{2,1,0:T(8,128)S(1)} %get-tuple-element.80.keep, bf16[384,512]{1,0:T(8,128)(2,1)S(1)} %bitcast.24, bf16[384,512]{1,0:T(8,128)(2,1)S(1)} %collective-permute-done.1.refs_1_, ...), custom_call_target="tpu_custom_call" | custom-call | flops 5000000000 | tf_op jit(solution)/shard_map/own_partials/pallas_call | solution.py:39
  16.5 2.8 %collective-permute-start.8 = (bf16[64,384]{1,0:T(8,128)(2,1)S(1)}, bf16[64,384]{1,0:T(8,128)(2,1)S(1)}, u32[]{:S(2)}, u32[]{:S(2)}) collective-permute-start(bf16[64,384]{1,0:T(8,128)(2,1)S(1)} %get-tuple-element.92), channel_id=1, source_target_pairs={{0,6},{1,7},{2,4},{3,5},{4,2},{5,3},{6,0},{7,1},{8,14},{9,15},{10,... | collective-permute-start | bytes 147464 | tf_op jit(solution)/shard_map/ppermute | solution.py:26
  20.0 1.8 %collective-permute-start.7 = (bf16[2,256,512]{2,1,0:T(8,128)(2,1)S(1)}, bf16[2,256,512]{2,1,0:T(8,128)(2,1)S(1)}, u32[]{:S(2)}, u32[]{:S(2)}) collective-permute-start(bf16[2,256,512]{2,1,0:T(8,128)(2,1)S(1)} %get-tuple-element.90.high), channel_id=1, source_target_pairs={{0,2},{1,3},{2,0},{3,1},{4,6},{5,7},{6,4},{7,5},{8,10},{9,11},{10,... | collective-permute-start | bytes 1572872 | tf_op jit(solution)/shard_map/ppermute | solution.py:26
  21.8 1.3 %prepare.1 = (bf16[2,256,256]{2,1,0:T(8,128)(2,1)S(1)}, bf16[2,256,256]{2,1,0:T(8,128)(2,1)S(1)}, f32[3,64,256]{2,1,0:T(8,128)S(1)}, bf16[3,256,256]{2,1,0:T(8,128)(2,1)S(1)}) custom-call(s32[4,3]{1,0:T(4,128)S(1)} %pad_add_fusion.spots, f32[3,256,256]{2,1,0:T(8,128)S(1)} %bitcast.18, f32[2,256,256]{2,1,0:T(8,128)S(1)} %bitcast.21, f32[3,256,512]{2,1,0:T(8,128)S(1)} %bitcast.17), custom_call_target="tpu_custom_call" | custom-call | flops 5000000000 | tf_op jit(solution)/shard_map/prepare/pallas_call | solution.py:39
  23.1 0.7 %collective-permute-done.9.same = bf16[64,384]{1,0:T(8,128)(2,1)S(1)} collective-permute-done((bf16[64,384]{1,0:T(8,128)(2,1)S(1)}, bf16[64,384]{1,0:T(8,128)(2,1)S(1)}, u32[]{:S(2)}, u32[]{:S(2)}) %collective-permute-start.9) | collective-permute-done | bytes 49184 | tf_op jit(solution)/shard_map/ppermute | solution.py:26
  23.9 0.8 %upward.1 = (f32[3,64,256]{2,1,0:T(8,128)S(1)}, bf16[2,64,256]{2,1,0:T(8,128)(2,1)S(1)}, bf16[1,64,256]{2,1,0:T(8,128)(2,1)S(1)}) custom-call(f32[64,384]{1,0:T(8,128)S(1)} %get-tuple-element.91.own, bf16[64,384]{1,0:T(8,128)(2,1)S(1)} %collective-permute-done.8.cross, bf16[64,384]{1,0:T(8,128)(2,1)S(1)} %collective-permute-done.9.same, ...), custom_call_target="tpu_custom_call" | custom-call | flops 5000000000 | tf_op jit(solution)/shard_map/upward/pallas_call | solution.py:39
  24.7 3.6 %collective-permute-start.15 = (bf16[1,64,256]{2,1,0:T(8,128)(2,1)S(1)}, bf16[1,64,256]{2,1,0:T(8,128)(2,1)S(1)}, u32[]{:S(2)}, u32[]{:S(2)}) collective-permute-start(bf16[1,64,256]{2,1,0:T(8,128)(2,1)S(1)} %get-tuple-element.111), channel_id=1, source_target_pairs={{0,24},{1,25},{2,26},{3,27},{4,28},{5,29},{6,30},{7,31},{8,16},{9,... | collective-permute-start | bytes 98312 | tf_op jit(solution)/shard_map/ppermute | solution.py:26
  28.3 0.8 %collective-permute-start.13 = (bf16[2,64,256]{2,1,0:T(8,128)(2,1)S(1)}, bf16[2,64,256]{2,1,0:T(8,128)(2,1)S(1)}, u32[]{:S(2)}, u32[]{:S(2)}) collective-permute-start(bf16[2,64,256]{2,1,0:T(8,128)(2,1)S(1)} %get-tuple-element.110), channel_id=1, source_target_pairs={{0,8},{1,9},{2,10},{3,11},{4,12},{5,13},{6,14},{7,15},{8,0},{9,1},... | collective-permute-start | bytes 196616 | tf_op jit(solution)/shard_map/ppermute | solution.py:26
  29.2 1.5 %lower_transposed.1 = (f32[512,512]{1,0:T(8,128)S(1)}, bf16[512,384]{1,0:T(8,128)(2,1)S(1)}) custom-call(bf16[2048,512]{1,0:T(8,128)(2,1)S(1)} %bitcast.15, bf16[384,512]{1,0:T(8,128)(2,1)S(1)} %bitcast.25, bf16[384,512]{1,0:T(8,128)(2,1)S(1)} %collective-permute-done.1.refs_1_, bf16[384,512]{1,0:T(8,128)(2,1)S(1)} %collective-permute-done.refs_0_.refs_2_, ...), custom_call_target="tpu_custom_call" | custom-call | flops 5000000000 | tf_op jit(solution)/shard_map/lower_transposed/pallas_call | solution.py:39
  30.7 0.9 %squares.1 = (bf16[3,256,256]{2,1,0:T(8,128)(2,1)S(1)}, bf16[3,256,256]{2,1,0:T(8,128)(2,1)S(1)}) custom-call(f32[3,256,256]{2,1,0:T(8,128)S(1)} %bitcast.19), custom_call_target="tpu_custom_call" | custom-call | flops 5000000000 | tf_op jit(solution)/shard_map/squares/pallas_call | solution.py:39
  31.6 1.6 %collective-permute-done.14.refs_1_ = bf16[1,64,256]{2,1,0:T(8,128)(2,1)S(1)} collective-permute-done((bf16[1,64,256]{2,1,0:T(8,128)(2,1)S(1)}, bf16[1,64,256]{2,1,0:T(8,128)(2,1)S(1)}, u32[]{:S(2)}, u32[]{:S(2)}) %collective-permute-start.14) | collective-permute-done | bytes 32800 | tf_op jit(solution)/shard_map/ppermute | solution.py:26
  33.2 0.8 %downward.1 = (f32[3,64,256]{2,1,0:T(8,128)S(1)}, bf16[64,384]{1,0:T(8,128)(2,1)S(1)}, bf16[64,384]{1,0:T(8,128)(2,1)S(1)}, bf16[3,64,256]{2,1,0:T(8,128)(2,1)S(1)}) custom-call(f32[3,64,256]{2,1,0:T(8,128)S(1)} %get-tuple-element.103.kept, f32[3,64,256]{2,1,0:T(8,128)S(1)} %get-tuple-element.98.right, bf16[3,256,256]{2,1,0:T(8,128)(2,1)S(1)} %get-tuple-element.108.q_high, ...), custom_call_target="tpu_custom_call" | custom-call | flops 5000000000 | tf_op jit(solution)/shard_map/downward/pallas_call | solution.py:39
  34.8 1.9 %collective-permute-start.18 = (bf16[64,384]{1,0:T(8,128)(2,1)S(1)}, bf16[64,384]{1,0:T(8,128)(2,1)S(1)}, u32[]{:S(2)}, u32[]{:S(2)}) collective-permute-start(bf16[64,384]{1,0:T(8,128)(2,1)S(1)} %get-tuple-element.114), channel_id=1, source_target_pairs={{0,6},{1,7},{2,4},{3,5},{4,2},{5,3},{6,0},{7,1},{8,14},{9,15},{10,... | collective-permute-start | bytes 147464 | tf_op jit(solution)/shard_map/ppermute | solution.py:26
  36.8 0.9 %collective-permute-start.17 = (bf16[64,384]{1,0:T(8,128)(2,1)S(1)}, bf16[64,384]{1,0:T(8,128)(2,1)S(1)}, u32[]{:S(2)}, u32[]{:S(2)}) collective-permute-start(bf16[64,384]{1,0:T(8,128)(2,1)S(1)} %get-tuple-element.114), channel_id=1, source_target_pairs={{0,4},{1,5},{2,6},{3,7},{4,0},{5,1},{6,2},{7,3},{8,12},{9,13},{10,... | collective-permute-start | bytes 147464 | tf_op jit(solution)/shard_map/ppermute | solution.py:26
  37.7 0.7 %collective-permute-start.16 = (bf16[64,384]{1,0:T(8,128)(2,1)S(1)}, bf16[64,384]{1,0:T(8,128)(2,1)S(1)}, u32[]{:S(2)}, u32[]{:S(2)}) collective-permute-start(bf16[64,384]{1,0:T(8,128)(2,1)S(1)} %get-tuple-element.124.refs_0_), channel_id=1, source_target_pairs={{0,2},{1,3},{2,0},{3,1},{4,6},{5,7},{6,4},{7,5},{8,10},{9,11},{10,... | collective-permute-start | bytes 147464 | tf_op jit(solution)/shard_map/ppermute | solution.py:26
  38.4 1.3 %collective-permute-start.20 = (bf16[3,64,256]{2,1,0:T(8,128)(2,1)S(1)}, bf16[3,64,256]{2,1,0:T(8,128)(2,1)S(1)}, u32[]{:S(2)}, u32[]{:S(2)}) collective-permute-start(bf16[3,64,256]{2,1,0:T(8,128)(2,1)S(1)} %get-tuple-element.122), channel_id=1, source_target_pairs={{0,4},{1,5},{2,6},{3,7},{4,0},{5,1},{6,2},{7,3},{8,12},{9,13},{10,... | collective-permute-start | bytes 294920 | tf_op jit(solution)/shard_map/ppermute | solution.py:26
  39.7 0.9 %upper_transposed.1.base = f32[512,512]{1,0:T(8,128)S(1)} custom-call(bf16[2048,512]{1,0:T(8,128)(2,1)S(1)} %bitcast.16, f32[512,512]{1,0:T(8,128)S(1)} %get-tuple-element.115.lower, bf16[2,256,512]{2,1,0:T(8,128)(2,1)S(1)} %convert_element_type.9.refs_0_, bf16[2,256,512]{2,1,0:T(8,128)(2,1)S(1)} %collective-permute-done.19.refs_1_), custom_call_target="tpu_custom_call" | custom-call | flops 5000000000 | tf_op jit(solution)/shard_map/upper_transposed/pallas_call | solution.py:39
  40.6 0.5 %collective-permute-done.17.refs_2_ = bf16[64,384]{1,0:T(8,128)(2,1)S(1)} collective-permute-done((bf16[64,384]{1,0:T(8,128)(2,1)S(1)}, bf16[64,384]{1,0:T(8,128)(2,1)S(1)}, u32[]{:S(2)}, u32[]{:S(2)}) %collective-permute-start.17) | collective-permute-done | bytes 49184 | tf_op jit(solution)/shard_map/ppermute | solution.py:26
  41.1 0.6 %collective-permute-done.16.refs_1_ = bf16[64,384]{1,0:T(8,128)(2,1)S(1)} collective-permute-done((bf16[64,384]{1,0:T(8,128)(2,1)S(1)}, bf16[64,384]{1,0:T(8,128)(2,1)S(1)}, u32[]{:S(2)}, u32[]{:S(2)}) %collective-permute-start.16) | collective-permute-done | bytes 49184 | tf_op jit(solution)/shard_map/ppermute | solution.py:26
  43.0 0.9 %assemble.1 = f32[3,256,128]{2,1,0:T(8,128)} custom-call(f32[3,64,256]{2,1,0:T(8,128)S(1)} %get-tuple-element.128.mine, bf16[3,64,256]{2,1,0:T(8,128)(2,1)S(1)} %collective-permute-done.20.passed), custom_call_target="tpu_custom_call" | custom-call | flops 5000000000 | tf_op jit(solution)/shard_map/assemble/pallas_call | solution.py:39
  43.9 1.3 %finish.1 = bf16[512,512]{1,0:T(8,128)(2,1)} custom-call(f32[512,512]{1,0:T(8,128)S(1)} %upper_transposed.1.base, bf16[512,384]{1,0:T(8,128)(2,1)S(1)} %get-tuple-element.123.weight_turned, bf16[64,384]{1,0:T(8,128)(2,1)S(1)} %get-tuple-element.124.refs_0_, bf16[64,384]{1,0:T(8,128)(2,1)S(1)} %collective-permute-done.16.refs_1_, ...), custom_call_target="tpu_custom_call" | custom-call | flops 5000000000 | tf_op jit(solution)/shard_map/finish/pallas_call | solution.py:39
  (53 shorter events, 3.6 us)
Async XLA Ops:
  0.6 14.6 %collective-permute-start.1 = (bf16[384,512]{1,0:T(8,128)(2,1)}, bf16[384,512]{1,0:T(8,128)(2,1)S(1)}, u32[]{:S(2)}, u32[]{:S(2)}) collective-permute-start(bf16[384,512]{1,0:T(8,128)(2,1)} %bitcast.22), channel_id=1, source_target_pairs={{0,1},{1,0},{2,3},{3,2},{4,5},{5,4},{6,7},{7,6},{8,9},{9,8},{10,11... | collective-permute-start | bytes 1179656 | tf_op jit(solution)/shard_map/ppermute | solution.py:26
  1.1 12.5 %collective-permute-start = (bf16[384,512]{1,0:T(8,128)(2,1)}, bf16[384,512]{1,0:T(8,128)(2,1)S(1)}, u32[]{:S(2)}, u32[]{:S(2)}) collective-permute-start(bf16[384,512]{1,0:T(8,128)(2,1)} %bitcast.23), channel_id=1, source_target_pairs={{0,2},{1,3},{2,0},{3,1},{4,6},{5,7},{6,4},{7,5},{8,10},{9,11},{10,... | collective-permute-start | bytes 1179656 | tf_op jit(solution)/shard_map/ppermute | solution.py:26
  3.7 1.6 %copy-start = (bf16[1,2048,512]{2,1,0:T(8,128)(2,1)S(1)}, bf16[1,2048,512]{2,1,0:T(8,128)(2,1)}, u32[]{:S(2)}) copy-start(bf16[1,2048,512]{2,1,0:T(8,128)(2,1)} %param.13) | copy-start | bytes 6291460
  6.4 1.3 %copy-start.8 = (s32[1,3]{1,0:T(1,128)S(1)}, s32[1,3]{1,0:T(1,128)}, u32[]{:S(2)}) copy-start(s32[1,3]{1,0:T(1,128)} %param.16) | copy-start | bytes 40
  6.4 8.8 %copy-start.6 = (bf16[1,3,128,512]{3,2,1,0:T(8,128)(2,1)S(1)}, bf16[1,3,128,512]{3,2,1,0:T(8,128)(2,1)}, u32[]{:S(2)}) copy-start(bf16[1,3,128,512]{3,2,1,0:T(8,128)(2,1)} %param.14) | copy-start | bytes 1179652
  7.7 3.6 %collective-permute-start.11 = (s32[2,3]{1,0:T(2,128)S(1)}, s32[2,3]{1,0:T(2,128)S(1)}, u32[]{:S(2)}, u32[]{:S(2)}) collective-permute-start(s32[2,3]{1,0:T(2,128)S(1)} %pad_add_fusion.1), channel_id=1, source_target_pairs={{0,4},{1,5},{2,6},{3,7},{4,0},{5,1},{6,2},{7,3},{8,12},{9,13},{10,... | collective-permute-start | bytes 80 | tf_op jit(solution)/shard_map/ppermute | solution.py:26
  9.3 4.4 %collective-permute-start.2 = (bf16[256,512]{1,0:T(8,128)(2,1)S(1)}, bf16[256,512]{1,0:T(8,128)(2,1)S(1)}, u32[]{:S(2)}, u32[]{:S(2)}) collective-permute-start(bf16[256,512]{1,0:T(8,128)(2,1)S(1)} %get-tuple-element.81), channel_id=1, source_target_pairs={{0,1},{1,0},{2,3},{3,2},{4,5},{5,4},{6,7},{7,6},{8,9},{9,8},{10,11... | collective-permute-start | bytes 786440 | tf_op jit(solution)/shard_map/ppermute | solution.py:26
  9.3 5.0 %collective-permute-start.3 = (bf16[256,512]{1,0:T(8,128)(2,1)S(1)}, bf16[256,512]{1,0:T(8,128)(2,1)S(1)}, u32[]{:S(2)}, u32[]{:S(2)}) collective-permute-start(bf16[256,512]{1,0:T(8,128)(2,1)S(1)} %get-tuple-element.82), channel_id=1, source_target_pairs={{0,1},{1,0},{2,3},{3,2},{4,5},{5,4},{6,7},{7,6},{8,9},{9,8},{10,11... | collective-permute-start | bytes 786440 | tf_op jit(solution)/shard_map/ppermute | solution.py:26
  11.4 2.9 %collective-permute-start.4 = (bf16[256,512]{1,0:T(8,128)(2,1)S(1)}, bf16[256,512]{1,0:T(8,128)(2,1)S(1)}, u32[]{:S(2)}, u32[]{:S(2)}) collective-permute-start(bf16[256,512]{1,0:T(8,128)(2,1)S(1)} %get-tuple-element.83), channel_id=1, source_target_pairs={{0,1},{1,0},{2,3},{3,2},{4,5},{5,4},{6,7},{7,6},{8,9},{9,8},{10,11... | collective-permute-start | bytes 786440 | tf_op jit(solution)/shard_map/ppermute | solution.py:26
  13.7 1.5 %collective-permute-start.5 = (bf16[256,512]{1,0:T(8,128)(2,1)S(1)}, bf16[256,512]{1,0:T(8,128)(2,1)S(1)}, u32[]{:S(2)}, u32[]{:S(2)}) collective-permute-start(bf16[256,512]{1,0:T(8,128)(2,1)S(1)} %get-tuple-element.84), channel_id=1, source_target_pairs={{0,1},{1,0},{2,3},{3,2},{4,5},{5,4},{6,7},{7,6},{8,9},{9,8},{10,11... | collective-permute-start | bytes 786440 | tf_op jit(solution)/shard_map/ppermute | solution.py:26
  13.7 2.3 %collective-permute-start.6 = (bf16[384,512]{1,0:T(8,128)(2,1)S(1)}, bf16[384,512]{1,0:T(8,128)(2,1)S(1)}, u32[]{:S(2)}, u32[]{:S(2)}) collective-permute-start(bf16[384,512]{1,0:T(8,128)(2,1)S(1)} %collective-permute-done.refs_0_.refs_2_), channel_id=1, source_target_pairs={{0,1},{1,0},{2,3},{3,2},{4,5},{5,4},{6,7},{7,6},{8,9},{9,8},{10,11... | collective-permute-start | bytes 1179656 | tf_op jit(solution)/shard_map/ppermute | solution.py:26
  15.8 13.4 %collective-permute-start.12 = (bf16[2,256,512]{2,1,0:T(8,128)(2,1)S(1)}, bf16[2,256,512]{2,1,0:T(8,128)(2,1)S(1)}, u32[]{:S(2)}, u32[]{:S(2)}) collective-permute-start(bf16[2,256,512]{2,1,0:T(8,128)(2,1)S(1)} %get-tuple-element.86.low.refs_4_), channel_id=1, source_target_pairs={{0,1},{1,0},{2,3},{3,2},{4,5},{5,4},{6,7},{7,6},{8,9},{9,8},{10,11... | collective-permute-start | bytes 1572872 | tf_op jit(solution)/shard_map/ppermute | solution.py:26
  16.0 5.9 %copy-start.2 = (f32[1,3,256,512]{3,2,1,0:T(8,128)S(1)}, f32[1,3,256,512]{3,2,1,0:T(8,128)}, u32[]{:S(2)}) copy-start(f32[1,3,256,512]{3,2,1,0:T(8,128)} %param.19) | copy-start | bytes 4718596
  16.0 5.9 %copy-start.3 = (f32[1,3,256,256]{3,2,1,0:T(8,128)S(1)}, f32[1,3,256,256]{3,2,1,0:T(8,128)}, u32[]{:S(2)}) copy-start(f32[1,3,256,256]{3,2,1,0:T(8,128)} %param.17) | copy-start | bytes 2359300
  16.0 5.9 %copy-start.5 = (f32[1,2,256,256]{3,2,1,0:T(8,128)S(1)}, f32[1,2,256,256]{3,2,1,0:T(8,128)}, u32[]{:S(2)}) copy-start(f32[1,2,256,256]{3,2,1,0:T(8,128)} %param.18) | copy-start | bytes 1572868
  16.5 6.7 %collective-permute-start.8 = (bf16[64,384]{1,0:T(8,128)(2,1)S(1)}, bf16[64,384]{1,0:T(8,128)(2,1)S(1)}, u32[]{:S(2)}, u32[]{:S(2)}) collective-permute-start(bf16[64,384]{1,0:T(8,128)(2,1)S(1)} %get-tuple-element.92), channel_id=1, source_target_pairs={{0,6},{1,7},{2,4},{3,5},{4,2},{5,3},{6,0},{7,1},{8,14},{9,15},{10,... | collective-permute-start | bytes 147464 | tf_op jit(solution)/shard_map/ppermute | solution.py:26
  19.3 4.6 %collective-permute-start.9 = (bf16[64,384]{1,0:T(8,128)(2,1)S(1)}, bf16[64,384]{1,0:T(8,128)(2,1)S(1)}, u32[]{:S(2)}, u32[]{:S(2)}) collective-permute-start(bf16[64,384]{1,0:T(8,128)(2,1)S(1)} %get-tuple-element.93), channel_id=1, source_target_pairs={{0,2},{1,3},{2,0},{3,1},{4,6},{5,7},{6,4},{7,5},{8,10},{9,11},{10,... | collective-permute-start | bytes 147464 | tf_op jit(solution)/shard_map/ppermute | solution.py:26
  19.8 4.1 %collective-permute-start.10 = (bf16[64,384]{1,0:T(8,128)(2,1)S(1)}, bf16[64,384]{1,0:T(8,128)(2,1)S(1)}, u32[]{:S(2)}, u32[]{:S(2)}) collective-permute-start(bf16[64,384]{1,0:T(8,128)(2,1)S(1)} %get-tuple-element.94), channel_id=1, source_target_pairs={{0,4},{1,5},{2,6},{3,7},{4,0},{5,1},{6,2},{7,3},{8,12},{9,13},{10,... | collective-permute-start | bytes 147464 | tf_op jit(solution)/shard_map/ppermute | solution.py:26
  20.0 14.2 %collective-permute-start.7 = (bf16[2,256,512]{2,1,0:T(8,128)(2,1)S(1)}, bf16[2,256,512]{2,1,0:T(8,128)(2,1)S(1)}, u32[]{:S(2)}, u32[]{:S(2)}) collective-permute-start(bf16[2,256,512]{2,1,0:T(8,128)(2,1)S(1)} %get-tuple-element.90.high), channel_id=1, source_target_pairs={{0,2},{1,3},{2,0},{3,1},{4,6},{5,7},{6,4},{7,5},{8,10},{9,11},{10,... | collective-permute-start | bytes 1572872 | tf_op jit(solution)/shard_map/ppermute | solution.py:26
  23.9 5.3 %copy-start.1 = (bf16[1,2048,512]{2,1,0:T(8,128)(2,1)S(1)}, bf16[1,2048,512]{2,1,0:T(8,128)(2,1)}, u32[]{:S(2)}) copy-start(bf16[1,2048,512]{2,1,0:T(8,128)(2,1)} %param.13) | copy-start | bytes 6291460
  24.7 6.9 %collective-permute-start.15 = (bf16[1,64,256]{2,1,0:T(8,128)(2,1)S(1)}, bf16[1,64,256]{2,1,0:T(8,128)(2,1)S(1)}, u32[]{:S(2)}, u32[]{:S(2)}) collective-permute-start(bf16[1,64,256]{2,1,0:T(8,128)(2,1)S(1)} %get-tuple-element.111), channel_id=1, source_target_pairs={{0,24},{1,25},{2,26},{3,27},{4,28},{5,29},{6,30},{7,31},{8,16},{9,... | collective-permute-start | bytes 98312 | tf_op jit(solution)/shard_map/ppermute | solution.py:26
  28.3 4.8 %collective-permute-start.14 = (bf16[1,64,256]{2,1,0:T(8,128)(2,1)S(1)}, bf16[1,64,256]{2,1,0:T(8,128)(2,1)S(1)}, u32[]{:S(2)}, u32[]{:S(2)}) collective-permute-start(bf16[1,64,256]{2,1,0:T(8,128)(2,1)S(1)} %get-tuple-element.111), channel_id=1, source_target_pairs={{0,16},{1,17},{2,18},{3,19},{4,20},{5,21},{6,22},{7,23},{8,24},{9,... | collective-permute-start | bytes 98312 | tf_op jit(solution)/shard_map/ppermute | solution.py:26
  28.3 4.8 %collective-permute-start.13 = (bf16[2,64,256]{2,1,0:T(8,128)(2,1)S(1)}, bf16[2,64,256]{2,1,0:T(8,128)(2,1)S(1)}, u32[]{:S(2)}, u32[]{:S(2)}) collective-permute-start(bf16[2,64,256]{2,1,0:T(8,128)(2,1)S(1)} %get-tuple-element.110), channel_id=1, source_target_pairs={{0,8},{1,9},{2,10},{3,11},{4,12},{5,13},{6,14},{7,15},{8,0},{9,1},... | collective-permute-start | bytes 196616 | tf_op jit(solution)/shard_map/ppermute | solution.py:26
  34.7 3.6 %collective-permute-start.19 = (bf16[2,256,512]{2,1,0:T(8,128)(2,1)S(1)}, bf16[2,256,512]{2,1,0:T(8,128)(2,1)S(1)}, u32[]{:S(2)}, u32[]{:S(2)}) collective-permute-start(bf16[2,256,512]{2,1,0:T(8,128)(2,1)S(1)} %convert_element_type.9.refs_0_), channel_id=1, source_target_pairs={{0,1},{1,0},{2,3},{3,2},{4,5},{5,4},{6,7},{7,6},{8,9},{9,8},{10,11... | collective-permute-start | bytes 1572872 | tf_op jit(solution)/shard_map/ppermute | solution.py:26
  34.8 5.7 %collective-permute-start.18 = (bf16[64,384]{1,0:T(8,128)(2,1)S(1)}, bf16[64,384]{1,0:T(8,128)(2,1)S(1)}, u32[]{:S(2)}, u32[]{:S(2)}) collective-permute-start(bf16[64,384]{1,0:T(8,128)(2,1)S(1)} %get-tuple-element.114), channel_id=1, source_target_pairs={{0,6},{1,7},{2,4},{3,5},{4,2},{5,3},{6,0},{7,1},{8,14},{9,15},{10,... | collective-permute-start | bytes 147464 | tf_op jit(solution)/shard_map/ppermute | solution.py:26
  36.8 4.4 %collective-permute-start.17 = (bf16[64,384]{1,0:T(8,128)(2,1)S(1)}, bf16[64,384]{1,0:T(8,128)(2,1)S(1)}, u32[]{:S(2)}, u32[]{:S(2)}) collective-permute-start(bf16[64,384]{1,0:T(8,128)(2,1)S(1)} %get-tuple-element.114), channel_id=1, source_target_pairs={{0,4},{1,5},{2,6},{3,7},{4,0},{5,1},{6,2},{7,3},{8,12},{9,13},{10,... | collective-permute-start | bytes 147464 | tf_op jit(solution)/shard_map/ppermute | solution.py:26
  37.7 4.1 %collective-permute-start.16 = (bf16[64,384]{1,0:T(8,128)(2,1)S(1)}, bf16[64,384]{1,0:T(8,128)(2,1)S(1)}, u32[]{:S(2)}, u32[]{:S(2)}) collective-permute-start(bf16[64,384]{1,0:T(8,128)(2,1)S(1)} %get-tuple-element.124.refs_0_), channel_id=1, source_target_pairs={{0,2},{1,3},{2,0},{3,1},{4,6},{5,7},{6,4},{7,5},{8,10},{9,11},{10,... | collective-permute-start | bytes 147464 | tf_op jit(solution)/shard_map/ppermute | solution.py:26
  38.4 4.6 %collective-permute-start.20 = (bf16[3,64,256]{2,1,0:T(8,128)(2,1)S(1)}, bf16[3,64,256]{2,1,0:T(8,128)(2,1)S(1)}, u32[]{:S(2)}, u32[]{:S(2)}) collective-permute-start(bf16[3,64,256]{2,1,0:T(8,128)(2,1)S(1)} %get-tuple-element.122), channel_id=1, source_target_pairs={{0,4},{1,5},{2,6},{3,7},{4,0},{5,1},{6,2},{7,3},{8,12},{9,13},{10,... | collective-permute-start | bytes 294920 | tf_op jit(solution)/shard_map/ppermute | solution.py:26
  41.7 2.1 %collective-permute-start.21 = (bf16[64,384]{1,0:T(8,128)(2,1)S(1)}, bf16[64,384]{1,0:T(8,128)(2,1)S(1)}, u32[]{:S(2)}, u32[]{:S(2)}) collective-permute-start(bf16[64,384]{1,0:T(8,128)(2,1)S(1)} %get-tuple-element.124.refs_0_), channel_id=1, source_target_pairs={{0,1},{1,0},{2,3},{3,2},{4,5},{5,4},{6,7},{7,6},{8,9},{9,8},{10,11... | collective-permute-start | bytes 147464 | tf_op jit(solution)/shard_map/ppermute | solution.py:26
  41.7 2.1 %collective-permute-start.22 = (bf16[64,384]{1,0:T(8,128)(2,1)S(1)}, bf16[64,384]{1,0:T(8,128)(2,1)S(1)}, u32[]{:S(2)}, u32[]{:S(2)}) collective-permute-start(bf16[64,384]{1,0:T(8,128)(2,1)S(1)} %collective-permute-done.16.refs_1_), channel_id=1, source_target_pairs={{0,1},{1,0},{2,3},{3,2},{4,5},{5,4},{6,7},{7,6},{8,9},{9,8},{10,11... | collective-permute-start | bytes 147464 | tf_op jit(solution)/shard_map/ppermute | solution.py:26
  42.3 1.6 %collective-permute-start.23 = (bf16[64,384]{1,0:T(8,128)(2,1)S(1)}, bf16[64,384]{1,0:T(8,128)(2,1)S(1)}, u32[]{:S(2)}, u32[]{:S(2)}) collective-permute-start(bf16[64,384]{1,0:T(8,128)(2,1)S(1)} %collective-permute-done.17.refs_2_), channel_id=1, source_target_pairs={{0,1},{1,0},{2,3},{3,2},{4,5},{5,4},{6,7},{7,6},{8,9},{9,8},{10,11... | collective-permute-start | bytes 147464 | tf_op jit(solution)/shard_map/ppermute | solution.py:26
  42.3 1.7 %collective-permute-start.24 = (bf16[64,384]{1,0:T(8,128)(2,1)S(1)}, bf16[64,384]{1,0:T(8,128)(2,1)S(1)}, u32[]{:S(2)}, u32[]{:S(2)}) collective-permute-start(bf16[64,384]{1,0:T(8,128)(2,1)S(1)} %collective-permute-done.18.refs_3_), channel_id=1, source_target_pairs={{0,1},{1,0},{2,3},{3,2},{4,5},{5,4},{6,7},{7,6},{8,9},{9,8},{10,11... | collective-permute-start | bytes 147464 | tf_op jit(solution)/shard_map/ppermute | solution.py:26
  (2 other events, 2.4 us)

commit v5 on v4

--- a/solution.py
+++ b/solution.py
@@ -128,8 +128,8 @@
 
 
 def own_partials(masks, keep, *refs):
-    panels, received = refs[: len(masks)], refs[len(masks) : -3]
-    low, high, out = refs[-3:]
+    panels, received = refs[: len(masks)], refs[len(masks) : -4]
+    low, high, kept, out = refs[-4:]
     column, _, top = position()
     half = low.shape[0]
     for block in range(2 * half):
@@ -140,6 +140,7 @@
             low[block] = value.astype(BF16)
         else:
             high[block - half] = value.astype(BF16)
+            kept[block - half] = value
     out[...] = panel_products(top, column, masks, panels, low, high)
 
 
@@ -314,7 +315,6 @@
         [inverse, rhs],
         [pltpu.VMEM((sources, rows), BF16)],
     )
-    keep, offsets, pattern = lax.optimization_barrier((keep, offsets, pattern))
     spots = jnp.concatenate([offsets, pattern], axis=0)
     spots = jnp.concatenate([spots, moved(spots, 1, 0)], axis=0)
     received = [moved(block, 0, n // groups + 1) for n, block in enumerate(sends)]
@@ -322,9 +322,9 @@
     near, far = list(range(half)), list(range(half, groups))
     partial_shape = (sources // half, levels * touched)
     keep, held[half] = lax.optimization_barrier((keep, held[half]))
-    low, high, early = call(
+    low, high, upper, early = call(
         functools.partial(own_partials, near),
-        [shape(upper_rows, BF16)] * 2 + [shape(partial_shape)],
+        [shape(upper_rows, BF16)] * 2 + [shape(upper_rows), shape(partial_shape)],
         [],
         [keep] + [held[mask] for mask in near] + received,
     )
@@ -338,7 +338,7 @@
         [low, high, early] + [held[mask] for mask in far],
         [pltpu.VMEM(partial_shape, F32)],
     )
-    high, own, inverses = lax.optimization_barrier((high, own, sep_inverse[0]))
+    high, low, own, inverses = lax.optimization_barrier((high, low, own, sep_inverse[0]))
     cross = moved(cross, 1, half)
     same, other = moved(same, 0, half), moved(other, 1, 0)
 
@@ -385,11 +385,7 @@
     )
 
     high, mine = lax.optimization_barrier((high, mine))
-    solved = keep[half:] + high.astype(F32)
-    for n, block in enumerate(received):
-        if n % groups >= half:
-            solved = solved.at[n % groups - half].add(block.astype(F32))
-    solved = solved.astype(BF16)
+    solved = (upper + high.astype(F32)).astype(BF16)
     solved = [solved] + [moved(solved, 0, j) for j in range(1, half)]
     *solved, passed = lax.optimization_barrier((*solved, passed))
     base = call(

time: 45.4 us -> 44.8 us (0.987)
  waiting for transfers between devices: 8.72 us -> 7.95 us
    ppermute x25, waiting for transfers between devices: 8.72 us -> 7.95 us  [moved(): return lax.ppermute(block, AXES, route)]
    concatenate x1, other arithmetic: 0.01 us -> 0.68 us  [on_device(): spots = jnp.concatenate([offsets, pattern], axis=0)]
  transfers between devices with their start and end apart: 25 -> 25, of which waited for: 9 -> 6; matrix products, arithmetic and copies ran while one was open for 0% -> 2% of each run, Pallas kernels for 21% -> 20%
where the time goes in v5:
time: 44.8 us; the launch traced here: 44.6 us
  starting transfers between devices  21.4 us (48%)
  Pallas kernels  10.9 us (24%)
  waiting for transfers between devices  7.95 us (18%)
  local copies, waits for them, and re-layouts  2.67 us (6%)
  between operations  0.86 us (2%)
  other arithmetic  0.85 us (2%)
    ppermute x25, starting transfers between devices, moved(): return lax.ppermute(block, AXES, route)  21.4 us
    pallas_call x11, Pallas kernels, call(): pl.pallas_call(body, out_shape=outs, in_specs=specs, out_specs=[pl.BlockS...  10.9 us
    ppermute x25, waiting for transfers between devices, moved(): return lax.ppermute(block, AXES, route)  7.95 us
    unnamed x18, local copies, waits for them, and re-layouts  2.67 us
  transfers between devices with their start and end apart: 25, of which 6 were waited for; matrix products, arithmetic and copies ran while one was open for 2% of the time, Pallas kernels for 20%

profile of v5, /device:TPU:0, one launch (start us, length us, event | category | flops | bytes accessed | tf_op | source)
XLA Modules:
  0.0 44.6 jit_solution(11349155285588939563)
XLA Ops:
  0.6 0.5 %collective-permute-start.1 = (bf16[384,512]{1,0:T(8,128)(2,1)}, bf16[384,512]{1,0:T(8,128)(2,1)S(1)}, u32[]{:S(2)}, u32[]{:S(2)}) collective-permute-start(bf16[384,512]{1,0:T(8,128)(2,1)} %bitcast.16), channel_id=1, source_target_pairs={{0,1},{1,0},{2,3},{3,2},{4,5},{5,4},{6,7},{7,6},{8,9},{9,8},{10,11... | collective-permute-start | bytes 1179656 | tf_op jit(solution)/shard_map/ppermute | solution.py:26
  1.1 2.6 %collective-permute-start = (bf16[384,512]{1,0:T(8,128)(2,1)}, bf16[384,512]{1,0:T(8,128)(2,1)S(1)}, u32[]{:S(2)}, u32[]{:S(2)}) collective-permute-start(bf16[384,512]{1,0:T(8,128)(2,1)} %bitcast.17), channel_id=1, source_target_pairs={{0,2},{1,3},{2,0},{3,1},{4,6},{5,7},{6,4},{7,5},{8,10},{9,11},{10,... | collective-permute-start | bytes 1179656 | tf_op jit(solution)/shard_map/ppermute | solution.py:26
  3.7 0.7 %pad_add_fusion.1 = s32[2,3]{1,0:T(2,128)S(1)} fusion(s32[1,3]{1,0:T(1,128)} %param.11, s32[1,3]{1,0:T(1,128)} %param.12), kind=kLoop, calls=%fused_computation.2 | loop fusion | flops 6 | bytes 48 | tf_op jit(solution)/shard_map/concatenate | solution.py:318
  4.4 1.5 %collective-permute-start.11 = (s32[2,3]{1,0:T(2,128)S(1)}, s32[2,3]{1,0:T(2,128)S(1)}, u32[]{:S(2)}, u32[]{:S(2)}) collective-permute-start(s32[2,3]{1,0:T(2,128)S(1)} %pad_add_fusion.1), channel_id=1, source_target_pairs={{0,4},{1,5},{2,6},{3,7},{4,0},{5,1},{6,2},{7,3},{8,12},{9,13},{10,... | collective-permute-start | bytes 80 | tf_op jit(solution)/shard_map/ppermute | solution.py:26
  5.9 1.6 %copy-done = bf16[1,2048,512]{2,1,0:T(8,128)(2,1)S(1)} copy-done((bf16[1,2048,512]{2,1,0:T(8,128)(2,1)S(1)}, bf16[1,2048,512]{2,1,0:T(8,128)(2,1)}, u32[]{:S(2)}) %copy-start) | copy-done | bytes 2097176
  7.5 1.0 %copy-done.4 = bf16[1,512,512]{2,1,0:T(8,128)(2,1)S(1)} copy-done((bf16[1,512,512]{2,1,0:T(8,128)(2,1)S(1)}, bf16[1,512,512]{2,1,0:T(8,128)(2,1)}, u32[]{:S(2)}) %copy-start.4) | copy-done | bytes 524312
  8.6 1.3 %leaf_products.1 = (f32[4,256,512]{2,1,0:T(8,128)S(1)}, bf16[256,512]{1,0:T(8,128)(2,1)S(1)}, bf16[256,512]{1,0:T(8,128)(2,1)S(1)}, bf16[256,512]{1,0:T(8,128)(2,1)S(1)}, bf16[256,512]{1,0:T(8,128)(2,1)S(1)}) custom-call(bf16[2048,512]{1,0:T(8,128)(2,1)S(1)} %bitcast.8, bf16[512,512]{1,0:T(8,128)(2,1)S(1)} %bitcast.14), custom_call_target="tpu_custom_call" | custom-call | flops 5000000000 | tf_op jit(solution)/shard_map/leaf_products/pallas_call | solution.py:39
  10.5 3.1 %collective-permute-done.refs_0_.refs_2_ = bf16[384,512]{1,0:T(8,128)(2,1)S(1)} collective-permute-done((bf16[384,512]{1,0:T(8,128)(2,1)}, bf16[384,512]{1,0:T(8,128)(2,1)S(1)}, u32[]{:S(2)}, u32[]{:S(2)}) %collective-permute-start) | collective-permute-done | bytes 393248 | tf_op jit(solution)/shard_map/ppermute | solution.py:26
  13.7 0.6 %collective-permute-start.6 = (bf16[384,512]{1,0:T(8,128)(2,1)S(1)}, bf16[384,512]{1,0:T(8,128)(2,1)S(1)}, u32[]{:S(2)}, u32[]{:S(2)}) collective-permute-start(bf16[384,512]{1,0:T(8,128)(2,1)S(1)} %collective-permute-done.refs_0_.refs_2_), channel_id=1, source_target_pairs={{0,1},{1,0},{2,3},{3,2},{4,5},{5,4},{6,7},{7,6},{8,9},{9,8},{10,11... | collective-permute-start | bytes 1179656 | tf_op jit(solution)/shard_map/ppermute | solution.py:26
  14.3 0.9 %collective-permute-done.5.refs_5_ = bf16[256,512]{1,0:T(8,128)(2,1)S(1)} collective-permute-done((bf16[256,512]{1,0:T(8,128)(2,1)S(1)}, bf16[256,512]{1,0:T(8,128)(2,1)S(1)}, u32[]{:S(2)}, u32[]{:S(2)}) %collective-permute-start.5) | collective-permute-done | bytes 262176 | tf_op jit(solution)/shard_map/ppermute | solution.py:26
  15.2 0.6 %own_partials.1 = (bf16[2,256,512]{2,1,0:T(8,128)(2,1)S(1)}, bf16[2,256,512]{2,1,0:T(8,128)(2,1)S(1)}, f32[2,256,512]{2,1,0:T(8,128)S(1)}, f32[256,384]{1,0:T(8,128)S(1)}) custom-call(f32[4,256,512]{2,1,0:T(8,128)S(1)} %get-tuple-element.54.keep, bf16[384,512]{1,0:T(8,128)(2,1)S(1)} %bitcast.18, bf16[384,512]{1,0:T(8,128)(2,1)S(1)} %collective-permute-done.1.refs_1_, ...), custom_call_target="tpu_custom_call" | custom-call | flops 5000000000 | tf_op jit(solution)/shard_map/own_partials/pallas_call | solution.py:39
  16.3 2.8 %collective-permute-start.8 = (bf16[64,384]{1,0:T(8,128)(2,1)S(1)}, bf16[64,384]{1,0:T(8,128)(2,1)S(1)}, u32[]{:S(2)}, u32[]{:S(2)}) collective-permute-start(bf16[64,384]{1,0:T(8,128)(2,1)S(1)} %get-tuple-element.66), channel_id=1, source_target_pairs={{0,6},{1,7},{2,4},{3,5},{4,2},{5,3},{6,0},{7,1},{8,14},{9,15},{10,... | collective-permute-start | bytes 147464 | tf_op jit(solution)/shard_map/ppermute | solution.py:26
  19.1 0.5 %collective-permute-start.9 = (bf16[64,384]{1,0:T(8,128)(2,1)S(1)}, bf16[64,384]{1,0:T(8,128)(2,1)S(1)}, u32[]{:S(2)}, u32[]{:S(2)}) collective-permute-start(bf16[64,384]{1,0:T(8,128)(2,1)S(1)} %get-tuple-element.67), channel_id=1, source_target_pairs={{0,2},{1,3},{2,0},{3,1},{4,6},{5,7},{6,4},{7,5},{8,10},{9,11},{10,... | collective-permute-start | bytes 147464 | tf_op jit(solution)/shard_map/ppermute | solution.py:26
  19.9 1.8 %collective-permute-start.7 = (bf16[2,256,512]{2,1,0:T(8,128)(2,1)S(1)}, bf16[2,256,512]{2,1,0:T(8,128)(2,1)S(1)}, u32[]{:S(2)}, u32[]{:S(2)}) collective-permute-start(bf16[2,256,512]{2,1,0:T(8,128)(2,1)S(1)} %get-tuple-element.64.high), channel_id=1, source_target_pairs={{0,2},{1,3},{2,0},{3,1},{4,6},{5,7},{6,4},{7,5},{8,10},{9,11},{10,... | collective-permute-start | bytes 1572872 | tf_op jit(solution)/shard_map/ppermute | solution.py:26
  21.7 1.3 %prepare.1 = (bf16[2,256,256]{2,1,0:T(8,128)(2,1)S(1)}, bf16[2,256,256]{2,1,0:T(8,128)(2,1)S(1)}, f32[3,64,256]{2,1,0:T(8,128)S(1)}, bf16[3,256,256]{2,1,0:T(8,128)(2,1)S(1)}) custom-call(s32[4,3]{1,0:T(4,128)S(1)} %pad_add_fusion.spots, f32[3,256,256]{2,1,0:T(8,128)S(1)} %bitcast.12, f32[2,256,256]{2,1,0:T(8,128)S(1)} %bitcast.15, f32[3,256,512]{2,1,0:T(8,128)S(1)} %bitcast.11), custom_call_target="tpu_custom_call" | custom-call | flops 5000000000 | tf_op jit(solution)/shard_map/prepare/pallas_call | solution.py:39
  23.0 0.7 %collective-permute-done.9.same = bf16[64,384]{1,0:T(8,128)(2,1)S(1)} collective-permute-done((bf16[64,384]{1,0:T(8,128)(2,1)S(1)}, bf16[64,384]{1,0:T(8,128)(2,1)S(1)}, u32[]{:S(2)}, u32[]{:S(2)}) %collective-permute-start.9) | collective-permute-done | bytes 49184 | tf_op jit(solution)/shard_map/ppermute | solution.py:26
  23.7 0.8 %upward.1 = (f32[3,64,256]{2,1,0:T(8,128)S(1)}, bf16[2,64,256]{2,1,0:T(8,128)(2,1)S(1)}, bf16[1,64,256]{2,1,0:T(8,128)(2,1)S(1)}) custom-call(f32[64,384]{1,0:T(8,128)S(1)} %get-tuple-element.65.own, bf16[64,384]{1,0:T(8,128)(2,1)S(1)} %collective-permute-done.8.cross, bf16[64,384]{1,0:T(8,128)(2,1)S(1)} %collective-permute-done.9.same, ...), custom_call_target="tpu_custom_call" | custom-call | flops 5000000000 | tf_op jit(solution)/shard_map/upward/pallas_call | solution.py:39
  24.6 3.7 %collective-permute-start.15 = (bf16[1,64,256]{2,1,0:T(8,128)(2,1)S(1)}, bf16[1,64,256]{2,1,0:T(8,128)(2,1)S(1)}, u32[]{:S(2)}, u32[]{:S(2)}) collective-permute-start(bf16[1,64,256]{2,1,0:T(8,128)(2,1)S(1)} %get-tuple-element.84), channel_id=1, source_target_pairs={{0,24},{1,25},{2,26},{3,27},{4,28},{5,29},{6,30},{7,31},{8,16},{9,... | collective-permute-start | bytes 98312 | tf_op jit(solution)/shard_map/ppermute | solution.py:26
  28.2 0.8 %collective-permute-start.13 = (bf16[2,64,256]{2,1,0:T(8,128)(2,1)S(1)}, bf16[2,64,256]{2,1,0:T(8,128)(2,1)S(1)}, u32[]{:S(2)}, u32[]{:S(2)}) collective-permute-start(bf16[2,64,256]{2,1,0:T(8,128)(2,1)S(1)} %get-tuple-element.83), channel_id=1, source_target_pairs={{0,8},{1,9},{2,10},{3,11},{4,12},{5,13},{6,14},{7,15},{8,0},{9,1},... | collective-permute-start | bytes 196616 | tf_op jit(solution)/shard_map/ppermute | solution.py:26
  29.0 1.5 %lower_transposed.1 = (f32[512,512]{1,0:T(8,128)S(1)}, bf16[512,384]{1,0:T(8,128)(2,1)S(1)}) custom-call(bf16[2048,512]{1,0:T(8,128)(2,1)S(1)} %bitcast.9, bf16[384,512]{1,0:T(8,128)(2,1)S(1)} %bitcast.19, bf16[384,512]{1,0:T(8,128)(2,1)S(1)} %collective-permute-done.1.refs_1_, bf16[384,512]{1,0:T(8,128)(2,1)S(1)} %collective-permute-done.refs_0_.refs_2_, ...), custom_call_target="tpu_custom_call" | custom-call | flops 5000000000 | tf_op jit(solution)/shard_map/lower_transposed/pallas_call | solution.py:39
  30.5 0.9 %squares.1 = (bf16[3,256,256]{2,1,0:T(8,128)(2,1)S(1)}, bf16[3,256,256]{2,1,0:T(8,128)(2,1)S(1)}) custom-call(f32[3,256,256]{2,1,0:T(8,128)S(1)} %bitcast.13), custom_call_target="tpu_custom_call" | custom-call | flops 5000000000 | tf_op jit(solution)/shard_map/squares/pallas_call | solution.py:39
  31.4 1.6 %collective-permute-done.14.refs_1_ = bf16[1,64,256]{2,1,0:T(8,128)(2,1)S(1)} collective-permute-done((bf16[1,64,256]{2,1,0:T(8,128)(2,1)S(1)}, bf16[1,64,256]{2,1,0:T(8,128)(2,1)S(1)}, u32[]{:S(2)}, u32[]{:S(2)}) %collective-permute-start.14) | collective-permute-done | bytes 32800 | tf_op jit(solution)/shard_map/ppermute | solution.py:26
  33.0 0.8 %downward.1 = (f32[3,64,256]{2,1,0:T(8,128)S(1)}, bf16[64,384]{1,0:T(8,128)(2,1)S(1)}, bf16[64,384]{1,0:T(8,128)(2,1)S(1)}, bf16[3,64,256]{2,1,0:T(8,128)(2,1)S(1)}) custom-call(f32[3,64,256]{2,1,0:T(8,128)S(1)} %get-tuple-element.75.kept, f32[3,64,256]{2,1,0:T(8,128)S(1)} %get-tuple-element.70.right, bf16[3,256,256]{2,1,0:T(8,128)(2,1)S(1)} %get-tuple-element.81.q_high, ...), custom_call_target="tpu_custom_call" | custom-call | flops 5000000000 | tf_op jit(solution)/shard_map/downward/pallas_call | solution.py:39
  34.1 1.9 %collective-permute-start.18 = (bf16[64,384]{1,0:T(8,128)(2,1)S(1)}, bf16[64,384]{1,0:T(8,128)(2,1)S(1)}, u32[]{:S(2)}, u32[]{:S(2)}) collective-permute-start(bf16[64,384]{1,0:T(8,128)(2,1)S(1)} %get-tuple-element.87), channel_id=1, source_target_pairs={{0,6},{1,7},{2,4},{3,5},{4,2},{5,3},{6,0},{7,1},{8,14},{9,15},{10,... | collective-permute-start | bytes 147464 | tf_op jit(solution)/shard_map/ppermute | solution.py:26
  36.0 1.1 %collective-permute-start.17 = (bf16[64,384]{1,0:T(8,128)(2,1)S(1)}, bf16[64,384]{1,0:T(8,128)(2,1)S(1)}, u32[]{:S(2)}, u32[]{:S(2)}) collective-permute-start(bf16[64,384]{1,0:T(8,128)(2,1)S(1)} %get-tuple-element.87), channel_id=1, source_target_pairs={{0,4},{1,5},{2,6},{3,7},{4,0},{5,1},{6,2},{7,3},{8,12},{9,13},{10,... | collective-permute-start | bytes 147464 | tf_op jit(solution)/shard_map/ppermute | solution.py:26
  37.2 0.5 %collective-permute-start.16 = (bf16[64,384]{1,0:T(8,128)(2,1)S(1)}, bf16[64,384]{1,0:T(8,128)(2,1)S(1)}, u32[]{:S(2)}, u32[]{:S(2)}) collective-permute-start(bf16[64,384]{1,0:T(8,128)(2,1)S(1)} %get-tuple-element.98.refs_0_), channel_id=1, source_target_pairs={{0,2},{1,3},{2,0},{3,1},{4,6},{5,7},{6,4},{7,5},{8,10},{9,11},{10,... | collective-permute-start | bytes 147464 | tf_op jit(solution)/shard_map/ppermute | solution.py:26
  37.7 1.2 %collective-permute-start.20 = (bf16[3,64,256]{2,1,0:T(8,128)(2,1)S(1)}, bf16[3,64,256]{2,1,0:T(8,128)(2,1)S(1)}, u32[]{:S(2)}, u32[]{:S(2)}) collective-permute-start(bf16[3,64,256]{2,1,0:T(8,128)(2,1)S(1)} %get-tuple-element.96), channel_id=1, source_target_pairs={{0,4},{1,5},{2,6},{3,7},{4,0},{5,1},{6,2},{7,3},{8,12},{9,13},{10,... | collective-permute-start | bytes 294920 | tf_op jit(solution)/shard_map/ppermute | solution.py:26
  38.9 0.9 %upper_transposed.1.base = f32[512,512]{1,0:T(8,128)S(1)} custom-call(bf16[2048,512]{1,0:T(8,128)(2,1)S(1)} %bitcast.10, f32[512,512]{1,0:T(8,128)S(1)} %get-tuple-element.88.lower, bf16[2,256,512]{2,1,0:T(8,128)(2,1)S(1)} %add_convert_fusion.refs_0_, bf16[2,256,512]{2,1,0:T(8,128)(2,1)S(1)} %collective-permute-done.19.refs_1_), custom_call_target="tpu_custom_call" | custom-call | flops 5000000000 | tf_op jit(solution)/shard_map/upper_transposed/pallas_call | solution.py:39
  39.8 1.4 %collective-permute-done.16.refs_1_ = bf16[64,384]{1,0:T(8,128)(2,1)S(1)} collective-permute-done((bf16[64,384]{1,0:T(8,128)(2,1)S(1)}, bf16[64,384]{1,0:T(8,128)(2,1)S(1)}, u32[]{:S(2)}, u32[]{:S(2)}) %collective-permute-start.16) | collective-permute-done | bytes 49184 | tf_op jit(solution)/shard_map/ppermute | solution.py:26
  41.3 0.5 %collective-permute-start.22 = (bf16[64,384]{1,0:T(8,128)(2,1)S(1)}, bf16[64,384]{1,0:T(8,128)(2,1)S(1)}, u32[]{:S(2)}, u32[]{:S(2)}) collective-permute-start(bf16[64,384]{1,0:T(8,128)(2,1)S(1)} %collective-permute-done.16.refs_1_), channel_id=1, source_target_pairs={{0,1},{1,0},{2,3},{3,2},{4,5},{5,4},{6,7},{7,6},{8,9},{9,8},{10,11... | collective-permute-start | bytes 147464 | tf_op jit(solution)/shard_map/ppermute | solution.py:26
  42.4 0.9 %assemble.1 = f32[3,256,128]{2,1,0:T(8,128)} custom-call(f32[3,64,256]{2,1,0:T(8,128)S(1)} %get-tuple-element.102.mine, bf16[3,64,256]{2,1,0:T(8,128)(2,1)S(1)} %collective-permute-done.20.passed), custom_call_target="tpu_custom_call" | custom-call | flops 5000000000 | tf_op jit(solution)/shard_map/assemble/pallas_call | solution.py:39
  43.3 1.3 %finish.1 = bf16[512,512]{1,0:T(8,128)(2,1)} custom-call(f32[512,512]{1,0:T(8,128)S(1)} %upper_transposed.1.base, bf16[512,384]{1,0:T(8,128)(2,1)S(1)} %get-tuple-element.97.weight_turned, bf16[64,384]{1,0:T(8,128)(2,1)S(1)} %get-tuple-element.98.refs_0_, bf16[64,384]{1,0:T(8,128)(2,1)S(1)} %collective-permute-done.16.refs_1_, ...), custom_call_target="tpu_custom_call" | custom-call | flops 5000000000 | tf_op jit(solution)/shard_map/finish/pallas_call | solution.py:39
  (50 shorter events, 2.4 us)
Async XLA Ops:
  0.6 14.6 %collective-permute-start.1 = (bf16[384,512]{1,0:T(8,128)(2,1)}, bf16[384,512]{1,0:T(8,128)(2,1)S(1)}, u32[]{:S(2)}, u32[]{:S(2)}) collective-permute-start(bf16[384,512]{1,0:T(8,128)(2,1)} %bitcast.16), channel_id=1, source_target_pairs={{0,1},{1,0},{2,3},{3,2},{4,5},{5,4},{6,7},{7,6},{8,9},{9,8},{10,11... | collective-permute-start | bytes 1179656 | tf_op jit(solution)/shard_map/ppermute | solution.py:26
  1.1 12.5 %collective-permute-start = (bf16[384,512]{1,0:T(8,128)(2,1)}, bf16[384,512]{1,0:T(8,128)(2,1)S(1)}, u32[]{:S(2)}, u32[]{:S(2)}) collective-permute-start(bf16[384,512]{1,0:T(8,128)(2,1)} %bitcast.17), channel_id=1, source_target_pairs={{0,2},{1,3},{2,0},{3,1},{4,6},{5,7},{6,4},{7,5},{8,10},{9,11},{10,... | collective-permute-start | bytes 1179656 | tf_op jit(solution)/shard_map/ppermute | solution.py:26
  4.4 6.0 %collective-permute-start.11 = (s32[2,3]{1,0:T(2,128)S(1)}, s32[2,3]{1,0:T(2,128)S(1)}, u32[]{:S(2)}, u32[]{:S(2)}) collective-permute-start(s32[2,3]{1,0:T(2,128)S(1)} %pad_add_fusion.1), channel_id=1, source_target_pairs={{0,4},{1,5},{2,6},{3,7},{4,0},{5,1},{6,2},{7,3},{8,12},{9,13},{10,... | collective-permute-start | bytes 80 | tf_op jit(solution)/shard_map/ppermute | solution.py:26
  8.5 5.1 %copy-start.7 = (s32[1,3]{1,0:T(1,128)S(1)}, s32[1,3]{1,0:T(1,128)}, u32[]{:S(2)}) copy-start(s32[1,3]{1,0:T(1,128)} %param.11) | copy-start | bytes 40
  8.5 5.1 %copy-start.8 = (s32[1,3]{1,0:T(1,128)S(1)}, s32[1,3]{1,0:T(1,128)}, u32[]{:S(2)}) copy-start(s32[1,3]{1,0:T(1,128)} %param.12) | copy-start | bytes 40
  8.6 6.6 %copy-start.6 = (bf16[1,3,128,512]{3,2,1,0:T(8,128)(2,1)S(1)}, bf16[1,3,128,512]{3,2,1,0:T(8,128)(2,1)}, u32[]{:S(2)}) copy-start(bf16[1,3,128,512]{3,2,1,0:T(8,128)(2,1)} %param.10) | copy-start | bytes 1179652
  9.9 3.8 %collective-permute-start.2 = (bf16[256,512]{1,0:T(8,128)(2,1)S(1)}, bf16[256,512]{1,0:T(8,128)(2,1)S(1)}, u32[]{:S(2)}, u32[]{:S(2)}) collective-permute-start(bf16[256,512]{1,0:T(8,128)(2,1)S(1)} %get-tuple-element.55), channel_id=1, source_target_pairs={{0,1},{1,0},{2,3},{3,2},{4,5},{5,4},{6,7},{7,6},{8,9},{9,8},{10,11... | collective-permute-start | bytes 786440 | tf_op jit(solution)/shard_map/ppermute | solution.py:26
  10.0 4.3 %collective-permute-start.3 = (bf16[256,512]{1,0:T(8,128)(2,1)S(1)}, bf16[256,512]{1,0:T(8,128)(2,1)S(1)}, u32[]{:S(2)}, u32[]{:S(2)}) collective-permute-start(bf16[256,512]{1,0:T(8,128)(2,1)S(1)} %get-tuple-element.56), channel_id=1, source_target_pairs={{0,1},{1,0},{2,3},{3,2},{4,5},{5,4},{6,7},{7,6},{8,9},{9,8},{10,11... | collective-permute-start | bytes 786440 | tf_op jit(solution)/shard_map/ppermute | solution.py:26
  10.5 3.8 %collective-permute-start.4 = (bf16[256,512]{1,0:T(8,128)(2,1)S(1)}, bf16[256,512]{1,0:T(8,128)(2,1)S(1)}, u32[]{:S(2)}, u32[]{:S(2)}) collective-permute-start(bf16[256,512]{1,0:T(8,128)(2,1)S(1)} %get-tuple-element.57), channel_id=1, source_target_pairs={{0,1},{1,0},{2,3},{3,2},{4,5},{5,4},{6,7},{7,6},{8,9},{9,8},{10,11... | collective-permute-start | bytes 786440 | tf_op jit(solution)/shard_map/ppermute | solution.py:26
  13.7 1.5 %collective-permute-start.5 = (bf16[256,512]{1,0:T(8,128)(2,1)S(1)}, bf16[256,512]{1,0:T(8,128)(2,1)S(1)}, u32[]{:S(2)}, u32[]{:S(2)}) collective-permute-start(bf16[256,512]{1,0:T(8,128)(2,1)S(1)} %get-tuple-element.58), channel_id=1, source_target_pairs={{0,1},{1,0},{2,3},{3,2},{4,5},{5,4},{6,7},{7,6},{8,9},{9,8},{10,11... | collective-permute-start | bytes 786440 | tf_op jit(solution)/shard_map/ppermute | solution.py:26
  13.7 2.1 %collective-permute-start.6 = (bf16[384,512]{1,0:T(8,128)(2,1)S(1)}, bf16[384,512]{1,0:T(8,128)(2,1)S(1)}, u32[]{:S(2)}, u32[]{:S(2)}) collective-permute-start(bf16[384,512]{1,0:T(8,128)(2,1)S(1)} %collective-permute-done.refs_0_.refs_2_), channel_id=1, source_target_pairs={{0,1},{1,0},{2,3},{3,2},{4,5},{5,4},{6,7},{7,6},{8,9},{9,8},{10,11... | collective-permute-start | bytes 1179656 | tf_op jit(solution)/shard_map/ppermute | solution.py:26
  15.8 5.8 %copy-start.2 = (f32[1,3,256,512]{3,2,1,0:T(8,128)S(1)}, f32[1,3,256,512]{3,2,1,0:T(8,128)}, u32[]{:S(2)}) copy-start(f32[1,3,256,512]{3,2,1,0:T(8,128)} %param.15) | copy-start | bytes 4718596
  15.8 5.8 %copy-start.3 = (f32[1,3,256,256]{3,2,1,0:T(8,128)S(1)}, f32[1,3,256,256]{3,2,1,0:T(8,128)}, u32[]{:S(2)}) copy-start(f32[1,3,256,256]{3,2,1,0:T(8,128)} %param.13) | copy-start | bytes 2359300
  15.8 5.8 %copy-start.5 = (f32[1,2,256,256]{3,2,1,0:T(8,128)S(1)}, f32[1,2,256,256]{3,2,1,0:T(8,128)}, u32[]{:S(2)}) copy-start(f32[1,2,256,256]{3,2,1,0:T(8,128)} %param.14) | copy-start | bytes 1572868
  16.3 6.6 %collective-permute-start.8 = (bf16[64,384]{1,0:T(8,128)(2,1)S(1)}, bf16[64,384]{1,0:T(8,128)(2,1)S(1)}, u32[]{:S(2)}, u32[]{:S(2)}) collective-permute-start(bf16[64,384]{1,0:T(8,128)(2,1)S(1)} %get-tuple-element.66), channel_id=1, source_target_pairs={{0,6},{1,7},{2,4},{3,5},{4,2},{5,3},{6,0},{7,1},{8,14},{9,15},{10,... | collective-permute-start | bytes 147464 | tf_op jit(solution)/shard_map/ppermute | solution.py:26
  19.1 4.6 %collective-permute-start.9 = (bf16[64,384]{1,0:T(8,128)(2,1)S(1)}, bf16[64,384]{1,0:T(8,128)(2,1)S(1)}, u32[]{:S(2)}, u32[]{:S(2)}) collective-permute-start(bf16[64,384]{1,0:T(8,128)(2,1)S(1)} %get-tuple-element.67), channel_id=1, source_target_pairs={{0,2},{1,3},{2,0},{3,1},{4,6},{5,7},{6,4},{7,5},{8,10},{9,11},{10,... | collective-permute-start | bytes 147464 | tf_op jit(solution)/shard_map/ppermute | solution.py:26
  19.6 4.1 %collective-permute-start.10 = (bf16[64,384]{1,0:T(8,128)(2,1)S(1)}, bf16[64,384]{1,0:T(8,128)(2,1)S(1)}, u32[]{:S(2)}, u32[]{:S(2)}) collective-permute-start(bf16[64,384]{1,0:T(8,128)(2,1)S(1)} %get-tuple-element.68), channel_id=1, source_target_pairs={{0,4},{1,5},{2,6},{3,7},{4,0},{5,1},{6,2},{7,3},{8,12},{9,13},{10,... | collective-permute-start | bytes 147464 | tf_op jit(solution)/shard_map/ppermute | solution.py:26
  19.9 14.0 %collective-permute-start.7 = (bf16[2,256,512]{2,1,0:T(8,128)(2,1)S(1)}, bf16[2,256,512]{2,1,0:T(8,128)(2,1)S(1)}, u32[]{:S(2)}, u32[]{:S(2)}) collective-permute-start(bf16[2,256,512]{2,1,0:T(8,128)(2,1)S(1)} %get-tuple-element.64.high), channel_id=1, source_target_pairs={{0,2},{1,3},{2,0},{3,1},{4,6},{5,7},{6,4},{7,5},{8,10},{9,11},{10,... | collective-permute-start | bytes 1572872 | tf_op jit(solution)/shard_map/ppermute | solution.py:26
  21.6 7.4 %collective-permute-start.12 = (bf16[2,256,512]{2,1,0:T(8,128)(2,1)S(1)}, bf16[2,256,512]{2,1,0:T(8,128)(2,1)S(1)}, u32[]{:S(2)}, u32[]{:S(2)}) collective-permute-start(bf16[2,256,512]{2,1,0:T(8,128)(2,1)S(1)} %get-tuple-element.77.low.refs_4_), channel_id=1, source_target_pairs={{0,1},{1,0},{2,3},{3,2},{4,5},{5,4},{6,7},{7,6},{8,9},{9,8},{10,11... | collective-permute-start | bytes 1572872 | tf_op jit(solution)/shard_map/ppermute | solution.py:26
  23.7 5.3 %copy-start.1 = (bf16[1,2048,512]{2,1,0:T(8,128)(2,1)S(1)}, bf16[1,2048,512]{2,1,0:T(8,128)(2,1)}, u32[]{:S(2)}) copy-start(bf16[1,2048,512]{2,1,0:T(8,128)(2,1)} %param.9) | copy-start | bytes 6291460
  24.6 6.9 %collective-permute-start.15 = (bf16[1,64,256]{2,1,0:T(8,128)(2,1)S(1)}, bf16[1,64,256]{2,1,0:T(8,128)(2,1)S(1)}, u32[]{:S(2)}, u32[]{:S(2)}) collective-permute-start(bf16[1,64,256]{2,1,0:T(8,128)(2,1)S(1)} %get-tuple-element.84), channel_id=1, source_target_pairs={{0,24},{1,25},{2,26},{3,27},{4,28},{5,29},{6,30},{7,31},{8,16},{9,... | collective-permute-start | bytes 98312 | tf_op jit(solution)/shard_map/ppermute | solution.py:26
  28.2 4.8 %collective-permute-start.14 = (bf16[1,64,256]{2,1,0:T(8,128)(2,1)S(1)}, bf16[1,64,256]{2,1,0:T(8,128)(2,1)S(1)}, u32[]{:S(2)}, u32[]{:S(2)}) collective-permute-start(bf16[1,64,256]{2,1,0:T(8,128)(2,1)S(1)} %get-tuple-element.84), channel_id=1, source_target_pairs={{0,16},{1,17},{2,18},{3,19},{4,20},{5,21},{6,22},{7,23},{8,24},{9,... | collective-permute-start | bytes 98312 | tf_op jit(solution)/shard_map/ppermute | solution.py:26
  28.2 4.8 %collective-permute-start.13 = (bf16[2,64,256]{2,1,0:T(8,128)(2,1)S(1)}, bf16[2,64,256]{2,1,0:T(8,128)(2,1)S(1)}, u32[]{:S(2)}, u32[]{:S(2)}) collective-permute-start(bf16[2,64,256]{2,1,0:T(8,128)(2,1)S(1)} %get-tuple-element.83), channel_id=1, source_target_pairs={{0,8},{1,9},{2,10},{3,11},{4,12},{5,13},{6,14},{7,15},{8,0},{9,1},... | collective-permute-start | bytes 196616 | tf_op jit(solution)/shard_map/ppermute | solution.py:26
  34.1 3.6 %collective-permute-start.19 = (bf16[2,256,512]{2,1,0:T(8,128)(2,1)S(1)}, bf16[2,256,512]{2,1,0:T(8,128)(2,1)S(1)}, u32[]{:S(2)}, u32[]{:S(2)}) collective-permute-start(bf16[2,256,512]{2,1,0:T(8,128)(2,1)S(1)} %add_convert_fusion.refs_0_), channel_id=1, source_target_pairs={{0,1},{1,0},{2,3},{3,2},{4,5},{5,4},{6,7},{7,6},{8,9},{9,8},{10,11... | collective-permute-start | bytes 1572872 | tf_op jit(solution)/shard_map/ppermute | solution.py:26
  34.1 7.1 %collective-permute-start.18 = (bf16[64,384]{1,0:T(8,128)(2,1)S(1)}, bf16[64,384]{1,0:T(8,128)(2,1)S(1)}, u32[]{:S(2)}, u32[]{:S(2)}) collective-permute-start(bf16[64,384]{1,0:T(8,128)(2,1)S(1)} %get-tuple-element.87), channel_id=1, source_target_pairs={{0,6},{1,7},{2,4},{3,5},{4,2},{5,3},{6,0},{7,1},{8,14},{9,15},{10,... | collective-permute-start | bytes 147464 | tf_op jit(solution)/shard_map/ppermute | solution.py:26
  36.0 5.2 %collective-permute-start.17 = (bf16[64,384]{1,0:T(8,128)(2,1)S(1)}, bf16[64,384]{1,0:T(8,128)(2,1)S(1)}, u32[]{:S(2)}, u32[]{:S(2)}) collective-permute-start(bf16[64,384]{1,0:T(8,128)(2,1)S(1)} %get-tuple-element.87), channel_id=1, source_target_pairs={{0,4},{1,5},{2,6},{3,7},{4,0},{5,1},{6,2},{7,3},{8,12},{9,13},{10,... | collective-permute-start | bytes 147464 | tf_op jit(solution)/shard_map/ppermute | solution.py:26
  37.2 4.1 %collective-permute-start.16 = (bf16[64,384]{1,0:T(8,128)(2,1)S(1)}, bf16[64,384]{1,0:T(8,128)(2,1)S(1)}, u32[]{:S(2)}, u32[]{:S(2)}) collective-permute-start(bf16[64,384]{1,0:T(8,128)(2,1)S(1)} %get-tuple-element.98.refs_0_), channel_id=1, source_target_pairs={{0,2},{1,3},{2,0},{3,1},{4,6},{5,7},{6,4},{7,5},{8,10},{9,11},{10,... | collective-permute-start | bytes 147464 | tf_op jit(solution)/shard_map/ppermute | solution.py:26
  37.7 4.7 %collective-permute-start.20 = (bf16[3,64,256]{2,1,0:T(8,128)(2,1)S(1)}, bf16[3,64,256]{2,1,0:T(8,128)(2,1)S(1)}, u32[]{:S(2)}, u32[]{:S(2)}) collective-permute-start(bf16[3,64,256]{2,1,0:T(8,128)(2,1)S(1)} %get-tuple-element.96), channel_id=1, source_target_pairs={{0,4},{1,5},{2,6},{3,7},{4,0},{5,1},{6,2},{7,3},{8,12},{9,13},{10,... | collective-permute-start | bytes 294920 | tf_op jit(solution)/shard_map/ppermute | solution.py:26
  41.3 2.0 %collective-permute-start.21 = (bf16[64,384]{1,0:T(8,128)(2,1)S(1)}, bf16[64,384]{1,0:T(8,128)(2,1)S(1)}, u32[]{:S(2)}, u32[]{:S(2)}) collective-permute-start(bf16[64,384]{1,0:T(8,128)(2,1)S(1)} %get-tuple-element.98.refs_0_), channel_id=1, source_target_pairs={{0,1},{1,0},{2,3},{3,2},{4,5},{5,4},{6,7},{7,6},{8,9},{9,8},{10,11... | collective-permute-start | bytes 147464 | tf_op jit(solution)/shard_map/ppermute | solution.py:26
  41.3 2.0 %collective-permute-start.22 = (bf16[64,384]{1,0:T(8,128)(2,1)S(1)}, bf16[64,384]{1,0:T(8,128)(2,1)S(1)}, u32[]{:S(2)}, u32[]{:S(2)}) collective-permute-start(bf16[64,384]{1,0:T(8,128)(2,1)S(1)} %collective-permute-done.16.refs_1_), channel_id=1, source_target_pairs={{0,1},{1,0},{2,3},{3,2},{4,5},{5,4},{6,7},{7,6},{8,9},{9,8},{10,11... | collective-permute-start | bytes 147464 | tf_op jit(solution)/shard_map/ppermute | solution.py:26
  41.8 1.5 %collective-permute-start.23 = (bf16[64,384]{1,0:T(8,128)(2,1)S(1)}, bf16[64,384]{1,0:T(8,128)(2,1)S(1)}, u32[]{:S(2)}, u32[]{:S(2)}) collective-permute-start(bf16[64,384]{1,0:T(8,128)(2,1)S(1)} %collective-permute-done.17.refs_2_), channel_id=1, source_target_pairs={{0,1},{1,0},{2,3},{3,2},{4,5},{5,4},{6,7},{7,6},{8,9},{9,8},{10,11... | collective-permute-start | bytes 147464 | tf_op jit(solution)/shard_map/ppermute | solution.py:26
  41.8 1.5 %collective-permute-start.24 = (bf16[64,384]{1,0:T(8,128)(2,1)S(1)}, bf16[64,384]{1,0:T(8,128)(2,1)S(1)}, u32[]{:S(2)}, u32[]{:S(2)}) collective-permute-start(bf16[64,384]{1,0:T(8,128)(2,1)S(1)} %collective-permute-done.18.refs_3_), channel_id=1, source_target_pairs={{0,1},{1,0},{2,3},{3,2},{4,5},{5,4},{6,7},{7,6},{8,9},{9,8},{10,11... | collective-permute-start | bytes 147464 | tf_op jit(solution)/shard_map/ppermute | solution.py:26
  (2 other events, 2.6 us)

commit v6 on v5

--- a/solution.py
+++ b/solution.py
@@ -303,8 +303,6 @@
         return jax.ShapeDtypeStruct(dims, dtype)
 
     held = {0: panel, half: moved(panel, 0, half)}
-    for mask in range(1, half):
-        held[mask] = moved(panel, 0, mask)
 
     mine_rows = (groups, sources // half, rows)
     upper_rows = (half, sources // half, rows)
@@ -315,6 +313,9 @@
         [inverse, rhs],
         [pltpu.VMEM((sources, rows), BF16)],
     )
+    keep, offsets, pattern, panel = lax.optimization_barrier((keep, offsets, pattern, panel))
+    for mask in range(1, half):
+        held[mask] = moved(panel, 0, mask)
     spots = jnp.concatenate([offsets, pattern], axis=0)
     spots = jnp.concatenate([spots, moved(spots, 1, 0)], axis=0)
     received = [moved(block, 0, n // groups + 1) for n, block in enumerate(sends)]
@@ -384,7 +385,7 @@
         [kept, right, q_high, q_low, k_high, k_low, place, *up_received],
     )
 
-    high, mine = lax.optimization_barrier((high, mine))
+    mine, high = lax.optimization_barrier((mine, high))
     solved = (upper + high.astype(F32)).astype(BF16)
     solved = [solved] + [moved(solved, 0, j) for j in range(1, half)]
     *solved, passed = lax.optimization_barrier((*solved, passed))

time: 44.8 us -> 44.9 us (level)
  other arithmetic: 0.85 us -> 0.18 us
  waiting for transfers between devices: 7.95 us -> 8.62 us
    concatenate x1, other arithmetic: 0.68 us -> 0.01 us  [on_device(): spots = jnp.concatenate([offsets, pattern], axis=0)]
    ppermute x25, waiting for transfers between devices: 7.95 us -> 8.62 us  [moved(): return lax.ppermute(block, AXES, route)]
  transfers between devices with their start and end apart: 25 -> 25, of which waited for: 6 -> 10; matrix products, arithmetic and copies ran while one was open for 2% -> 0% of each run, Pallas kernels for 20% -> 20%
where the time goes in v6:
time: 44.9 us; the launch traced here: 44.7 us
  starting transfers between devices  21.5 us (48%)
  Pallas kernels  10.9 us (24%)
  waiting for transfers between devices  8.62 us (19%)
  local copies, waits for them, and re-layouts  2.67 us (6%)
  between operations  0.85 us (2%)
    ppermute x25, starting transfers between devices, moved(): return lax.ppermute(block, AXES, route)  21.5 us
    pallas_call x11, Pallas kernels, call(): pl.pallas_call(body, out_shape=outs, in_specs=specs, out_specs=[pl.BlockS...  10.9 us
    ppermute x25, waiting for transfers between devices, moved(): return lax.ppermute(block, AXES, route)  8.62 us
    unnamed x18, local copies, waits for them, and re-layouts  2.67 us
  transfers between devices with their start and end apart: 25, of which 10 were waited for; matrix products, arithmetic and copies ran while one was open for 0% of the time, Pallas kernels for 20%

profile of v6, /device:TPU:0, one launch (start us, length us, event | category | flops | bytes accessed | tf_op | source)
XLA Modules:
  0.0 44.7 jit_solution(16929548368065122776)
XLA Ops:
  0.6 3.0 %collective-permute-start = (bf16[384,512]{1,0:T(8,128)(2,1)}, bf16[384,512]{1,0:T(8,128)(2,1)S(1)}, u32[]{:S(2)}, u32[]{:S(2)}) collective-permute-start(bf16[384,512]{1,0:T(8,128)(2,1)} %bitcast.16), channel_id=1, source_target_pairs={{0,2},{1,3},{2,0},{3,1},{4,6},{5,7},{6,4},{7,5},{8,10},{9,11},{10,... | collective-permute-start | bytes 1179656 | tf_op jit(solution)/shard_map/ppermute | solution.py:26
  3.7 1.6 %copy-done = bf16[1,2048,512]{2,1,0:T(8,128)(2,1)S(1)} copy-done((bf16[1,2048,512]{2,1,0:T(8,128)(2,1)S(1)}, bf16[1,2048,512]{2,1,0:T(8,128)(2,1)}, u32[]{:S(2)}) %copy-start) | copy-done | bytes 2097176
  5.3 1.0 %copy-done.4 = bf16[1,512,512]{2,1,0:T(8,128)(2,1)S(1)} copy-done((bf16[1,512,512]{2,1,0:T(8,128)(2,1)S(1)}, bf16[1,512,512]{2,1,0:T(8,128)(2,1)}, u32[]{:S(2)}) %copy-start.4) | copy-done | bytes 524312
  6.3 1.3 %leaf_products.1 = (f32[4,256,512]{2,1,0:T(8,128)S(1)}, bf16[256,512]{1,0:T(8,128)(2,1)S(1)}, bf16[256,512]{1,0:T(8,128)(2,1)S(1)}, bf16[256,512]{1,0:T(8,128)(2,1)S(1)}, bf16[256,512]{1,0:T(8,128)(2,1)S(1)}) custom-call(bf16[2048,512]{1,0:T(8,128)(2,1)S(1)} %bitcast.8, bf16[512,512]{1,0:T(8,128)(2,1)S(1)} %bitcast.14), custom_call_target="tpu_custom_call" | custom-call | flops 5000000000 | tf_op jit(solution)/shard_map/leaf_products/pallas_call | solution.py:39
  7.7 0.5 %collective-permute-start.2 = (bf16[256,512]{1,0:T(8,128)(2,1)S(1)}, bf16[256,512]{1,0:T(8,128)(2,1)S(1)}, u32[]{:S(2)}, u32[]{:S(2)}) collective-permute-start(bf16[256,512]{1,0:T(8,128)(2,1)S(1)} %get-tuple-element.61), channel_id=1, source_target_pairs={{0,1},{1,0},{2,3},{3,2},{4,5},{5,4},{6,7},{7,6},{8,9},{9,8},{10,11... | collective-permute-start | bytes 786440 | tf_op jit(solution)/shard_map/ppermute | solution.py:26
  8.3 1.6 %collective-permute-start.10 = (s32[2,3]{1,0:T(2,128)S(1)}, s32[2,3]{1,0:T(2,128)S(1)}, u32[]{:S(2)}, u32[]{:S(2)}) collective-permute-start(s32[2,3]{1,0:T(2,128)S(1)} %pad_add_fusion.1), channel_id=1, source_target_pairs={{0,4},{1,5},{2,6},{3,7},{4,0},{5,1},{6,2},{7,3},{8,12},{9,13},{10,... | collective-permute-start | bytes 80 | tf_op jit(solution)/shard_map/ppermute | solution.py:26
  9.9 2.1 %collective-permute-done.10 = s32[2,3]{1,0:T(2,128)S(1)} collective-permute-done((s32[2,3]{1,0:T(2,128)S(1)}, s32[2,3]{1,0:T(2,128)S(1)}, u32[]{:S(2)}, u32[]{:S(2)}) %collective-permute-start.10) | collective-permute-done | bytes 56 | tf_op jit(solution)/shard_map/ppermute | solution.py:26
  11.9 1.0 %collective-permute-done.refs_0_.refs_2_ = bf16[384,512]{1,0:T(8,128)(2,1)S(1)} collective-permute-done((bf16[384,512]{1,0:T(8,128)(2,1)}, bf16[384,512]{1,0:T(8,128)(2,1)S(1)}, u32[]{:S(2)}, u32[]{:S(2)}) %collective-permute-start) | collective-permute-done | bytes 393248 | tf_op jit(solution)/shard_map/ppermute | solution.py:26
  13.0 0.6 %collective-permute-start.6 = (bf16[384,512]{1,0:T(8,128)(2,1)S(1)}, bf16[384,512]{1,0:T(8,128)(2,1)S(1)}, u32[]{:S(2)}, u32[]{:S(2)}) collective-permute-start(bf16[384,512]{1,0:T(8,128)(2,1)S(1)} %collective-permute-done.refs_0_.refs_2_), channel_id=1, source_target_pairs={{0,1},{1,0},{2,3},{3,2},{4,5},{5,4},{6,7},{7,6},{8,9},{9,8},{10,11... | collective-permute-start | bytes 1179656 | tf_op jit(solution)/shard_map/ppermute | solution.py:26
  13.6 0.9 %collective-permute-done.5.refs_5_ = bf16[256,512]{1,0:T(8,128)(2,1)S(1)} collective-permute-done((bf16[256,512]{1,0:T(8,128)(2,1)S(1)}, bf16[256,512]{1,0:T(8,128)(2,1)S(1)}, u32[]{:S(2)}, u32[]{:S(2)}) %collective-permute-start.5) | collective-permute-done | bytes 262176 | tf_op jit(solution)/shard_map/ppermute | solution.py:26
  14.5 0.6 %own_partials.1 = (bf16[2,256,512]{2,1,0:T(8,128)(2,1)S(1)}, bf16[2,256,512]{2,1,0:T(8,128)(2,1)S(1)}, f32[2,256,512]{2,1,0:T(8,128)S(1)}, f32[256,384]{1,0:T(8,128)S(1)}) custom-call(f32[4,256,512]{2,1,0:T(8,128)S(1)} %get-tuple-element.59.keep, bf16[384,512]{1,0:T(8,128)(2,1)S(1)} %bitcast.18, bf16[384,512]{1,0:T(8,128)(2,1)S(1)} %collective-permute-done.1.refs_1_, ...), custom_call_target="tpu_custom_call" | custom-call | flops 5000000000 | tf_op jit(solution)/shard_map/own_partials/pallas_call | solution.py:39
  15.2 0.5 %partials.1 = (f32[64,384]{1,0:T(8,128)S(1)}, bf16[64,384]{1,0:T(8,128)(2,1)S(1)}, bf16[64,384]{1,0:T(8,128)(2,1)S(1)}, bf16[64,384]{1,0:T(8,128)(2,1)S(1)}) custom-call(bf16[2,256,512]{2,1,0:T(8,128)(2,1)S(1)} %get-tuple-element.84.low.refs_4_, bf16[2,256,512]{2,1,0:T(8,128)(2,1)S(1)} %get-tuple-element.93.high, f32[256,384]{1,0:T(8,128)S(1)} %get-tuple-element.67.early, ...), custom_call_target="tpu_custom_call" | custom-call | flops 5000000000 | tf_op jit(solution)/shard_map/partials/pallas_call | solution.py:39
  15.7 2.7 %collective-permute-start.7 = (bf16[64,384]{1,0:T(8,128)(2,1)S(1)}, bf16[64,384]{1,0:T(8,128)(2,1)S(1)}, u32[]{:S(2)}, u32[]{:S(2)}) collective-permute-start(bf16[64,384]{1,0:T(8,128)(2,1)S(1)} %get-tuple-element.71), channel_id=1, source_target_pairs={{0,6},{1,7},{2,4},{3,5},{4,2},{5,3},{6,0},{7,1},{8,14},{9,15},{10,... | collective-permute-start | bytes 147464 | tf_op jit(solution)/shard_map/ppermute | solution.py:26
  18.4 0.5 %collective-permute-start.8 = (bf16[64,384]{1,0:T(8,128)(2,1)S(1)}, bf16[64,384]{1,0:T(8,128)(2,1)S(1)}, u32[]{:S(2)}, u32[]{:S(2)}) collective-permute-start(bf16[64,384]{1,0:T(8,128)(2,1)S(1)} %get-tuple-element.72), channel_id=1, source_target_pairs={{0,2},{1,3},{2,0},{3,1},{4,6},{5,7},{6,4},{7,5},{8,10},{9,11},{10,... | collective-permute-start | bytes 147464 | tf_op jit(solution)/shard_map/ppermute | solution.py:26
  19.2 1.7 %collective-permute-start.15 = (bf16[2,256,512]{2,1,0:T(8,128)(2,1)S(1)}, bf16[2,256,512]{2,1,0:T(8,128)(2,1)S(1)}, u32[]{:S(2)}, u32[]{:S(2)}) collective-permute-start(bf16[2,256,512]{2,1,0:T(8,128)(2,1)S(1)} %get-tuple-element.93.high), channel_id=1, source_target_pairs={{0,2},{1,3},{2,0},{3,1},{4,6},{5,7},{6,4},{7,5},{8,10},{9,11},{10,... | collective-permute-start | bytes 1572872 | tf_op jit(solution)/shard_map/ppermute | solution.py:26
  21.0 1.3 %prepare.1 = (bf16[2,256,256]{2,1,0:T(8,128)(2,1)S(1)}, bf16[2,256,256]{2,1,0:T(8,128)(2,1)S(1)}, f32[3,64,256]{2,1,0:T(8,128)S(1)}, bf16[3,256,256]{2,1,0:T(8,128)(2,1)S(1)}) custom-call(s32[4,3]{1,0:T(4,128)S(1)} %pad_add_fusion.spots, f32[3,256,256]{2,1,0:T(8,128)S(1)} %bitcast.12, f32[2,256,256]{2,1,0:T(8,128)S(1)} %bitcast.15, f32[3,256,512]{2,1,0:T(8,128)S(1)} %bitcast.11), custom_call_target="tpu_custom_call" | custom-call | flops 5000000000 | tf_op jit(solution)/shard_map/prepare/pallas_call | solution.py:39
  22.3 0.5 %collective-permute-done.8.same = bf16[64,384]{1,0:T(8,128)(2,1)S(1)} collective-permute-done((bf16[64,384]{1,0:T(8,128)(2,1)S(1)}, bf16[64,384]{1,0:T(8,128)(2,1)S(1)}, u32[]{:S(2)}, u32[]{:S(2)}) %collective-permute-start.8) | collective-permute-done | bytes 49184 | tf_op jit(solution)/shard_map/ppermute | solution.py:26
  23.0 0.8 %upward.1 = (f32[3,64,256]{2,1,0:T(8,128)S(1)}, bf16[2,64,256]{2,1,0:T(8,128)(2,1)S(1)}, bf16[1,64,256]{2,1,0:T(8,128)(2,1)S(1)}) custom-call(f32[64,384]{1,0:T(8,128)S(1)} %get-tuple-element.70.own, bf16[64,384]{1,0:T(8,128)(2,1)S(1)} %collective-permute-done.7.cross, bf16[64,384]{1,0:T(8,128)(2,1)S(1)} %collective-permute-done.8.same, ...), custom_call_target="tpu_custom_call" | custom-call | flops 5000000000 | tf_op jit(solution)/shard_map/upward/pallas_call | solution.py:39
  23.8 2.7 %collective-permute-start.13 = (bf16[1,64,256]{2,1,0:T(8,128)(2,1)S(1)}, bf16[1,64,256]{2,1,0:T(8,128)(2,1)S(1)}, u32[]{:S(2)}, u32[]{:S(2)}) collective-permute-start(bf16[1,64,256]{2,1,0:T(8,128)(2,1)S(1)} %get-tuple-element.91), channel_id=1, source_target_pairs={{0,16},{1,17},{2,18},{3,19},{4,20},{5,21},{6,22},{7,23},{8,24},{9,... | collective-permute-start | bytes 98312 | tf_op jit(solution)/shard_map/ppermute | solution.py:26
  26.5 1.3 %collective-permute-start.14 = (bf16[1,64,256]{2,1,0:T(8,128)(2,1)S(1)}, bf16[1,64,256]{2,1,0:T(8,128)(2,1)S(1)}, u32[]{:S(2)}, u32[]{:S(2)}) collective-permute-start(bf16[1,64,256]{2,1,0:T(8,128)(2,1)S(1)} %get-tuple-element.91), channel_id=1, source_target_pairs={{0,24},{1,25},{2,26},{3,27},{4,28},{5,29},{6,30},{7,31},{8,16},{9,... | collective-permute-start | bytes 98312 | tf_op jit(solution)/shard_map/ppermute | solution.py:26
  28.1 1.5 %lower_transposed.1 = (f32[512,512]{1,0:T(8,128)S(1)}, bf16[512,384]{1,0:T(8,128)(2,1)S(1)}) custom-call(bf16[2048,512]{1,0:T(8,128)(2,1)S(1)} %bitcast.9, bf16[384,512]{1,0:T(8,128)(2,1)S(1)} %bitcast.19, bf16[384,512]{1,0:T(8,128)(2,1)S(1)} %collective-permute-done.1.refs_1_, bf16[384,512]{1,0:T(8,128)(2,1)S(1)} %collective-permute-done.refs_0_.refs_2_, ...), custom_call_target="tpu_custom_call" | custom-call | flops 5000000000 | tf_op jit(solution)/shard_map/lower_transposed/pallas_call | solution.py:39
  29.6 0.9 %squares.1 = (bf16[3,256,256]{2,1,0:T(8,128)(2,1)S(1)}, bf16[3,256,256]{2,1,0:T(8,128)(2,1)S(1)}) custom-call(f32[3,256,256]{2,1,0:T(8,128)S(1)} %bitcast.13), custom_call_target="tpu_custom_call" | custom-call | flops 5000000000 | tf_op jit(solution)/shard_map/squares/pallas_call | solution.py:39
  30.5 1.8 %collective-permute-done.14.refs_2_ = bf16[1,64,256]{2,1,0:T(8,128)(2,1)S(1)} collective-permute-done((bf16[1,64,256]{2,1,0:T(8,128)(2,1)S(1)}, bf16[1,64,256]{2,1,0:T(8,128)(2,1)S(1)}, u32[]{:S(2)}, u32[]{:S(2)}) %collective-permute-start.14) | collective-permute-done | bytes 32800 | tf_op jit(solution)/shard_map/ppermute | solution.py:26
  32.5 0.8 %downward.1 = (f32[3,64,256]{2,1,0:T(8,128)S(1)}, bf16[64,384]{1,0:T(8,128)(2,1)S(1)}, bf16[64,384]{1,0:T(8,128)(2,1)S(1)}, bf16[3,64,256]{2,1,0:T(8,128)(2,1)S(1)}) custom-call(f32[3,64,256]{2,1,0:T(8,128)S(1)} %get-tuple-element.82.kept, f32[3,64,256]{2,1,0:T(8,128)S(1)} %get-tuple-element.77.right, bf16[3,256,256]{2,1,0:T(8,128)(2,1)S(1)} %get-tuple-element.88.q_high, ...), custom_call_target="tpu_custom_call" | custom-call | flops 5000000000 | tf_op jit(solution)/shard_map/downward/pallas_call | solution.py:39
  34.0 1.6 %collective-permute-start.17 = (bf16[64,384]{1,0:T(8,128)(2,1)S(1)}, bf16[64,384]{1,0:T(8,128)(2,1)S(1)}, u32[]{:S(2)}, u32[]{:S(2)}) collective-permute-start(bf16[64,384]{1,0:T(8,128)(2,1)S(1)} %get-tuple-element.95), channel_id=1, source_target_pairs={{0,4},{1,5},{2,6},{3,7},{4,0},{5,1},{6,2},{7,3},{8,12},{9,13},{10,... | collective-permute-start | bytes 147464 | tf_op jit(solution)/shard_map/ppermute | solution.py:26
  35.6 1.5 %collective-permute-start.18 = (bf16[64,384]{1,0:T(8,128)(2,1)S(1)}, bf16[64,384]{1,0:T(8,128)(2,1)S(1)}, u32[]{:S(2)}, u32[]{:S(2)}) collective-permute-start(bf16[64,384]{1,0:T(8,128)(2,1)S(1)} %get-tuple-element.95), channel_id=1, source_target_pairs={{0,6},{1,7},{2,4},{3,5},{4,2},{5,3},{6,0},{7,1},{8,14},{9,15},{10,... | collective-permute-start | bytes 147464 | tf_op jit(solution)/shard_map/ppermute | solution.py:26
  37.5 1.5 %collective-permute-start.20 = (bf16[3,64,256]{2,1,0:T(8,128)(2,1)S(1)}, bf16[3,64,256]{2,1,0:T(8,128)(2,1)S(1)}, u32[]{:S(2)}, u32[]{:S(2)}) collective-permute-start(bf16[3,64,256]{2,1,0:T(8,128)(2,1)S(1)} %get-tuple-element.104), channel_id=1, source_target_pairs={{0,4},{1,5},{2,6},{3,7},{4,0},{5,1},{6,2},{7,3},{8,12},{9,13},{10,... | collective-permute-start | bytes 294920 | tf_op jit(solution)/shard_map/ppermute | solution.py:26
  39.1 0.9 %upper_transposed.1.base = f32[512,512]{1,0:T(8,128)S(1)} custom-call(bf16[2048,512]{1,0:T(8,128)(2,1)S(1)} %bitcast.10, f32[512,512]{1,0:T(8,128)S(1)} %get-tuple-element.96.lower, bf16[2,256,512]{2,1,0:T(8,128)(2,1)S(1)} %add_convert_fusion.refs_0_, bf16[2,256,512]{2,1,0:T(8,128)(2,1)S(1)} %collective-permute-done.19.refs_1_), custom_call_target="tpu_custom_call" | custom-call | flops 5000000000 | tf_op jit(solution)/shard_map/upper_transposed/pallas_call | solution.py:39
  40.0 1.4 %collective-permute-done.16.refs_1_ = bf16[64,384]{1,0:T(8,128)(2,1)S(1)} collective-permute-done((bf16[64,384]{1,0:T(8,128)(2,1)S(1)}, bf16[64,384]{1,0:T(8,128)(2,1)S(1)}, u32[]{:S(2)}, u32[]{:S(2)}) %collective-permute-start.16) | collective-permute-done | bytes 49184 | tf_op jit(solution)/shard_map/ppermute | solution.py:26
  41.4 0.5 %collective-permute-start.22 = (bf16[64,384]{1,0:T(8,128)(2,1)S(1)}, bf16[64,384]{1,0:T(8,128)(2,1)S(1)}, u32[]{:S(2)}, u32[]{:S(2)}) collective-permute-start(bf16[64,384]{1,0:T(8,128)(2,1)S(1)} %collective-permute-done.16.refs_1_), channel_id=1, source_target_pairs={{0,1},{1,0},{2,3},{3,2},{4,5},{5,4},{6,7},{7,6},{8,9},{9,8},{10,11... | collective-permute-start | bytes 147464 | tf_op jit(solution)/shard_map/ppermute | solution.py:26
  42.5 0.9 %assemble.1 = f32[3,256,128]{2,1,0:T(8,128)} custom-call(f32[3,64,256]{2,1,0:T(8,128)S(1)} %get-tuple-element.110.mine, bf16[3,64,256]{2,1,0:T(8,128)(2,1)S(1)} %collective-permute-done.20.passed), custom_call_target="tpu_custom_call" | custom-call | flops 5000000000 | tf_op jit(solution)/shard_map/assemble/pallas_call | solution.py:39
  43.4 1.3 %finish.1 = bf16[512,512]{1,0:T(8,128)(2,1)} custom-call(f32[512,512]{1,0:T(8,128)S(1)} %upper_transposed.1.base, bf16[512,384]{1,0:T(8,128)(2,1)S(1)} %get-tuple-element.105.weight_turned, bf16[64,384]{1,0:T(8,128)(2,1)S(1)} %get-tuple-element.106.refs_0_, bf16[64,384]{1,0:T(8,128)(2,1)S(1)} %collective-permute-done.16.refs_1_, ...), custom_call_target="tpu_custom_call" | custom-call | flops 5000000000 | tf_op jit(solution)/shard_map/finish/pallas_call | solution.py:39
  (50 shorter events, 2.9 us)
Async XLA Ops:
  0.6 12.4 %collective-permute-start = (bf16[384,512]{1,0:T(8,128)(2,1)}, bf16[384,512]{1,0:T(8,128)(2,1)S(1)}, u32[]{:S(2)}, u32[]{:S(2)}) collective-permute-start(bf16[384,512]{1,0:T(8,128)(2,1)} %bitcast.16), channel_id=1, source_target_pairs={{0,2},{1,3},{2,0},{3,1},{4,6},{5,7},{6,4},{7,5},{8,10},{9,11},{10,... | collective-permute-start | bytes 1179656 | tf_op jit(solution)/shard_map/ppermute | solution.py:26
  3.7 1.6 %copy-start = (bf16[1,2048,512]{2,1,0:T(8,128)(2,1)S(1)}, bf16[1,2048,512]{2,1,0:T(8,128)(2,1)}, u32[]{:S(2)}) copy-start(bf16[1,2048,512]{2,1,0:T(8,128)(2,1)} %param.9) | copy-start | bytes 6291460
  6.3 2.0 %copy-start.7 = (s32[1,3]{1,0:T(1,128)S(1)}, s32[1,3]{1,0:T(1,128)}, u32[]{:S(2)}) copy-start(s32[1,3]{1,0:T(1,128)} %param.11) | copy-start | bytes 40
  6.3 2.0 %copy-start.8 = (s32[1,3]{1,0:T(1,128)S(1)}, s32[1,3]{1,0:T(1,128)}, u32[]{:S(2)}) copy-start(s32[1,3]{1,0:T(1,128)} %param.12) | copy-start | bytes 40
  7.6 6.9 %collective-permute-start.1 = (bf16[384,512]{1,0:T(8,128)(2,1)S(1)}, bf16[384,512]{1,0:T(8,128)(2,1)S(1)}, u32[]{:S(2)}, u32[]{:S(2)}) collective-permute-start(bf16[384,512]{1,0:T(8,128)(2,1)S(1)} %bitcast.17), channel_id=1, source_target_pairs={{0,1},{1,0},{2,3},{3,2},{4,5},{5,4},{6,7},{7,6},{8,9},{9,8},{10,11... | collective-permute-start | bytes 1179656 | tf_op jit(solution)/shard_map/ppermute | solution.py:26
  7.7 5.3 %collective-permute-start.2 = (bf16[256,512]{1,0:T(8,128)(2,1)S(1)}, bf16[256,512]{1,0:T(8,128)(2,1)S(1)}, u32[]{:S(2)}, u32[]{:S(2)}) collective-permute-start(bf16[256,512]{1,0:T(8,128)(2,1)S(1)} %get-tuple-element.61), channel_id=1, source_target_pairs={{0,1},{1,0},{2,3},{3,2},{4,5},{5,4},{6,7},{7,6},{8,9},{9,8},{10,11... | collective-permute-start | bytes 786440 | tf_op jit(solution)/shard_map/ppermute | solution.py:26
  8.2 5.4 %collective-permute-start.3 = (bf16[256,512]{1,0:T(8,128)(2,1)S(1)}, bf16[256,512]{1,0:T(8,128)(2,1)S(1)}, u32[]{:S(2)}, u32[]{:S(2)}) collective-permute-start(bf16[256,512]{1,0:T(8,128)(2,1)S(1)} %get-tuple-element.62), channel_id=1, source_target_pairs={{0,1},{1,0},{2,3},{3,2},{4,5},{5,4},{6,7},{7,6},{8,9},{9,8},{10,11... | collective-permute-start | bytes 786440 | tf_op jit(solution)/shard_map/ppermute | solution.py:26
  8.3 3.6 %collective-permute-start.10 = (s32[2,3]{1,0:T(2,128)S(1)}, s32[2,3]{1,0:T(2,128)S(1)}, u32[]{:S(2)}, u32[]{:S(2)}) collective-permute-start(s32[2,3]{1,0:T(2,128)S(1)} %pad_add_fusion.1), channel_id=1, source_target_pairs={{0,4},{1,5},{2,6},{3,7},{4,0},{5,1},{6,2},{7,3},{8,12},{9,13},{10,... | collective-permute-start | bytes 80 | tf_op jit(solution)/shard_map/ppermute | solution.py:26
  11.9 1.7 %collective-permute-start.4 = (bf16[256,512]{1,0:T(8,128)(2,1)S(1)}, bf16[256,512]{1,0:T(8,128)(2,1)S(1)}, u32[]{:S(2)}, u32[]{:S(2)}) collective-permute-start(bf16[256,512]{1,0:T(8,128)(2,1)S(1)} %get-tuple-element.63), channel_id=1, source_target_pairs={{0,1},{1,0},{2,3},{3,2},{4,5},{5,4},{6,7},{7,6},{8,9},{9,8},{10,11... | collective-permute-start | bytes 786440 | tf_op jit(solution)/shard_map/ppermute | solution.py:26
  13.0 1.5 %collective-permute-start.5 = (bf16[256,512]{1,0:T(8,128)(2,1)S(1)}, bf16[256,512]{1,0:T(8,128)(2,1)S(1)}, u32[]{:S(2)}, u32[]{:S(2)}) collective-permute-start(bf16[256,512]{1,0:T(8,128)(2,1)S(1)} %get-tuple-element.64), channel_id=1, source_target_pairs={{0,1},{1,0},{2,3},{3,2},{4,5},{5,4},{6,7},{7,6},{8,9},{9,8},{10,11... | collective-permute-start | bytes 786440 | tf_op jit(solution)/shard_map/ppermute | solution.py:26
  13.0 2.1 %collective-permute-start.6 = (bf16[384,512]{1,0:T(8,128)(2,1)S(1)}, bf16[384,512]{1,0:T(8,128)(2,1)S(1)}, u32[]{:S(2)}, u32[]{:S(2)}) collective-permute-start(bf16[384,512]{1,0:T(8,128)(2,1)S(1)} %collective-permute-done.refs_0_.refs_2_), channel_id=1, source_target_pairs={{0,1},{1,0},{2,3},{3,2},{4,5},{5,4},{6,7},{7,6},{8,9},{9,8},{10,11... | collective-permute-start | bytes 1179656 | tf_op jit(solution)/shard_map/ppermute | solution.py:26
  15.1 5.8 %copy-start.2 = (f32[1,3,256,512]{3,2,1,0:T(8,128)S(1)}, f32[1,3,256,512]{3,2,1,0:T(8,128)}, u32[]{:S(2)}) copy-start(f32[1,3,256,512]{3,2,1,0:T(8,128)} %param.15) | copy-start | bytes 4718596
  15.1 5.8 %copy-start.3 = (f32[1,3,256,256]{3,2,1,0:T(8,128)S(1)}, f32[1,3,256,256]{3,2,1,0:T(8,128)}, u32[]{:S(2)}) copy-start(f32[1,3,256,256]{3,2,1,0:T(8,128)} %param.13) | copy-start | bytes 2359300
  15.2 5.8 %copy-start.5 = (f32[1,2,256,256]{3,2,1,0:T(8,128)S(1)}, f32[1,2,256,256]{3,2,1,0:T(8,128)}, u32[]{:S(2)}) copy-start(f32[1,2,256,256]{3,2,1,0:T(8,128)} %param.14) | copy-start | bytes 1572868
  15.7 6.6 %collective-permute-start.7 = (bf16[64,384]{1,0:T(8,128)(2,1)S(1)}, bf16[64,384]{1,0:T(8,128)(2,1)S(1)}, u32[]{:S(2)}, u32[]{:S(2)}) collective-permute-start(bf16[64,384]{1,0:T(8,128)(2,1)S(1)} %get-tuple-element.71), channel_id=1, source_target_pairs={{0,6},{1,7},{2,4},{3,5},{4,2},{5,3},{6,0},{7,1},{8,14},{9,15},{10,... | collective-permute-start | bytes 147464 | tf_op jit(solution)/shard_map/ppermute | solution.py:26
  18.4 4.3 %collective-permute-start.8 = (bf16[64,384]{1,0:T(8,128)(2,1)S(1)}, bf16[64,384]{1,0:T(8,128)(2,1)S(1)}, u32[]{:S(2)}, u32[]{:S(2)}) collective-permute-start(bf16[64,384]{1,0:T(8,128)(2,1)S(1)} %get-tuple-element.72), channel_id=1, source_target_pairs={{0,2},{1,3},{2,0},{3,1},{4,6},{5,7},{6,4},{7,5},{8,10},{9,11},{10,... | collective-permute-start | bytes 147464 | tf_op jit(solution)/shard_map/ppermute | solution.py:26
  18.9 4.1 %collective-permute-start.9 = (bf16[64,384]{1,0:T(8,128)(2,1)S(1)}, bf16[64,384]{1,0:T(8,128)(2,1)S(1)}, u32[]{:S(2)}, u32[]{:S(2)}) collective-permute-start(bf16[64,384]{1,0:T(8,128)(2,1)S(1)} %get-tuple-element.73), channel_id=1, source_target_pairs={{0,4},{1,5},{2,6},{3,7},{4,0},{5,1},{6,2},{7,3},{8,12},{9,13},{10,... | collective-permute-start | bytes 147464 | tf_op jit(solution)/shard_map/ppermute | solution.py:26
  19.2 8.9 %collective-permute-start.11 = (bf16[2,256,512]{2,1,0:T(8,128)(2,1)S(1)}, bf16[2,256,512]{2,1,0:T(8,128)(2,1)S(1)}, u32[]{:S(2)}, u32[]{:S(2)}) collective-permute-start(bf16[2,256,512]{2,1,0:T(8,128)(2,1)S(1)} %get-tuple-element.84.low.refs_4_), channel_id=1, source_target_pairs={{0,1},{1,0},{2,3},{3,2},{4,5},{5,4},{6,7},{7,6},{8,9},{9,8},{10,11... | collective-permute-start | bytes 1572872 | tf_op jit(solution)/shard_map/ppermute | solution.py:26
  19.2 14.5 %collective-permute-start.15 = (bf16[2,256,512]{2,1,0:T(8,128)(2,1)S(1)}, bf16[2,256,512]{2,1,0:T(8,128)(2,1)S(1)}, u32[]{:S(2)}, u32[]{:S(2)}) collective-permute-start(bf16[2,256,512]{2,1,0:T(8,128)(2,1)S(1)} %get-tuple-element.93.high), channel_id=1, source_target_pairs={{0,2},{1,3},{2,0},{3,1},{4,6},{5,7},{6,4},{7,5},{8,10},{9,11},{10,... | collective-permute-start | bytes 1572872 | tf_op jit(solution)/shard_map/ppermute | solution.py:26
  23.0 5.1 %copy-start.1 = (bf16[1,2048,512]{2,1,0:T(8,128)(2,1)S(1)}, bf16[1,2048,512]{2,1,0:T(8,128)(2,1)}, u32[]{:S(2)}) copy-start(bf16[1,2048,512]{2,1,0:T(8,128)(2,1)} %param.9) | copy-start | bytes 6291460
  23.8 6.6 %collective-permute-start.13 = (bf16[1,64,256]{2,1,0:T(8,128)(2,1)S(1)}, bf16[1,64,256]{2,1,0:T(8,128)(2,1)S(1)}, u32[]{:S(2)}, u32[]{:S(2)}) collective-permute-start(bf16[1,64,256]{2,1,0:T(8,128)(2,1)S(1)} %get-tuple-element.91), channel_id=1, source_target_pairs={{0,16},{1,17},{2,18},{3,19},{4,20},{5,21},{6,22},{7,23},{8,24},{9,... | collective-permute-start | bytes 98312 | tf_op jit(solution)/shard_map/ppermute | solution.py:26
  26.5 5.8 %collective-permute-start.14 = (bf16[1,64,256]{2,1,0:T(8,128)(2,1)S(1)}, bf16[1,64,256]{2,1,0:T(8,128)(2,1)S(1)}, u32[]{:S(2)}, u32[]{:S(2)}) collective-permute-start(bf16[1,64,256]{2,1,0:T(8,128)(2,1)S(1)} %get-tuple-element.91), channel_id=1, source_target_pairs={{0,24},{1,25},{2,26},{3,27},{4,28},{5,29},{6,30},{7,31},{8,16},{9,... | collective-permute-start | bytes 98312 | tf_op jit(solution)/shard_map/ppermute | solution.py:26
  27.8 4.6 %collective-permute-start.12 = (bf16[2,64,256]{2,1,0:T(8,128)(2,1)S(1)}, bf16[2,64,256]{2,1,0:T(8,128)(2,1)S(1)}, u32[]{:S(2)}, u32[]{:S(2)}) collective-permute-start(bf16[2,64,256]{2,1,0:T(8,128)(2,1)S(1)} %get-tuple-element.90), channel_id=1, source_target_pairs={{0,8},{1,9},{2,10},{3,11},{4,12},{5,13},{6,14},{7,15},{8,0},{9,1},... | collective-permute-start | bytes 196616 | tf_op jit(solution)/shard_map/ppermute | solution.py:26
  33.9 3.6 %collective-permute-start.19 = (bf16[2,256,512]{2,1,0:T(8,128)(2,1)S(1)}, bf16[2,256,512]{2,1,0:T(8,128)(2,1)S(1)}, u32[]{:S(2)}, u32[]{:S(2)}) collective-permute-start(bf16[2,256,512]{2,1,0:T(8,128)(2,1)S(1)} %add_convert_fusion.refs_0_), channel_id=1, source_target_pairs={{0,1},{1,0},{2,3},{3,2},{4,5},{5,4},{6,7},{7,6},{8,9},{9,8},{10,11... | collective-permute-start | bytes 1572872 | tf_op jit(solution)/shard_map/ppermute | solution.py:26
  34.0 7.4 %collective-permute-start.17 = (bf16[64,384]{1,0:T(8,128)(2,1)S(1)}, bf16[64,384]{1,0:T(8,128)(2,1)S(1)}, u32[]{:S(2)}, u32[]{:S(2)}) collective-permute-start(bf16[64,384]{1,0:T(8,128)(2,1)S(1)} %get-tuple-element.95), channel_id=1, source_target_pairs={{0,4},{1,5},{2,6},{3,7},{4,0},{5,1},{6,2},{7,3},{8,12},{9,13},{10,... | collective-permute-start | bytes 147464 | tf_op jit(solution)/shard_map/ppermute | solution.py:26
  35.6 5.8 %collective-permute-start.18 = (bf16[64,384]{1,0:T(8,128)(2,1)S(1)}, bf16[64,384]{1,0:T(8,128)(2,1)S(1)}, u32[]{:S(2)}, u32[]{:S(2)}) collective-permute-start(bf16[64,384]{1,0:T(8,128)(2,1)S(1)} %get-tuple-element.95), channel_id=1, source_target_pairs={{0,6},{1,7},{2,4},{3,5},{4,2},{5,3},{6,0},{7,1},{8,14},{9,15},{10,... | collective-permute-start | bytes 147464 | tf_op jit(solution)/shard_map/ppermute | solution.py:26
  37.1 4.3 %collective-permute-start.16 = (bf16[64,384]{1,0:T(8,128)(2,1)S(1)}, bf16[64,384]{1,0:T(8,128)(2,1)S(1)}, u32[]{:S(2)}, u32[]{:S(2)}) collective-permute-start(bf16[64,384]{1,0:T(8,128)(2,1)S(1)} %get-tuple-element.106.refs_0_), channel_id=1, source_target_pairs={{0,2},{1,3},{2,0},{3,1},{4,6},{5,7},{6,4},{7,5},{8,10},{9,11},{10,... | collective-permute-start | bytes 147464 | tf_op jit(solution)/shard_map/ppermute | solution.py:26
  37.5 4.9 %collective-permute-start.20 = (bf16[3,64,256]{2,1,0:T(8,128)(2,1)S(1)}, bf16[3,64,256]{2,1,0:T(8,128)(2,1)S(1)}, u32[]{:S(2)}, u32[]{:S(2)}) collective-permute-start(bf16[3,64,256]{2,1,0:T(8,128)(2,1)S(1)} %get-tuple-element.104), channel_id=1, source_target_pairs={{0,4},{1,5},{2,6},{3,7},{4,0},{5,1},{6,2},{7,3},{8,12},{9,13},{10,... | collective-permute-start | bytes 294920 | tf_op jit(solution)/shard_map/ppermute | solution.py:26
  41.3 2.0 %collective-permute-start.21 = (bf16[64,384]{1,0:T(8,128)(2,1)S(1)}, bf16[64,384]{1,0:T(8,128)(2,1)S(1)}, u32[]{:S(2)}, u32[]{:S(2)}) collective-permute-start(bf16[64,384]{1,0:T(8,128)(2,1)S(1)} %get-tuple-element.106.refs_0_), channel_id=1, source_target_pairs={{0,1},{1,0},{2,3},{3,2},{4,5},{5,4},{6,7},{7,6},{8,9},{9,8},{10,11... | collective-permute-start | bytes 147464 | tf_op jit(solution)/shard_map/ppermute | solution.py:26
  41.4 2.0 %collective-permute-start.22 = (bf16[64,384]{1,0:T(8,128)(2,1)S(1)}, bf16[64,384]{1,0:T(8,128)(2,1)S(1)}, u32[]{:S(2)}, u32[]{:S(2)}) collective-permute-start(bf16[64,384]{1,0:T(8,128)(2,1)S(1)} %collective-permute-done.16.refs_1_), channel_id=1, source_target_pairs={{0,1},{1,0},{2,3},{3,2},{4,5},{5,4},{6,7},{7,6},{8,9},{9,8},{10,11... | collective-permute-start | bytes 147464 | tf_op jit(solution)/shard_map/ppermute | solution.py:26
  41.9 1.5 %collective-permute-start.23 = (bf16[64,384]{1,0:T(8,128)(2,1)S(1)}, bf16[64,384]{1,0:T(8,128)(2,1)S(1)}, u32[]{:S(2)}, u32[]{:S(2)}) collective-permute-start(bf16[64,384]{1,0:T(8,128)(2,1)S(1)} %collective-permute-done.17.refs_2_), channel_id=1, source_target_pairs={{0,1},{1,0},{2,3},{3,2},{4,5},{5,4},{6,7},{7,6},{8,9},{9,8},{10,11... | collective-permute-start | bytes 147464 | tf_op jit(solution)/shard_map/ppermute | solution.py:26
  41.9 1.4 %collective-permute-start.24 = (bf16[64,384]{1,0:T(8,128)(2,1)S(1)}, bf16[64,384]{1,0:T(8,128)(2,1)S(1)}, u32[]{:S(2)}, u32[]{:S(2)}) collective-permute-start(bf16[64,384]{1,0:T(8,128)(2,1)S(1)} %collective-permute-done.18.refs_3_), channel_id=1, source_target_pairs={{0,1},{1,0},{2,3},{3,2},{4,5},{5,4},{6,7},{7,6},{8,9},{9,8},{10,11... | collective-permute-start | bytes 147464 | tf_op jit(solution)/shard_map/ppermute | solution.py:26
  (2 other events, 2.4 us)

commit v7 on v5

--- a/solution.py
+++ b/solution.py
@@ -338,7 +338,7 @@
         [low, high, early] + [held[mask] for mask in far],
         [pltpu.VMEM(partial_shape, F32)],
     )
-    high, low, own, inverses = lax.optimization_barrier((high, low, own, sep_inverse[0]))
+    high, low, own, inverses, spots = lax.optimization_barrier((high, low, own, sep_inverse[0], spots))
     cross = moved(cross, 1, half)
     same, other = moved(same, 0, half), moved(other, 1, 0)
 
@@ -410,7 +410,7 @@
         [
             pltpu.VMEM((sources, levels * touched), BF16),
             pltpu.VMEM((rows, sources), BF16),
-            pltpu.SemaphoreType.DMA((half,)),
+            pltpu.SemaphoreType.DMA((groups,)),
         ],
         space=pl.ANY,
     )[0]

time: 44.8 us -> 44.8 us (level)
  no operation moved by 1% of the time
where the time goes in v7:
time: 44.8 us; the launch traced here: 44.6 us
  starting transfers between devices  21.4 us (48%)
  Pallas kernels  10.9 us (24%)
  waiting for transfers between devices  7.95 us (18%)
  local copies, waits for them, and re-layouts  2.67 us (6%)
  between operations  0.86 us (2%)
  other arithmetic  0.85 us (2%)
    ppermute x25, starting transfers between devices, moved(): return lax.ppermute(block, AXES, route)  21.4 us
    pallas_call x11, Pallas kernels, call(): pl.pallas_call(body, out_shape=outs, in_specs=specs, out_specs=[pl.BlockS...  10.9 us
    ppermute x25, waiting for transfers between devices, moved(): return lax.ppermute(block, AXES, route)  7.95 us
    unnamed x18, local copies, waits for them, and re-layouts  2.67 us
  transfers between devices with their start and end apart: 25, of which 6 were waited for; matrix products, arithmetic and copies ran while one was open for 2% of the time, Pallas kernels for 20%

profile of v7, /device:TPU:0, one launch (start us, length us, event | category | flops | bytes accessed | tf_op | source)
XLA Modules:
  0.0 44.6 jit_solution(17235765874804320384)
XLA Ops:
  0.6 0.5 %collective-permute-start.1 = (bf16[384,512]{1,0:T(8,128)(2,1)}, bf16[384,512]{1,0:T(8,128)(2,1)S(1)}, u32[]{:S(2)}, u32[]{:S(2)}) collective-permute-start(bf16[384,512]{1,0:T(8,128)(2,1)} %bitcast.16), channel_id=1, source_target_pairs={{0,1},{1,0},{2,3},{3,2},{4,5},{5,4},{6,7},{7,6},{8,9},{9,8},{10,11... | collective-permute-start | bytes 1179656 | tf_op jit(solution)/shard_map/ppermute | solution.py:26
  1.1 2.6 %collective-permute-start = (bf16[384,512]{1,0:T(8,128)(2,1)}, bf16[384,512]{1,0:T(8,128)(2,1)S(1)}, u32[]{:S(2)}, u32[]{:S(2)}) collective-permute-start(bf16[384,512]{1,0:T(8,128)(2,1)} %bitcast.17), channel_id=1, source_target_pairs={{0,2},{1,3},{2,0},{3,1},{4,6},{5,7},{6,4},{7,5},{8,10},{9,11},{10,... | collective-permute-start | bytes 1179656 | tf_op jit(solution)/shard_map/ppermute | solution.py:26
  3.7 0.7 %pad_add_fusion.1 = s32[2,3]{1,0:T(2,128)S(1)} fusion(s32[1,3]{1,0:T(1,128)} %param.11, s32[1,3]{1,0:T(1,128)} %param.12), kind=kLoop, calls=%fused_computation.2 | loop fusion | flops 6 | bytes 48 | tf_op jit(solution)/shard_map/concatenate | solution.py:318
  4.4 1.5 %collective-permute-start.7 = (s32[2,3]{1,0:T(2,128)S(1)}, s32[2,3]{1,0:T(2,128)S(1)}, u32[]{:S(2)}, u32[]{:S(2)}) collective-permute-start(s32[2,3]{1,0:T(2,128)S(1)} %pad_add_fusion.1), channel_id=1, source_target_pairs={{0,4},{1,5},{2,6},{3,7},{4,0},{5,1},{6,2},{7,3},{8,12},{9,13},{10,... | collective-permute-start | bytes 80 | tf_op jit(solution)/shard_map/ppermute | solution.py:26
  5.9 1.6 %copy-done = bf16[1,2048,512]{2,1,0:T(8,128)(2,1)S(1)} copy-done((bf16[1,2048,512]{2,1,0:T(8,128)(2,1)S(1)}, bf16[1,2048,512]{2,1,0:T(8,128)(2,1)}, u32[]{:S(2)}) %copy-start) | copy-done | bytes 2097176
  7.5 1.0 %copy-done.4 = bf16[1,512,512]{2,1,0:T(8,128)(2,1)S(1)} copy-done((bf16[1,512,512]{2,1,0:T(8,128)(2,1)S(1)}, bf16[1,512,512]{2,1,0:T(8,128)(2,1)}, u32[]{:S(2)}) %copy-start.4) | copy-done | bytes 524312
  8.6 1.3 %leaf_products.1 = (f32[4,256,512]{2,1,0:T(8,128)S(1)}, bf16[256,512]{1,0:T(8,128)(2,1)S(1)}, bf16[256,512]{1,0:T(8,128)(2,1)S(1)}, bf16[256,512]{1,0:T(8,128)(2,1)S(1)}, bf16[256,512]{1,0:T(8,128)(2,1)S(1)}) custom-call(bf16[2048,512]{1,0:T(8,128)(2,1)S(1)} %bitcast.8, bf16[512,512]{1,0:T(8,128)(2,1)S(1)} %bitcast.14), custom_call_target="tpu_custom_call" | custom-call | flops 5000000000 | tf_op jit(solution)/shard_map/leaf_products/pallas_call | solution.py:39
  10.5 3.1 %collective-permute-done.refs_0_.refs_2_ = bf16[384,512]{1,0:T(8,128)(2,1)S(1)} collective-permute-done((bf16[384,512]{1,0:T(8,128)(2,1)}, bf16[384,512]{1,0:T(8,128)(2,1)S(1)}, u32[]{:S(2)}, u32[]{:S(2)}) %collective-permute-start) | collective-permute-done | bytes 393248 | tf_op jit(solution)/shard_map/ppermute | solution.py:26
  13.7 0.6 %collective-permute-start.6 = (bf16[384,512]{1,0:T(8,128)(2,1)S(1)}, bf16[384,512]{1,0:T(8,128)(2,1)S(1)}, u32[]{:S(2)}, u32[]{:S(2)}) collective-permute-start(bf16[384,512]{1,0:T(8,128)(2,1)S(1)} %collective-permute-done.refs_0_.refs_2_), channel_id=1, source_target_pairs={{0,1},{1,0},{2,3},{3,2},{4,5},{5,4},{6,7},{7,6},{8,9},{9,8},{10,11... | collective-permute-start | bytes 1179656 | tf_op jit(solution)/shard_map/ppermute | solution.py:26
  14.3 0.9 %collective-permute-done.5.refs_5_ = bf16[256,512]{1,0:T(8,128)(2,1)S(1)} collective-permute-done((bf16[256,512]{1,0:T(8,128)(2,1)S(1)}, bf16[256,512]{1,0:T(8,128)(2,1)S(1)}, u32[]{:S(2)}, u32[]{:S(2)}) %collective-permute-start.5) | collective-permute-done | bytes 262176 | tf_op jit(solution)/shard_map/ppermute | solution.py:26
  15.2 0.6 %own_partials.1 = (bf16[2,256,512]{2,1,0:T(8,128)(2,1)S(1)}, bf16[2,256,512]{2,1,0:T(8,128)(2,1)S(1)}, f32[2,256,512]{2,1,0:T(8,128)S(1)}, f32[256,384]{1,0:T(8,128)S(1)}) custom-call(f32[4,256,512]{2,1,0:T(8,128)S(1)} %get-tuple-element.55.keep, bf16[384,512]{1,0:T(8,128)(2,1)S(1)} %bitcast.18, bf16[384,512]{1,0:T(8,128)(2,1)S(1)} %collective-permute-done.1.refs_1_, ...), custom_call_target="tpu_custom_call" | custom-call | flops 5000000000 | tf_op jit(solution)/shard_map/own_partials/pallas_call | solution.py:39
  16.3 2.8 %collective-permute-start.9 = (bf16[64,384]{1,0:T(8,128)(2,1)S(1)}, bf16[64,384]{1,0:T(8,128)(2,1)S(1)}, u32[]{:S(2)}, u32[]{:S(2)}) collective-permute-start(bf16[64,384]{1,0:T(8,128)(2,1)S(1)} %get-tuple-element.67), channel_id=1, source_target_pairs={{0,6},{1,7},{2,4},{3,5},{4,2},{5,3},{6,0},{7,1},{8,14},{9,15},{10,... | collective-permute-start | bytes 147464 | tf_op jit(solution)/shard_map/ppermute | solution.py:26
  19.1 0.5 %collective-permute-start.10 = (bf16[64,384]{1,0:T(8,128)(2,1)S(1)}, bf16[64,384]{1,0:T(8,128)(2,1)S(1)}, u32[]{:S(2)}, u32[]{:S(2)}) collective-permute-start(bf16[64,384]{1,0:T(8,128)(2,1)S(1)} %get-tuple-element.68), channel_id=1, source_target_pairs={{0,2},{1,3},{2,0},{3,1},{4,6},{5,7},{6,4},{7,5},{8,10},{9,11},{10,... | collective-permute-start | bytes 147464 | tf_op jit(solution)/shard_map/ppermute | solution.py:26
  19.9 1.8 %collective-permute-start.8 = (bf16[2,256,512]{2,1,0:T(8,128)(2,1)S(1)}, bf16[2,256,512]{2,1,0:T(8,128)(2,1)S(1)}, u32[]{:S(2)}, u32[]{:S(2)}) collective-permute-start(bf16[2,256,512]{2,1,0:T(8,128)(2,1)S(1)} %get-tuple-element.65.high), channel_id=1, source_target_pairs={{0,2},{1,3},{2,0},{3,1},{4,6},{5,7},{6,4},{7,5},{8,10},{9,11},{10,... | collective-permute-start | bytes 1572872 | tf_op jit(solution)/shard_map/ppermute | solution.py:26
  21.7 1.3 %prepare.1 = (bf16[2,256,256]{2,1,0:T(8,128)(2,1)S(1)}, bf16[2,256,256]{2,1,0:T(8,128)(2,1)S(1)}, f32[3,64,256]{2,1,0:T(8,128)S(1)}, bf16[3,256,256]{2,1,0:T(8,128)(2,1)S(1)}) custom-call(s32[4,3]{1,0:T(4,128)S(1)} %pad_add_fusion.spots, f32[3,256,256]{2,1,0:T(8,128)S(1)} %bitcast.12, f32[2,256,256]{2,1,0:T(8,128)S(1)} %bitcast.15, f32[3,256,512]{2,1,0:T(8,128)S(1)} %bitcast.11), custom_call_target="tpu_custom_call" | custom-call | flops 5000000000 | tf_op jit(solution)/shard_map/prepare/pallas_call | solution.py:39
  23.0 0.7 %collective-permute-done.10.same = bf16[64,384]{1,0:T(8,128)(2,1)S(1)} collective-permute-done((bf16[64,384]{1,0:T(8,128)(2,1)S(1)}, bf16[64,384]{1,0:T(8,128)(2,1)S(1)}, u32[]{:S(2)}, u32[]{:S(2)}) %collective-permute-start.10) | collective-permute-done | bytes 49184 | tf_op jit(solution)/shard_map/ppermute | solution.py:26
  23.7 0.8 %upward.1 = (f32[3,64,256]{2,1,0:T(8,128)S(1)}, bf16[2,64,256]{2,1,0:T(8,128)(2,1)S(1)}, bf16[1,64,256]{2,1,0:T(8,128)(2,1)S(1)}) custom-call(f32[64,384]{1,0:T(8,128)S(1)} %get-tuple-element.66.own, bf16[64,384]{1,0:T(8,128)(2,1)S(1)} %collective-permute-done.9.cross, bf16[64,384]{1,0:T(8,128)(2,1)S(1)} %collective-permute-done.10.same, ...), custom_call_target="tpu_custom_call" | custom-call | flops 5000000000 | tf_op jit(solution)/shard_map/upward/pallas_call | solution.py:39
  24.6 3.7 %collective-permute-start.15 = (bf16[1,64,256]{2,1,0:T(8,128)(2,1)S(1)}, bf16[1,64,256]{2,1,0:T(8,128)(2,1)S(1)}, u32[]{:S(2)}, u32[]{:S(2)}) collective-permute-start(bf16[1,64,256]{2,1,0:T(8,128)(2,1)S(1)} %get-tuple-element.86), channel_id=1, source_target_pairs={{0,24},{1,25},{2,26},{3,27},{4,28},{5,29},{6,30},{7,31},{8,16},{9,... | collective-permute-start | bytes 98312 | tf_op jit(solution)/shard_map/ppermute | solution.py:26
  28.2 0.8 %collective-permute-start.13 = (bf16[2,64,256]{2,1,0:T(8,128)(2,1)S(1)}, bf16[2,64,256]{2,1,0:T(8,128)(2,1)S(1)}, u32[]{:S(2)}, u32[]{:S(2)}) collective-permute-start(bf16[2,64,256]{2,1,0:T(8,128)(2,1)S(1)} %get-tuple-element.85), channel_id=1, source_target_pairs={{0,8},{1,9},{2,10},{3,11},{4,12},{5,13},{6,14},{7,15},{8,0},{9,1},... | collective-permute-start | bytes 196616 | tf_op jit(solution)/shard_map/ppermute | solution.py:26
  29.0 1.5 %lower_transposed.1 = (f32[512,512]{1,0:T(8,128)S(1)}, bf16[512,384]{1,0:T(8,128)(2,1)S(1)}) custom-call(bf16[2048,512]{1,0:T(8,128)(2,1)S(1)} %bitcast.9, bf16[384,512]{1,0:T(8,128)(2,1)S(1)} %bitcast.19, bf16[384,512]{1,0:T(8,128)(2,1)S(1)} %collective-permute-done.1.refs_1_, bf16[384,512]{1,0:T(8,128)(2,1)S(1)} %collective-permute-done.refs_0_.refs_2_, ...), custom_call_target="tpu_custom_call" | custom-call | flops 5000000000 | tf_op jit(solution)/shard_map/lower_transposed/pallas_call | solution.py:39
  30.5 0.9 %squares.1 = (bf16[3,256,256]{2,1,0:T(8,128)(2,1)S(1)}, bf16[3,256,256]{2,1,0:T(8,128)(2,1)S(1)}) custom-call(f32[3,256,256]{2,1,0:T(8,128)S(1)} %bitcast.13), custom_call_target="tpu_custom_call" | custom-call | flops 5000000000 | tf_op jit(solution)/shard_map/squares/pallas_call | solution.py:39
  31.4 1.6 %collective-permute-done.14.refs_1_ = bf16[1,64,256]{2,1,0:T(8,128)(2,1)S(1)} collective-permute-done((bf16[1,64,256]{2,1,0:T(8,128)(2,1)S(1)}, bf16[1,64,256]{2,1,0:T(8,128)(2,1)S(1)}, u32[]{:S(2)}, u32[]{:S(2)}) %collective-permute-start.14) | collective-permute-done | bytes 32800 | tf_op jit(solution)/shard_map/ppermute | solution.py:26
  33.0 0.8 %downward.1 = (f32[3,64,256]{2,1,0:T(8,128)S(1)}, bf16[64,384]{1,0:T(8,128)(2,1)S(1)}, bf16[64,384]{1,0:T(8,128)(2,1)S(1)}, bf16[3,64,256]{2,1,0:T(8,128)(2,1)S(1)}) custom-call(f32[3,64,256]{2,1,0:T(8,128)S(1)} %get-tuple-element.77.kept, f32[3,64,256]{2,1,0:T(8,128)S(1)} %get-tuple-element.72.right, bf16[3,256,256]{2,1,0:T(8,128)(2,1)S(1)} %get-tuple-element.83.q_high, ...), custom_call_target="tpu_custom_call" | custom-call | flops 5000000000 | tf_op jit(solution)/shard_map/downward/pallas_call | solution.py:39
  34.1 1.9 %collective-permute-start.18 = (bf16[64,384]{1,0:T(8,128)(2,1)S(1)}, bf16[64,384]{1,0:T(8,128)(2,1)S(1)}, u32[]{:S(2)}, u32[]{:S(2)}) collective-permute-start(bf16[64,384]{1,0:T(8,128)(2,1)S(1)} %get-tuple-element.89), channel_id=1, source_target_pairs={{0,6},{1,7},{2,4},{3,5},{4,2},{5,3},{6,0},{7,1},{8,14},{9,15},{10,... | collective-permute-start | bytes 147464 | tf_op jit(solution)/shard_map/ppermute | solution.py:26
  36.0 1.1 %collective-permute-start.17 = (bf16[64,384]{1,0:T(8,128)(2,1)S(1)}, bf16[64,384]{1,0:T(8,128)(2,1)S(1)}, u32[]{:S(2)}, u32[]{:S(2)}) collective-permute-start(bf16[64,384]{1,0:T(8,128)(2,1)S(1)} %get-tuple-element.89), channel_id=1, source_target_pairs={{0,4},{1,5},{2,6},{3,7},{4,0},{5,1},{6,2},{7,3},{8,12},{9,13},{10,... | collective-permute-start | bytes 147464 | tf_op jit(solution)/shard_map/ppermute | solution.py:26
  37.2 0.5 %collective-permute-start.16 = (bf16[64,384]{1,0:T(8,128)(2,1)S(1)}, bf16[64,384]{1,0:T(8,128)(2,1)S(1)}, u32[]{:S(2)}, u32[]{:S(2)}) collective-permute-start(bf16[64,384]{1,0:T(8,128)(2,1)S(1)} %get-tuple-element.100.refs_0_), channel_id=1, source_target_pairs={{0,2},{1,3},{2,0},{3,1},{4,6},{5,7},{6,4},{7,5},{8,10},{9,11},{10,... | collective-permute-start | bytes 147464 | tf_op jit(solution)/shard_map/ppermute | solution.py:26
  37.7 1.2 %collective-permute-start.20 = (bf16[3,64,256]{2,1,0:T(8,128)(2,1)S(1)}, bf16[3,64,256]{2,1,0:T(8,128)(2,1)S(1)}, u32[]{:S(2)}, u32[]{:S(2)}) collective-permute-start(bf16[3,64,256]{2,1,0:T(8,128)(2,1)S(1)} %get-tuple-element.98), channel_id=1, source_target_pairs={{0,4},{1,5},{2,6},{3,7},{4,0},{5,1},{6,2},{7,3},{8,12},{9,13},{10,... | collective-permute-start | bytes 294920 | tf_op jit(solution)/shard_map/ppermute | solution.py:26
  38.9 0.9 %upper_transposed.1.base = f32[512,512]{1,0:T(8,128)S(1)} custom-call(bf16[2048,512]{1,0:T(8,128)(2,1)S(1)} %bitcast.10, f32[512,512]{1,0:T(8,128)S(1)} %get-tuple-element.90.lower, bf16[2,256,512]{2,1,0:T(8,128)(2,1)S(1)} %add_convert_fusion.refs_0_, bf16[2,256,512]{2,1,0:T(8,128)(2,1)S(1)} %collective-permute-done.19.refs_1_), custom_call_target="tpu_custom_call" | custom-call | flops 5000000000 | tf_op jit(solution)/shard_map/upper_transposed/pallas_call | solution.py:39
  39.8 1.4 %collective-permute-done.16.refs_1_ = bf16[64,384]{1,0:T(8,128)(2,1)S(1)} collective-permute-done((bf16[64,384]{1,0:T(8,128)(2,1)S(1)}, bf16[64,384]{1,0:T(8,128)(2,1)S(1)}, u32[]{:S(2)}, u32[]{:S(2)}) %collective-permute-start.16) | collective-permute-done | bytes 49184 | tf_op jit(solution)/shard_map/ppermute | solution.py:26
  41.3 0.5 %collective-permute-start.22 = (bf16[64,384]{1,0:T(8,128)(2,1)S(1)}, bf16[64,384]{1,0:T(8,128)(2,1)S(1)}, u32[]{:S(2)}, u32[]{:S(2)}) collective-permute-start(bf16[64,384]{1,0:T(8,128)(2,1)S(1)} %collective-permute-done.16.refs_1_), channel_id=1, source_target_pairs={{0,1},{1,0},{2,3},{3,2},{4,5},{5,4},{6,7},{7,6},{8,9},{9,8},{10,11... | collective-permute-start | bytes 147464 | tf_op jit(solution)/shard_map/ppermute | solution.py:26
  42.4 0.9 %assemble.1 = f32[3,256,128]{2,1,0:T(8,128)} custom-call(f32[3,64,256]{2,1,0:T(8,128)S(1)} %get-tuple-element.104.mine, bf16[3,64,256]{2,1,0:T(8,128)(2,1)S(1)} %collective-permute-done.20.passed), custom_call_target="tpu_custom_call" | custom-call | flops 5000000000 | tf_op jit(solution)/shard_map/assemble/pallas_call | solution.py:39
  43.3 1.3 %finish.1 = bf16[512,512]{1,0:T(8,128)(2,1)} custom-call(f32[512,512]{1,0:T(8,128)S(1)} %upper_transposed.1.base, bf16[512,384]{1,0:T(8,128)(2,1)S(1)} %get-tuple-element.99.weight_turned, bf16[64,384]{1,0:T(8,128)(2,1)S(1)} %get-tuple-element.100.refs_0_, bf16[64,384]{1,0:T(8,128)(2,1)S(1)} %collective-permute-done.16.refs_1_, ...), custom_call_target="tpu_custom_call" | custom-call | flops 5000000000 | tf_op jit(solution)/shard_map/finish/pallas_call | solution.py:39
  (50 shorter events, 2.4 us)
Async XLA Ops:
  0.6 14.6 %collective-permute-start.1 = (bf16[384,512]{1,0:T(8,128)(2,1)}, bf16[384,512]{1,0:T(8,128)(2,1)S(1)}, u32[]{:S(2)}, u32[]{:S(2)}) collective-permute-start(bf16[384,512]{1,0:T(8,128)(2,1)} %bitcast.16), channel_id=1, source_target_pairs={{0,1},{1,0},{2,3},{3,2},{4,5},{5,4},{6,7},{7,6},{8,9},{9,8},{10,11... | collective-permute-start | bytes 1179656 | tf_op jit(solution)/shard_map/ppermute | solution.py:26
  1.1 12.5 %collective-permute-start = (bf16[384,512]{1,0:T(8,128)(2,1)}, bf16[384,512]{1,0:T(8,128)(2,1)S(1)}, u32[]{:S(2)}, u32[]{:S(2)}) collective-permute-start(bf16[384,512]{1,0:T(8,128)(2,1)} %bitcast.17), channel_id=1, source_target_pairs={{0,2},{1,3},{2,0},{3,1},{4,6},{5,7},{6,4},{7,5},{8,10},{9,11},{10,... | collective-permute-start | bytes 1179656 | tf_op jit(solution)/shard_map/ppermute | solution.py:26
  4.4 6.0 %collective-permute-start.7 = (s32[2,3]{1,0:T(2,128)S(1)}, s32[2,3]{1,0:T(2,128)S(1)}, u32[]{:S(2)}, u32[]{:S(2)}) collective-permute-start(s32[2,3]{1,0:T(2,128)S(1)} %pad_add_fusion.1), channel_id=1, source_target_pairs={{0,4},{1,5},{2,6},{3,7},{4,0},{5,1},{6,2},{7,3},{8,12},{9,13},{10,... | collective-permute-start | bytes 80 | tf_op jit(solution)/shard_map/ppermute | solution.py:26
  8.5 5.1 %copy-start.7 = (s32[1,3]{1,0:T(1,128)S(1)}, s32[1,3]{1,0:T(1,128)}, u32[]{:S(2)}) copy-start(s32[1,3]{1,0:T(1,128)} %param.11) | copy-start | bytes 40
  8.5 5.1 %copy-start.8 = (s32[1,3]{1,0:T(1,128)S(1)}, s32[1,3]{1,0:T(1,128)}, u32[]{:S(2)}) copy-start(s32[1,3]{1,0:T(1,128)} %param.12) | copy-start | bytes 40
  8.6 6.6 %copy-start.6 = (bf16[1,3,128,512]{3,2,1,0:T(8,128)(2,1)S(1)}, bf16[1,3,128,512]{3,2,1,0:T(8,128)(2,1)}, u32[]{:S(2)}) copy-start(bf16[1,3,128,512]{3,2,1,0:T(8,128)(2,1)} %param.10) | copy-start | bytes 1179652
  9.9 3.8 %collective-permute-start.2 = (bf16[256,512]{1,0:T(8,128)(2,1)S(1)}, bf16[256,512]{1,0:T(8,128)(2,1)S(1)}, u32[]{:S(2)}, u32[]{:S(2)}) collective-permute-start(bf16[256,512]{1,0:T(8,128)(2,1)S(1)} %get-tuple-element.56), channel_id=1, source_target_pairs={{0,1},{1,0},{2,3},{3,2},{4,5},{5,4},{6,7},{7,6},{8,9},{9,8},{10,11... | collective-permute-start | bytes 786440 | tf_op jit(solution)/shard_map/ppermute | solution.py:26
  10.0 4.3 %collective-permute-start.3 = (bf16[256,512]{1,0:T(8,128)(2,1)S(1)}, bf16[256,512]{1,0:T(8,128)(2,1)S(1)}, u32[]{:S(2)}, u32[]{:S(2)}) collective-permute-start(bf16[256,512]{1,0:T(8,128)(2,1)S(1)} %get-tuple-element.57), channel_id=1, source_target_pairs={{0,1},{1,0},{2,3},{3,2},{4,5},{5,4},{6,7},{7,6},{8,9},{9,8},{10,11... | collective-permute-start | bytes 786440 | tf_op jit(solution)/shard_map/ppermute | solution.py:26
  10.5 3.8 %collective-permute-start.4 = (bf16[256,512]{1,0:T(8,128)(2,1)S(1)}, bf16[256,512]{1,0:T(8,128)(2,1)S(1)}, u32[]{:S(2)}, u32[]{:S(2)}) collective-permute-start(bf16[256,512]{1,0:T(8,128)(2,1)S(1)} %get-tuple-element.58), channel_id=1, source_target_pairs={{0,1},{1,0},{2,3},{3,2},{4,5},{5,4},{6,7},{7,6},{8,9},{9,8},{10,11... | collective-permute-start | bytes 786440 | tf_op jit(solution)/shard_map/ppermute | solution.py:26
  13.7 1.5 %collective-permute-start.5 = (bf16[256,512]{1,0:T(8,128)(2,1)S(1)}, bf16[256,512]{1,0:T(8,128)(2,1)S(1)}, u32[]{:S(2)}, u32[]{:S(2)}) collective-permute-start(bf16[256,512]{1,0:T(8,128)(2,1)S(1)} %get-tuple-element.59), channel_id=1, source_target_pairs={{0,1},{1,0},{2,3},{3,2},{4,5},{5,4},{6,7},{7,6},{8,9},{9,8},{10,11... | collective-permute-start | bytes 786440 | tf_op jit(solution)/shard_map/ppermute | solution.py:26
  13.7 2.1 %collective-permute-start.6 = (bf16[384,512]{1,0:T(8,128)(2,1)S(1)}, bf16[384,512]{1,0:T(8,128)(2,1)S(1)}, u32[]{:S(2)}, u32[]{:S(2)}) collective-permute-start(bf16[384,512]{1,0:T(8,128)(2,1)S(1)} %collective-permute-done.refs_0_.refs_2_), channel_id=1, source_target_pairs={{0,1},{1,0},{2,3},{3,2},{4,5},{5,4},{6,7},{7,6},{8,9},{9,8},{10,11... | collective-permute-start | bytes 1179656 | tf_op jit(solution)/shard_map/ppermute | solution.py:26
  15.8 5.8 %copy-start.2 = (f32[1,3,256,512]{3,2,1,0:T(8,128)S(1)}, f32[1,3,256,512]{3,2,1,0:T(8,128)}, u32[]{:S(2)}) copy-start(f32[1,3,256,512]{3,2,1,0:T(8,128)} %param.15) | copy-start | bytes 4718596
  15.8 5.8 %copy-start.3 = (f32[1,3,256,256]{3,2,1,0:T(8,128)S(1)}, f32[1,3,256,256]{3,2,1,0:T(8,128)}, u32[]{:S(2)}) copy-start(f32[1,3,256,256]{3,2,1,0:T(8,128)} %param.13) | copy-start | bytes 2359300
  15.8 5.8 %copy-start.5 = (f32[1,2,256,256]{3,2,1,0:T(8,128)S(1)}, f32[1,2,256,256]{3,2,1,0:T(8,128)}, u32[]{:S(2)}) copy-start(f32[1,2,256,256]{3,2,1,0:T(8,128)} %param.14) | copy-start | bytes 1572868
  16.3 6.6 %collective-permute-start.9 = (bf16[64,384]{1,0:T(8,128)(2,1)S(1)}, bf16[64,384]{1,0:T(8,128)(2,1)S(1)}, u32[]{:S(2)}, u32[]{:S(2)}) collective-permute-start(bf16[64,384]{1,0:T(8,128)(2,1)S(1)} %get-tuple-element.67), channel_id=1, source_target_pairs={{0,6},{1,7},{2,4},{3,5},{4,2},{5,3},{6,0},{7,1},{8,14},{9,15},{10,... | collective-permute-start | bytes 147464 | tf_op jit(solution)/shard_map/ppermute | solution.py:26
  19.1 4.6 %collective-permute-start.10 = (bf16[64,384]{1,0:T(8,128)(2,1)S(1)}, bf16[64,384]{1,0:T(8,128)(2,1)S(1)}, u32[]{:S(2)}, u32[]{:S(2)}) collective-permute-start(bf16[64,384]{1,0:T(8,128)(2,1)S(1)} %get-tuple-element.68), channel_id=1, source_target_pairs={{0,2},{1,3},{2,0},{3,1},{4,6},{5,7},{6,4},{7,5},{8,10},{9,11},{10,... | collective-permute-start | bytes 147464 | tf_op jit(solution)/shard_map/ppermute | solution.py:26
  19.6 4.1 %collective-permute-start.11 = (bf16[64,384]{1,0:T(8,128)(2,1)S(1)}, bf16[64,384]{1,0:T(8,128)(2,1)S(1)}, u32[]{:S(2)}, u32[]{:S(2)}) collective-permute-start(bf16[64,384]{1,0:T(8,128)(2,1)S(1)} %get-tuple-element.69), channel_id=1, source_target_pairs={{0,4},{1,5},{2,6},{3,7},{4,0},{5,1},{6,2},{7,3},{8,12},{9,13},{10,... | collective-permute-start | bytes 147464 | tf_op jit(solution)/shard_map/ppermute | solution.py:26
  19.9 14.0 %collective-permute-start.8 = (bf16[2,256,512]{2,1,0:T(8,128)(2,1)S(1)}, bf16[2,256,512]{2,1,0:T(8,128)(2,1)S(1)}, u32[]{:S(2)}, u32[]{:S(2)}) collective-permute-start(bf16[2,256,512]{2,1,0:T(8,128)(2,1)S(1)} %get-tuple-element.65.high), channel_id=1, source_target_pairs={{0,2},{1,3},{2,0},{3,1},{4,6},{5,7},{6,4},{7,5},{8,10},{9,11},{10,... | collective-permute-start | bytes 1572872 | tf_op jit(solution)/shard_map/ppermute | solution.py:26
  21.6 7.4 %collective-permute-start.12 = (bf16[2,256,512]{2,1,0:T(8,128)(2,1)S(1)}, bf16[2,256,512]{2,1,0:T(8,128)(2,1)S(1)}, u32[]{:S(2)}, u32[]{:S(2)}) collective-permute-start(bf16[2,256,512]{2,1,0:T(8,128)(2,1)S(1)} %get-tuple-element.79.low.refs_4_), channel_id=1, source_target_pairs={{0,1},{1,0},{2,3},{3,2},{4,5},{5,4},{6,7},{7,6},{8,9},{9,8},{10,11... | collective-permute-start | bytes 1572872 | tf_op jit(solution)/shard_map/ppermute | solution.py:26
  23.7 5.3 %copy-start.1 = (bf16[1,2048,512]{2,1,0:T(8,128)(2,1)S(1)}, bf16[1,2048,512]{2,1,0:T(8,128)(2,1)}, u32[]{:S(2)}) copy-start(bf16[1,2048,512]{2,1,0:T(8,128)(2,1)} %param.9) | copy-start | bytes 6291460
  24.6 6.9 %collective-permute-start.15 = (bf16[1,64,256]{2,1,0:T(8,128)(2,1)S(1)}, bf16[1,64,256]{2,1,0:T(8,128)(2,1)S(1)}, u32[]{:S(2)}, u32[]{:S(2)}) collective-permute-start(bf16[1,64,256]{2,1,0:T(8,128)(2,1)S(1)} %get-tuple-element.86), channel_id=1, source_target_pairs={{0,24},{1,25},{2,26},{3,27},{4,28},{5,29},{6,30},{7,31},{8,16},{9,... | collective-permute-start | bytes 98312 | tf_op jit(solution)/shard_map/ppermute | solution.py:26
  28.2 4.8 %collective-permute-start.14 = (bf16[1,64,256]{2,1,0:T(8,128)(2,1)S(1)}, bf16[1,64,256]{2,1,0:T(8,128)(2,1)S(1)}, u32[]{:S(2)}, u32[]{:S(2)}) collective-permute-start(bf16[1,64,256]{2,1,0:T(8,128)(2,1)S(1)} %get-tuple-element.86), channel_id=1, source_target_pairs={{0,16},{1,17},{2,18},{3,19},{4,20},{5,21},{6,22},{7,23},{8,24},{9,... | collective-permute-start | bytes 98312 | tf_op jit(solution)/shard_map/ppermute | solution.py:26
  28.2 4.8 %collective-permute-start.13 = (bf16[2,64,256]{2,1,0:T(8,128)(2,1)S(1)}, bf16[2,64,256]{2,1,0:T(8,128)(2,1)S(1)}, u32[]{:S(2)}, u32[]{:S(2)}) collective-permute-start(bf16[2,64,256]{2,1,0:T(8,128)(2,1)S(1)} %get-tuple-element.85), channel_id=1, source_target_pairs={{0,8},{1,9},{2,10},{3,11},{4,12},{5,13},{6,14},{7,15},{8,0},{9,1},... | collective-permute-start | bytes 196616 | tf_op jit(solution)/shard_map/ppermute | solution.py:26
  34.1 3.6 %collective-permute-start.19 = (bf16[2,256,512]{2,1,0:T(8,128)(2,1)S(1)}, bf16[2,256,512]{2,1,0:T(8,128)(2,1)S(1)}, u32[]{:S(2)}, u32[]{:S(2)}) collective-permute-start(bf16[2,256,512]{2,1,0:T(8,128)(2,1)S(1)} %add_convert_fusion.refs_0_), channel_id=1, source_target_pairs={{0,1},{1,0},{2,3},{3,2},{4,5},{5,4},{6,7},{7,6},{8,9},{9,8},{10,11... | collective-permute-start | bytes 1572872 | tf_op jit(solution)/shard_map/ppermute | solution.py:26
  34.1 7.1 %collective-permute-start.18 = (bf16[64,384]{1,0:T(8,128)(2,1)S(1)}, bf16[64,384]{1,0:T(8,128)(2,1)S(1)}, u32[]{:S(2)}, u32[]{:S(2)}) collective-permute-start(bf16[64,384]{1,0:T(8,128)(2,1)S(1)} %get-tuple-element.89), channel_id=1, source_target_pairs={{0,6},{1,7},{2,4},{3,5},{4,2},{5,3},{6,0},{7,1},{8,14},{9,15},{10,... | collective-permute-start | bytes 147464 | tf_op jit(solution)/shard_map/ppermute | solution.py:26
  36.0 5.2 %collective-permute-start.17 = (bf16[64,384]{1,0:T(8,128)(2,1)S(1)}, bf16[64,384]{1,0:T(8,128)(2,1)S(1)}, u32[]{:S(2)}, u32[]{:S(2)}) collective-permute-start(bf16[64,384]{1,0:T(8,128)(2,1)S(1)} %get-tuple-element.89), channel_id=1, source_target_pairs={{0,4},{1,5},{2,6},{3,7},{4,0},{5,1},{6,2},{7,3},{8,12},{9,13},{10,... | collective-permute-start | bytes 147464 | tf_op jit(solution)/shard_map/ppermute | solution.py:26
  37.2 4.1 %collective-permute-start.16 = (bf16[64,384]{1,0:T(8,128)(2,1)S(1)}, bf16[64,384]{1,0:T(8,128)(2,1)S(1)}, u32[]{:S(2)}, u32[]{:S(2)}) collective-permute-start(bf16[64,384]{1,0:T(8,128)(2,1)S(1)} %get-tuple-element.100.refs_0_), channel_id=1, source_target_pairs={{0,2},{1,3},{2,0},{3,1},{4,6},{5,7},{6,4},{7,5},{8,10},{9,11},{10,... | collective-permute-start | bytes 147464 | tf_op jit(solution)/shard_map/ppermute | solution.py:26
  37.7 4.7 %collective-permute-start.20 = (bf16[3,64,256]{2,1,0:T(8,128)(2,1)S(1)}, bf16[3,64,256]{2,1,0:T(8,128)(2,1)S(1)}, u32[]{:S(2)}, u32[]{:S(2)}) collective-permute-start(bf16[3,64,256]{2,1,0:T(8,128)(2,1)S(1)} %get-tuple-element.98), channel_id=1, source_target_pairs={{0,4},{1,5},{2,6},{3,7},{4,0},{5,1},{6,2},{7,3},{8,12},{9,13},{10,... | collective-permute-start | bytes 294920 | tf_op jit(solution)/shard_map/ppermute | solution.py:26
  41.3 2.0 %collective-permute-start.21 = (bf16[64,384]{1,0:T(8,128)(2,1)S(1)}, bf16[64,384]{1,0:T(8,128)(2,1)S(1)}, u32[]{:S(2)}, u32[]{:S(2)}) collective-permute-start(bf16[64,384]{1,0:T(8,128)(2,1)S(1)} %get-tuple-element.100.refs_0_), channel_id=1, source_target_pairs={{0,1},{1,0},{2,3},{3,2},{4,5},{5,4},{6,7},{7,6},{8,9},{9,8},{10,11... | collective-permute-start | bytes 147464 | tf_op jit(solution)/shard_map/ppermute | solution.py:26
  41.3 2.0 %collective-permute-start.22 = (bf16[64,384]{1,0:T(8,128)(2,1)S(1)}, bf16[64,384]{1,0:T(8,128)(2,1)S(1)}, u32[]{:S(2)}, u32[]{:S(2)}) collective-permute-start(bf16[64,384]{1,0:T(8,128)(2,1)S(1)} %collective-permute-done.16.refs_1_), channel_id=1, source_target_pairs={{0,1},{1,0},{2,3},{3,2},{4,5},{5,4},{6,7},{7,6},{8,9},{9,8},{10,11... | collective-permute-start | bytes 147464 | tf_op jit(solution)/shard_map/ppermute | solution.py:26
  41.8 1.5 %collective-permute-start.23 = (bf16[64,384]{1,0:T(8,128)(2,1)S(1)}, bf16[64,384]{1,0:T(8,128)(2,1)S(1)}, u32[]{:S(2)}, u32[]{:S(2)}) collective-permute-start(bf16[64,384]{1,0:T(8,128)(2,1)S(1)} %collective-permute-done.17.refs_2_), channel_id=1, source_target_pairs={{0,1},{1,0},{2,3},{3,2},{4,5},{5,4},{6,7},{7,6},{8,9},{9,8},{10,11... | collective-permute-start | bytes 147464 | tf_op jit(solution)/shard_map/ppermute | solution.py:26
  41.8 1.5 %collective-permute-start.24 = (bf16[64,384]{1,0:T(8,128)(2,1)S(1)}, bf16[64,384]{1,0:T(8,128)(2,1)S(1)}, u32[]{:S(2)}, u32[]{:S(2)}) collective-permute-start(bf16[64,384]{1,0:T(8,128)(2,1)S(1)} %collective-permute-done.18.refs_3_), channel_id=1, source_target_pairs={{0,1},{1,0},{2,3},{3,2},{4,5},{5,4},{6,7},{7,6},{8,9},{9,8},{10,11... | collective-permute-start | bytes 147464 | tf_op jit(solution)/shard_map/ppermute | solution.py:26
  (2 other events, 2.6 us)

commit v8 on v6

--- a/solution.py
+++ b/solution.py
@@ -313,7 +313,7 @@
         [inverse, rhs],
         [pltpu.VMEM((sources, rows), BF16)],
     )
-    keep, offsets, pattern, panel = lax.optimization_barrier((keep, offsets, pattern, panel))
+    keep, panel = lax.optimization_barrier((keep, panel))
     for mask in range(1, half):
         held[mask] = moved(panel, 0, mask)
     spots = jnp.concatenate([offsets, pattern], axis=0)
@@ -411,7 +411,7 @@
         [
             pltpu.VMEM((sources, levels * touched), BF16),
             pltpu.VMEM((rows, sources), BF16),
-            pltpu.SemaphoreType.DMA((half,)),
+            pltpu.SemaphoreType.DMA((groups,)),
         ],
         space=pl.ANY,
     )[0]

time: 44.9 us -> 44.9 us (level)
  no operation moved by 1% of the time
where the time goes in v8:
time: 44.9 us; the launch traced here: 44.7 us
  starting transfers between devices  21.5 us (48%)
  Pallas kernels  10.9 us (24%)
  waiting for transfers between devices  8.62 us (19%)
  local copies, waits for them, and re-layouts  2.67 us (6%)
  between operations  0.85 us (2%)
    ppermute x25, starting transfers between devices, moved(): return lax.ppermute(block, AXES, route)  21.5 us
    pallas_call x11, Pallas kernels, call(): pl.pallas_call(body, out_shape=outs, in_specs=specs, out_specs=[pl.BlockS...  10.9 us
    ppermute x25, waiting for transfers between devices, moved(): return lax.ppermute(block, AXES, route)  8.62 us
    unnamed x18, local copies, waits for them, and re-layouts  2.67 us
  transfers between devices with their start and end apart: 25, of which 10 were waited for; matrix products, arithmetic and copies ran while one was open for 0% of the time, Pallas kernels for 20%

profile of v8, /device:TPU:0, one launch (start us, length us, event | category | flops | bytes accessed | tf_op | source)
XLA Modules:
  0.0 44.7 jit_solution(14870641492896228614)
XLA Ops:
  0.6 3.0 %collective-permute-start = (bf16[384,512]{1,0:T(8,128)(2,1)}, bf16[384,512]{1,0:T(8,128)(2,1)S(1)}, u32[]{:S(2)}, u32[]{:S(2)}) collective-permute-start(bf16[384,512]{1,0:T(8,128)(2,1)} %bitcast.16), channel_id=1, source_target_pairs={{0,2},{1,3},{2,0},{3,1},{4,6},{5,7},{6,4},{7,5},{8,10},{9,11},{10,... | collective-permute-start | bytes 1179656 | tf_op jit(solution)/shard_map/ppermute | solution.py:26
  3.7 1.6 %copy-done = bf16[1,2048,512]{2,1,0:T(8,128)(2,1)S(1)} copy-done((bf16[1,2048,512]{2,1,0:T(8,128)(2,1)S(1)}, bf16[1,2048,512]{2,1,0:T(8,128)(2,1)}, u32[]{:S(2)}) %copy-start) | copy-done | bytes 2097176
  5.3 1.0 %copy-done.4 = bf16[1,512,512]{2,1,0:T(8,128)(2,1)S(1)} copy-done((bf16[1,512,512]{2,1,0:T(8,128)(2,1)S(1)}, bf16[1,512,512]{2,1,0:T(8,128)(2,1)}, u32[]{:S(2)}) %copy-start.4) | copy-done | bytes 524312
  6.3 1.3 %leaf_products.1 = (f32[4,256,512]{2,1,0:T(8,128)S(1)}, bf16[256,512]{1,0:T(8,128)(2,1)S(1)}, bf16[256,512]{1,0:T(8,128)(2,1)S(1)}, bf16[256,512]{1,0:T(8,128)(2,1)S(1)}, bf16[256,512]{1,0:T(8,128)(2,1)S(1)}) custom-call(bf16[2048,512]{1,0:T(8,128)(2,1)S(1)} %bitcast.8, bf16[512,512]{1,0:T(8,128)(2,1)S(1)} %bitcast.14), custom_call_target="tpu_custom_call" | custom-call | flops 5000000000 | tf_op jit(solution)/shard_map/leaf_products/pallas_call | solution.py:39
  7.7 0.5 %collective-permute-start.2 = (bf16[256,512]{1,0:T(8,128)(2,1)S(1)}, bf16[256,512]{1,0:T(8,128)(2,1)S(1)}, u32[]{:S(2)}, u32[]{:S(2)}) collective-permute-start(bf16[256,512]{1,0:T(8,128)(2,1)S(1)} %get-tuple-element.59), channel_id=1, source_target_pairs={{0,1},{1,0},{2,3},{3,2},{4,5},{5,4},{6,7},{7,6},{8,9},{9,8},{10,11... | collective-permute-start | bytes 786440 | tf_op jit(solution)/shard_map/ppermute | solution.py:26
  8.3 1.6 %collective-permute-start.10 = (s32[2,3]{1,0:T(2,128)S(1)}, s32[2,3]{1,0:T(2,128)S(1)}, u32[]{:S(2)}, u32[]{:S(2)}) collective-permute-start(s32[2,3]{1,0:T(2,128)S(1)} %pad_add_fusion.1), channel_id=1, source_target_pairs={{0,4},{1,5},{2,6},{3,7},{4,0},{5,1},{6,2},{7,3},{8,12},{9,13},{10,... | collective-permute-start | bytes 80 | tf_op jit(solution)/shard_map/ppermute | solution.py:26
  9.9 2.1 %collective-permute-done.10 = s32[2,3]{1,0:T(2,128)S(1)} collective-permute-done((s32[2,3]{1,0:T(2,128)S(1)}, s32[2,3]{1,0:T(2,128)S(1)}, u32[]{:S(2)}, u32[]{:S(2)}) %collective-permute-start.10) | collective-permute-done | bytes 56 | tf_op jit(solution)/shard_map/ppermute | solution.py:26
  11.9 1.0 %collective-permute-done.refs_0_.refs_2_ = bf16[384,512]{1,0:T(8,128)(2,1)S(1)} collective-permute-done((bf16[384,512]{1,0:T(8,128)(2,1)}, bf16[384,512]{1,0:T(8,128)(2,1)S(1)}, u32[]{:S(2)}, u32[]{:S(2)}) %collective-permute-start) | collective-permute-done | bytes 393248 | tf_op jit(solution)/shard_map/ppermute | solution.py:26
  13.0 0.6 %collective-permute-start.6 = (bf16[384,512]{1,0:T(8,128)(2,1)S(1)}, bf16[384,512]{1,0:T(8,128)(2,1)S(1)}, u32[]{:S(2)}, u32[]{:S(2)}) collective-permute-start(bf16[384,512]{1,0:T(8,128)(2,1)S(1)} %collective-permute-done.refs_0_.refs_2_), channel_id=1, source_target_pairs={{0,1},{1,0},{2,3},{3,2},{4,5},{5,4},{6,7},{7,6},{8,9},{9,8},{10,11... | collective-permute-start | bytes 1179656 | tf_op jit(solution)/shard_map/ppermute | solution.py:26
  13.6 0.9 %collective-permute-done.5.refs_5_ = bf16[256,512]{1,0:T(8,128)(2,1)S(1)} collective-permute-done((bf16[256,512]{1,0:T(8,128)(2,1)S(1)}, bf16[256,512]{1,0:T(8,128)(2,1)S(1)}, u32[]{:S(2)}, u32[]{:S(2)}) %collective-permute-start.5) | collective-permute-done | bytes 262176 | tf_op jit(solution)/shard_map/ppermute | solution.py:26
  14.5 0.6 %own_partials.1 = (bf16[2,256,512]{2,1,0:T(8,128)(2,1)S(1)}, bf16[2,256,512]{2,1,0:T(8,128)(2,1)S(1)}, f32[2,256,512]{2,1,0:T(8,128)S(1)}, f32[256,384]{1,0:T(8,128)S(1)}) custom-call(f32[4,256,512]{2,1,0:T(8,128)S(1)} %get-tuple-element.57.keep, bf16[384,512]{1,0:T(8,128)(2,1)S(1)} %bitcast.18, bf16[384,512]{1,0:T(8,128)(2,1)S(1)} %collective-permute-done.1.refs_1_, ...), custom_call_target="tpu_custom_call" | custom-call | flops 5000000000 | tf_op jit(solution)/shard_map/own_partials/pallas_call | solution.py:39
  15.2 0.5 %partials.1 = (f32[64,384]{1,0:T(8,128)S(1)}, bf16[64,384]{1,0:T(8,128)(2,1)S(1)}, bf16[64,384]{1,0:T(8,128)(2,1)S(1)}, bf16[64,384]{1,0:T(8,128)(2,1)S(1)}) custom-call(bf16[2,256,512]{2,1,0:T(8,128)(2,1)S(1)} %get-tuple-element.80.low.refs_4_, bf16[2,256,512]{2,1,0:T(8,128)(2,1)S(1)} %get-tuple-element.89.high, f32[256,384]{1,0:T(8,128)S(1)} %get-tuple-element.65.early, ...), custom_call_target="tpu_custom_call" | custom-call | flops 5000000000 | tf_op jit(solution)/shard_map/partials/pallas_call | solution.py:39
  15.7 2.7 %collective-permute-start.7 = (bf16[64,384]{1,0:T(8,128)(2,1)S(1)}, bf16[64,384]{1,0:T(8,128)(2,1)S(1)}, u32[]{:S(2)}, u32[]{:S(2)}) collective-permute-start(bf16[64,384]{1,0:T(8,128)(2,1)S(1)} %get-tuple-element.69), channel_id=1, source_target_pairs={{0,6},{1,7},{2,4},{3,5},{4,2},{5,3},{6,0},{7,1},{8,14},{9,15},{10,... | collective-permute-start | bytes 147464 | tf_op jit(solution)/shard_map/ppermute | solution.py:26
  18.4 0.5 %collective-permute-start.8 = (bf16[64,384]{1,0:T(8,128)(2,1)S(1)}, bf16[64,384]{1,0:T(8,128)(2,1)S(1)}, u32[]{:S(2)}, u32[]{:S(2)}) collective-permute-start(bf16[64,384]{1,0:T(8,128)(2,1)S(1)} %get-tuple-element.70), channel_id=1, source_target_pairs={{0,2},{1,3},{2,0},{3,1},{4,6},{5,7},{6,4},{7,5},{8,10},{9,11},{10,... | collective-permute-start | bytes 147464 | tf_op jit(solution)/shard_map/ppermute | solution.py:26
  19.2 1.7 %collective-permute-start.15 = (bf16[2,256,512]{2,1,0:T(8,128)(2,1)S(1)}, bf16[2,256,512]{2,1,0:T(8,128)(2,1)S(1)}, u32[]{:S(2)}, u32[]{:S(2)}) collective-permute-start(bf16[2,256,512]{2,1,0:T(8,128)(2,1)S(1)} %get-tuple-element.89.high), channel_id=1, source_target_pairs={{0,2},{1,3},{2,0},{3,1},{4,6},{5,7},{6,4},{7,5},{8,10},{9,11},{10,... | collective-permute-start | bytes 1572872 | tf_op jit(solution)/shard_map/ppermute | solution.py:26
  21.0 1.3 %prepare.1 = (bf16[2,256,256]{2,1,0:T(8,128)(2,1)S(1)}, bf16[2,256,256]{2,1,0:T(8,128)(2,1)S(1)}, f32[3,64,256]{2,1,0:T(8,128)S(1)}, bf16[3,256,256]{2,1,0:T(8,128)(2,1)S(1)}) custom-call(s32[4,3]{1,0:T(4,128)S(1)} %pad_add_fusion.spots, f32[3,256,256]{2,1,0:T(8,128)S(1)} %bitcast.12, f32[2,256,256]{2,1,0:T(8,128)S(1)} %bitcast.15, f32[3,256,512]{2,1,0:T(8,128)S(1)} %bitcast.11), custom_call_target="tpu_custom_call" | custom-call | flops 5000000000 | tf_op jit(solution)/shard_map/prepare/pallas_call | solution.py:39
  22.3 0.5 %collective-permute-done.8.same = bf16[64,384]{1,0:T(8,128)(2,1)S(1)} collective-permute-done((bf16[64,384]{1,0:T(8,128)(2,1)S(1)}, bf16[64,384]{1,0:T(8,128)(2,1)S(1)}, u32[]{:S(2)}, u32[]{:S(2)}) %collective-permute-start.8) | collective-permute-done | bytes 49184 | tf_op jit(solution)/shard_map/ppermute | solution.py:26
  23.0 0.8 %upward.1 = (f32[3,64,256]{2,1,0:T(8,128)S(1)}, bf16[2,64,256]{2,1,0:T(8,128)(2,1)S(1)}, bf16[1,64,256]{2,1,0:T(8,128)(2,1)S(1)}) custom-call(f32[64,384]{1,0:T(8,128)S(1)} %get-tuple-element.68.own, bf16[64,384]{1,0:T(8,128)(2,1)S(1)} %collective-permute-done.7.cross, bf16[64,384]{1,0:T(8,128)(2,1)S(1)} %collective-permute-done.8.same, ...), custom_call_target="tpu_custom_call" | custom-call | flops 5000000000 | tf_op jit(solution)/shard_map/upward/pallas_call | solution.py:39
  23.8 2.7 %collective-permute-start.13 = (bf16[1,64,256]{2,1,0:T(8,128)(2,1)S(1)}, bf16[1,64,256]{2,1,0:T(8,128)(2,1)S(1)}, u32[]{:S(2)}, u32[]{:S(2)}) collective-permute-start(bf16[1,64,256]{2,1,0:T(8,128)(2,1)S(1)} %get-tuple-element.87), channel_id=1, source_target_pairs={{0,16},{1,17},{2,18},{3,19},{4,20},{5,21},{6,22},{7,23},{8,24},{9,... | collective-permute-start | bytes 98312 | tf_op jit(solution)/shard_map/ppermute | solution.py:26
  26.5 1.3 %collective-permute-start.14 = (bf16[1,64,256]{2,1,0:T(8,128)(2,1)S(1)}, bf16[1,64,256]{2,1,0:T(8,128)(2,1)S(1)}, u32[]{:S(2)}, u32[]{:S(2)}) collective-permute-start(bf16[1,64,256]{2,1,0:T(8,128)(2,1)S(1)} %get-tuple-element.87), channel_id=1, source_target_pairs={{0,24},{1,25},{2,26},{3,27},{4,28},{5,29},{6,30},{7,31},{8,16},{9,... | collective-permute-start | bytes 98312 | tf_op jit(solution)/shard_map/ppermute | solution.py:26
  28.1 1.5 %lower_transposed.1 = (f32[512,512]{1,0:T(8,128)S(1)}, bf16[512,384]{1,0:T(8,128)(2,1)S(1)}) custom-call(bf16[2048,512]{1,0:T(8,128)(2,1)S(1)} %bitcast.9, bf16[384,512]{1,0:T(8,128)(2,1)S(1)} %bitcast.19, bf16[384,512]{1,0:T(8,128)(2,1)S(1)} %collective-permute-done.1.refs_1_, bf16[384,512]{1,0:T(8,128)(2,1)S(1)} %collective-permute-done.refs_0_.refs_2_, ...), custom_call_target="tpu_custom_call" | custom-call | flops 5000000000 | tf_op jit(solution)/shard_map/lower_transposed/pallas_call | solution.py:39
  29.6 0.9 %squares.1 = (bf16[3,256,256]{2,1,0:T(8,128)(2,1)S(1)}, bf16[3,256,256]{2,1,0:T(8,128)(2,1)S(1)}) custom-call(f32[3,256,256]{2,1,0:T(8,128)S(1)} %bitcast.13), custom_call_target="tpu_custom_call" | custom-call | flops 5000000000 | tf_op jit(solution)/shard_map/squares/pallas_call | solution.py:39
  30.5 1.8 %collective-permute-done.14.refs_2_ = bf16[1,64,256]{2,1,0:T(8,128)(2,1)S(1)} collective-permute-done((bf16[1,64,256]{2,1,0:T(8,128)(2,1)S(1)}, bf16[1,64,256]{2,1,0:T(8,128)(2,1)S(1)}, u32[]{:S(2)}, u32[]{:S(2)}) %collective-permute-start.14) | collective-permute-done | bytes 32800 | tf_op jit(solution)/shard_map/ppermute | solution.py:26
  32.5 0.8 %downward.1 = (f32[3,64,256]{2,1,0:T(8,128)S(1)}, bf16[64,384]{1,0:T(8,128)(2,1)S(1)}, bf16[64,384]{1,0:T(8,128)(2,1)S(1)}, bf16[3,64,256]{2,1,0:T(8,128)(2,1)S(1)}) custom-call(f32[3,64,256]{2,1,0:T(8,128)S(1)} %get-tuple-element.78.kept, f32[3,64,256]{2,1,0:T(8,128)S(1)} %get-tuple-element.73.right, bf16[3,256,256]{2,1,0:T(8,128)(2,1)S(1)} %get-tuple-element.84.q_high, ...), custom_call_target="tpu_custom_call" | custom-call | flops 5000000000 | tf_op jit(solution)/shard_map/downward/pallas_call | solution.py:39
  34.0 1.6 %collective-permute-start.17 = (bf16[64,384]{1,0:T(8,128)(2,1)S(1)}, bf16[64,384]{1,0:T(8,128)(2,1)S(1)}, u32[]{:S(2)}, u32[]{:S(2)}) collective-permute-start(bf16[64,384]{1,0:T(8,128)(2,1)S(1)} %get-tuple-element.91), channel_id=1, source_target_pairs={{0,4},{1,5},{2,6},{3,7},{4,0},{5,1},{6,2},{7,3},{8,12},{9,13},{10,... | collective-permute-start | bytes 147464 | tf_op jit(solution)/shard_map/ppermute | solution.py:26
  35.6 1.5 %collective-permute-start.18 = (bf16[64,384]{1,0:T(8,128)(2,1)S(1)}, bf16[64,384]{1,0:T(8,128)(2,1)S(1)}, u32[]{:S(2)}, u32[]{:S(2)}) collective-permute-start(bf16[64,384]{1,0:T(8,128)(2,1)S(1)} %get-tuple-element.91), channel_id=1, source_target_pairs={{0,6},{1,7},{2,4},{3,5},{4,2},{5,3},{6,0},{7,1},{8,14},{9,15},{10,... | collective-permute-start | bytes 147464 | tf_op jit(solution)/shard_map/ppermute | solution.py:26
  37.5 1.5 %collective-permute-start.20 = (bf16[3,64,256]{2,1,0:T(8,128)(2,1)S(1)}, bf16[3,64,256]{2,1,0:T(8,128)(2,1)S(1)}, u32[]{:S(2)}, u32[]{:S(2)}) collective-permute-start(bf16[3,64,256]{2,1,0:T(8,128)(2,1)S(1)} %get-tuple-element.100), channel_id=1, source_target_pairs={{0,4},{1,5},{2,6},{3,7},{4,0},{5,1},{6,2},{7,3},{8,12},{9,13},{10,... | collective-permute-start | bytes 294920 | tf_op jit(solution)/shard_map/ppermute | solution.py:26
  39.1 0.9 %upper_transposed.1.base = f32[512,512]{1,0:T(8,128)S(1)} custom-call(bf16[2048,512]{1,0:T(8,128)(2,1)S(1)} %bitcast.10, f32[512,512]{1,0:T(8,128)S(1)} %get-tuple-element.92.lower, bf16[2,256,512]{2,1,0:T(8,128)(2,1)S(1)} %add_convert_fusion.refs_0_, bf16[2,256,512]{2,1,0:T(8,128)(2,1)S(1)} %collective-permute-done.19.refs_1_), custom_call_target="tpu_custom_call" | custom-call | flops 5000000000 | tf_op jit(solution)/shard_map/upper_transposed/pallas_call | solution.py:39
  40.0 1.4 %collective-permute-done.16.refs_1_ = bf16[64,384]{1,0:T(8,128)(2,1)S(1)} collective-permute-done((bf16[64,384]{1,0:T(8,128)(2,1)S(1)}, bf16[64,384]{1,0:T(8,128)(2,1)S(1)}, u32[]{:S(2)}, u32[]{:S(2)}) %collective-permute-start.16) | collective-permute-done | bytes 49184 | tf_op jit(solution)/shard_map/ppermute | solution.py:26
  41.4 0.5 %collective-permute-start.22 = (bf16[64,384]{1,0:T(8,128)(2,1)S(1)}, bf16[64,384]{1,0:T(8,128)(2,1)S(1)}, u32[]{:S(2)}, u32[]{:S(2)}) collective-permute-start(bf16[64,384]{1,0:T(8,128)(2,1)S(1)} %collective-permute-done.16.refs_1_), channel_id=1, source_target_pairs={{0,1},{1,0},{2,3},{3,2},{4,5},{5,4},{6,7},{7,6},{8,9},{9,8},{10,11... | collective-permute-start | bytes 147464 | tf_op jit(solution)/shard_map/ppermute | solution.py:26
  42.5 0.9 %assemble.1 = f32[3,256,128]{2,1,0:T(8,128)} custom-call(f32[3,64,256]{2,1,0:T(8,128)S(1)} %get-tuple-element.106.mine, bf16[3,64,256]{2,1,0:T(8,128)(2,1)S(1)} %collective-permute-done.20.passed), custom_call_target="tpu_custom_call" | custom-call | flops 5000000000 | tf_op jit(solution)/shard_map/assemble/pallas_call | solution.py:39
  43.4 1.3 %finish.1 = bf16[512,512]{1,0:T(8,128)(2,1)} custom-call(f32[512,512]{1,0:T(8,128)S(1)} %upper_transposed.1.base, bf16[512,384]{1,0:T(8,128)(2,1)S(1)} %get-tuple-element.101.weight_turned, bf16[64,384]{1,0:T(8,128)(2,1)S(1)} %get-tuple-element.102.refs_0_, bf16[64,384]{1,0:T(8,128)(2,1)S(1)} %collective-permute-done.16.refs_1_, ...), custom_call_target="tpu_custom_call" | custom-call | flops 5000000000 | tf_op jit(solution)/shard_map/finish/pallas_call | solution.py:39
  (50 shorter events, 2.9 us)
Async XLA Ops:
  0.6 12.4 %collective-permute-start = (bf16[384,512]{1,0:T(8,128)(2,1)}, bf16[384,512]{1,0:T(8,128)(2,1)S(1)}, u32[]{:S(2)}, u32[]{:S(2)}) collective-permute-start(bf16[384,512]{1,0:T(8,128)(2,1)} %bitcast.16), channel_id=1, source_target_pairs={{0,2},{1,3},{2,0},{3,1},{4,6},{5,7},{6,4},{7,5},{8,10},{9,11},{10,... | collective-permute-start | bytes 1179656 | tf_op jit(solution)/shard_map/ppermute | solution.py:26
  3.7 1.6 %copy-start = (bf16[1,2048,512]{2,1,0:T(8,128)(2,1)S(1)}, bf16[1,2048,512]{2,1,0:T(8,128)(2,1)}, u32[]{:S(2)}) copy-start(bf16[1,2048,512]{2,1,0:T(8,128)(2,1)} %param.9) | copy-start | bytes 6291460
  6.3 2.0 %copy-start.7 = (s32[1,3]{1,0:T(1,128)S(1)}, s32[1,3]{1,0:T(1,128)}, u32[]{:S(2)}) copy-start(s32[1,3]{1,0:T(1,128)} %param.11) | copy-start | bytes 40
  6.3 2.0 %copy-start.8 = (s32[1,3]{1,0:T(1,128)S(1)}, s32[1,3]{1,0:T(1,128)}, u32[]{:S(2)}) copy-start(s32[1,3]{1,0:T(1,128)} %param.12) | copy-start | bytes 40
  7.6 6.9 %collective-permute-start.1 = (bf16[384,512]{1,0:T(8,128)(2,1)S(1)}, bf16[384,512]{1,0:T(8,128)(2,1)S(1)}, u32[]{:S(2)}, u32[]{:S(2)}) collective-permute-start(bf16[384,512]{1,0:T(8,128)(2,1)S(1)} %bitcast.17), channel_id=1, source_target_pairs={{0,1},{1,0},{2,3},{3,2},{4,5},{5,4},{6,7},{7,6},{8,9},{9,8},{10,11... | collective-permute-start | bytes 1179656 | tf_op jit(solution)/shard_map/ppermute | solution.py:26
  7.7 5.3 %collective-permute-start.2 = (bf16[256,512]{1,0:T(8,128)(2,1)S(1)}, bf16[256,512]{1,0:T(8,128)(2,1)S(1)}, u32[]{:S(2)}, u32[]{:S(2)}) collective-permute-start(bf16[256,512]{1,0:T(8,128)(2,1)S(1)} %get-tuple-element.59), channel_id=1, source_target_pairs={{0,1},{1,0},{2,3},{3,2},{4,5},{5,4},{6,7},{7,6},{8,9},{9,8},{10,11... | collective-permute-start | bytes 786440 | tf_op jit(solution)/shard_map/ppermute | solution.py:26
  8.2 5.4 %collective-permute-start.3 = (bf16[256,512]{1,0:T(8,128)(2,1)S(1)}, bf16[256,512]{1,0:T(8,128)(2,1)S(1)}, u32[]{:S(2)}, u32[]{:S(2)}) collective-permute-start(bf16[256,512]{1,0:T(8,128)(2,1)S(1)} %get-tuple-element.60), channel_id=1, source_target_pairs={{0,1},{1,0},{2,3},{3,2},{4,5},{5,4},{6,7},{7,6},{8,9},{9,8},{10,11... | collective-permute-start | bytes 786440 | tf_op jit(solution)/shard_map/ppermute | solution.py:26
  8.3 3.6 %collective-permute-start.10 = (s32[2,3]{1,0:T(2,128)S(1)}, s32[2,3]{1,0:T(2,128)S(1)}, u32[]{:S(2)}, u32[]{:S(2)}) collective-permute-start(s32[2,3]{1,0:T(2,128)S(1)} %pad_add_fusion.1), channel_id=1, source_target_pairs={{0,4},{1,5},{2,6},{3,7},{4,0},{5,1},{6,2},{7,3},{8,12},{9,13},{10,... | collective-permute-start | bytes 80 | tf_op jit(solution)/shard_map/ppermute | solution.py:26
  11.9 1.7 %collective-permute-start.4 = (bf16[256,512]{1,0:T(8,128)(2,1)S(1)}, bf16[256,512]{1,0:T(8,128)(2,1)S(1)}, u32[]{:S(2)}, u32[]{:S(2)}) collective-permute-start(bf16[256,512]{1,0:T(8,128)(2,1)S(1)} %get-tuple-element.61), channel_id=1, source_target_pairs={{0,1},{1,0},{2,3},{3,2},{4,5},{5,4},{6,7},{7,6},{8,9},{9,8},{10,11... | collective-permute-start | bytes 786440 | tf_op jit(solution)/shard_map/ppermute | solution.py:26
  13.0 1.5 %collective-permute-start.5 = (bf16[256,512]{1,0:T(8,128)(2,1)S(1)}, bf16[256,512]{1,0:T(8,128)(2,1)S(1)}, u32[]{:S(2)}, u32[]{:S(2)}) collective-permute-start(bf16[256,512]{1,0:T(8,128)(2,1)S(1)} %get-tuple-element.62), channel_id=1, source_target_pairs={{0,1},{1,0},{2,3},{3,2},{4,5},{5,4},{6,7},{7,6},{8,9},{9,8},{10,11... | collective-permute-start | bytes 786440 | tf_op jit(solution)/shard_map/ppermute | solution.py:26
  13.0 2.1 %collective-permute-start.6 = (bf16[384,512]{1,0:T(8,128)(2,1)S(1)}, bf16[384,512]{1,0:T(8,128)(2,1)S(1)}, u32[]{:S(2)}, u32[]{:S(2)}) collective-permute-start(bf16[384,512]{1,0:T(8,128)(2,1)S(1)} %collective-permute-done.refs_0_.refs_2_), channel_id=1, source_target_pairs={{0,1},{1,0},{2,3},{3,2},{4,5},{5,4},{6,7},{7,6},{8,9},{9,8},{10,11... | collective-permute-start | bytes 1179656 | tf_op jit(solution)/shard_map/ppermute | solution.py:26
  15.1 5.8 %copy-start.2 = (f32[1,3,256,512]{3,2,1,0:T(8,128)S(1)}, f32[1,3,256,512]{3,2,1,0:T(8,128)}, u32[]{:S(2)}) copy-start(f32[1,3,256,512]{3,2,1,0:T(8,128)} %param.15) | copy-start | bytes 4718596
  15.1 5.8 %copy-start.3 = (f32[1,3,256,256]{3,2,1,0:T(8,128)S(1)}, f32[1,3,256,256]{3,2,1,0:T(8,128)}, u32[]{:S(2)}) copy-start(f32[1,3,256,256]{3,2,1,0:T(8,128)} %param.13) | copy-start | bytes 2359300
  15.2 5.8 %copy-start.5 = (f32[1,2,256,256]{3,2,1,0:T(8,128)S(1)}, f32[1,2,256,256]{3,2,1,0:T(8,128)}, u32[]{:S(2)}) copy-start(f32[1,2,256,256]{3,2,1,0:T(8,128)} %param.14) | copy-start | bytes 1572868
  15.7 6.6 %collective-permute-start.7 = (bf16[64,384]{1,0:T(8,128)(2,1)S(1)}, bf16[64,384]{1,0:T(8,128)(2,1)S(1)}, u32[]{:S(2)}, u32[]{:S(2)}) collective-permute-start(bf16[64,384]{1,0:T(8,128)(2,1)S(1)} %get-tuple-element.69), channel_id=1, source_target_pairs={{0,6},{1,7},{2,4},{3,5},{4,2},{5,3},{6,0},{7,1},{8,14},{9,15},{10,... | collective-permute-start | bytes 147464 | tf_op jit(solution)/shard_map/ppermute | solution.py:26
  18.4 4.3 %collective-permute-start.8 = (bf16[64,384]{1,0:T(8,128)(2,1)S(1)}, bf16[64,384]{1,0:T(8,128)(2,1)S(1)}, u32[]{:S(2)}, u32[]{:S(2)}) collective-permute-start(bf16[64,384]{1,0:T(8,128)(2,1)S(1)} %get-tuple-element.70), channel_id=1, source_target_pairs={{0,2},{1,3},{2,0},{3,1},{4,6},{5,7},{6,4},{7,5},{8,10},{9,11},{10,... | collective-permute-start | bytes 147464 | tf_op jit(solution)/shard_map/ppermute | solution.py:26
  18.9 4.1 %collective-permute-start.9 = (bf16[64,384]{1,0:T(8,128)(2,1)S(1)}, bf16[64,384]{1,0:T(8,128)(2,1)S(1)}, u32[]{:S(2)}, u32[]{:S(2)}) collective-permute-start(bf16[64,384]{1,0:T(8,128)(2,1)S(1)} %get-tuple-element.71), channel_id=1, source_target_pairs={{0,4},{1,5},{2,6},{3,7},{4,0},{5,1},{6,2},{7,3},{8,12},{9,13},{10,... | collective-permute-start | bytes 147464 | tf_op jit(solution)/shard_map/ppermute | solution.py:26
  19.2 8.9 %collective-permute-start.11 = (bf16[2,256,512]{2,1,0:T(8,128)(2,1)S(1)}, bf16[2,256,512]{2,1,0:T(8,128)(2,1)S(1)}, u32[]{:S(2)}, u32[]{:S(2)}) collective-permute-start(bf16[2,256,512]{2,1,0:T(8,128)(2,1)S(1)} %get-tuple-element.80.low.refs_4_), channel_id=1, source_target_pairs={{0,1},{1,0},{2,3},{3,2},{4,5},{5,4},{6,7},{7,6},{8,9},{9,8},{10,11... | collective-permute-start | bytes 1572872 | tf_op jit(solution)/shard_map/ppermute | solution.py:26
  19.2 14.5 %collective-permute-start.15 = (bf16[2,256,512]{2,1,0:T(8,128)(2,1)S(1)}, bf16[2,256,512]{2,1,0:T(8,128)(2,1)S(1)}, u32[]{:S(2)}, u32[]{:S(2)}) collective-permute-start(bf16[2,256,512]{2,1,0:T(8,128)(2,1)S(1)} %get-tuple-element.89.high), channel_id=1, source_target_pairs={{0,2},{1,3},{2,0},{3,1},{4,6},{5,7},{6,4},{7,5},{8,10},{9,11},{10,... | collective-permute-start | bytes 1572872 | tf_op jit(solution)/shard_map/ppermute | solution.py:26
  23.0 5.1 %copy-start.1 = (bf16[1,2048,512]{2,1,0:T(8,128)(2,1)S(1)}, bf16[1,2048,512]{2,1,0:T(8,128)(2,1)}, u32[]{:S(2)}) copy-start(bf16[1,2048,512]{2,1,0:T(8,128)(2,1)} %param.9) | copy-start | bytes 6291460
  23.8 6.6 %collective-permute-start.13 = (bf16[1,64,256]{2,1,0:T(8,128)(2,1)S(1)}, bf16[1,64,256]{2,1,0:T(8,128)(2,1)S(1)}, u32[]{:S(2)}, u32[]{:S(2)}) collective-permute-start(bf16[1,64,256]{2,1,0:T(8,128)(2,1)S(1)} %get-tuple-element.87), channel_id=1, source_target_pairs={{0,16},{1,17},{2,18},{3,19},{4,20},{5,21},{6,22},{7,23},{8,24},{9,... | collective-permute-start | bytes 98312 | tf_op jit(solution)/shard_map/ppermute | solution.py:26
  26.5 5.8 %collective-permute-start.14 = (bf16[1,64,256]{2,1,0:T(8,128)(2,1)S(1)}, bf16[1,64,256]{2,1,0:T(8,128)(2,1)S(1)}, u32[]{:S(2)}, u32[]{:S(2)}) collective-permute-start(bf16[1,64,256]{2,1,0:T(8,128)(2,1)S(1)} %get-tuple-element.87), channel_id=1, source_target_pairs={{0,24},{1,25},{2,26},{3,27},{4,28},{5,29},{6,30},{7,31},{8,16},{9,... | collective-permute-start | bytes 98312 | tf_op jit(solution)/shard_map/ppermute | solution.py:26
  27.8 4.6 %collective-permute-start.12 = (bf16[2,64,256]{2,1,0:T(8,128)(2,1)S(1)}, bf16[2,64,256]{2,1,0:T(8,128)(2,1)S(1)}, u32[]{:S(2)}, u32[]{:S(2)}) collective-permute-start(bf16[2,64,256]{2,1,0:T(8,128)(2,1)S(1)} %get-tuple-element.86), channel_id=1, source_target_pairs={{0,8},{1,9},{2,10},{3,11},{4,12},{5,13},{6,14},{7,15},{8,0},{9,1},... | collective-permute-start | bytes 196616 | tf_op jit(solution)/shard_map/ppermute | solution.py:26
  33.9 3.6 %collective-permute-start.19 = (bf16[2,256,512]{2,1,0:T(8,128)(2,1)S(1)}, bf16[2,256,512]{2,1,0:T(8,128)(2,1)S(1)}, u32[]{:S(2)}, u32[]{:S(2)}) collective-permute-start(bf16[2,256,512]{2,1,0:T(8,128)(2,1)S(1)} %add_convert_fusion.refs_0_), channel_id=1, source_target_pairs={{0,1},{1,0},{2,3},{3,2},{4,5},{5,4},{6,7},{7,6},{8,9},{9,8},{10,11... | collective-permute-start | bytes 1572872 | tf_op jit(solution)/shard_map/ppermute | solution.py:26
  34.0 7.4 %collective-permute-start.17 = (bf16[64,384]{1,0:T(8,128)(2,1)S(1)}, bf16[64,384]{1,0:T(8,128)(2,1)S(1)}, u32[]{:S(2)}, u32[]{:S(2)}) collective-permute-start(bf16[64,384]{1,0:T(8,128)(2,1)S(1)} %get-tuple-element.91), channel_id=1, source_target_pairs={{0,4},{1,5},{2,6},{3,7},{4,0},{5,1},{6,2},{7,3},{8,12},{9,13},{10,... | collective-permute-start | bytes 147464 | tf_op jit(solution)/shard_map/ppermute | solution.py:26
  35.6 5.8 %collective-permute-start.18 = (bf16[64,384]{1,0:T(8,128)(2,1)S(1)}, bf16[64,384]{1,0:T(8,128)(2,1)S(1)}, u32[]{:S(2)}, u32[]{:S(2)}) collective-permute-start(bf16[64,384]{1,0:T(8,128)(2,1)S(1)} %get-tuple-element.91), channel_id=1, source_target_pairs={{0,6},{1,7},{2,4},{3,5},{4,2},{5,3},{6,0},{7,1},{8,14},{9,15},{10,... | collective-permute-start | bytes 147464 | tf_op jit(solution)/shard_map/ppermute | solution.py:26
  37.1 4.3 %collective-permute-start.16 = (bf16[64,384]{1,0:T(8,128)(2,1)S(1)}, bf16[64,384]{1,0:T(8,128)(2,1)S(1)}, u32[]{:S(2)}, u32[]{:S(2)}) collective-permute-start(bf16[64,384]{1,0:T(8,128)(2,1)S(1)} %get-tuple-element.102.refs_0_), channel_id=1, source_target_pairs={{0,2},{1,3},{2,0},{3,1},{4,6},{5,7},{6,4},{7,5},{8,10},{9,11},{10,... | collective-permute-start | bytes 147464 | tf_op jit(solution)/shard_map/ppermute | solution.py:26
  37.5 4.9 %collective-permute-start.20 = (bf16[3,64,256]{2,1,0:T(8,128)(2,1)S(1)}, bf16[3,64,256]{2,1,0:T(8,128)(2,1)S(1)}, u32[]{:S(2)}, u32[]{:S(2)}) collective-permute-start(bf16[3,64,256]{2,1,0:T(8,128)(2,1)S(1)} %get-tuple-element.100), channel_id=1, source_target_pairs={{0,4},{1,5},{2,6},{3,7},{4,0},{5,1},{6,2},{7,3},{8,12},{9,13},{10,... | collective-permute-start | bytes 294920 | tf_op jit(solution)/shard_map/ppermute | solution.py:26
  41.3 2.0 %collective-permute-start.21 = (bf16[64,384]{1,0:T(8,128)(2,1)S(1)}, bf16[64,384]{1,0:T(8,128)(2,1)S(1)}, u32[]{:S(2)}, u32[]{:S(2)}) collective-permute-start(bf16[64,384]{1,0:T(8,128)(2,1)S(1)} %get-tuple-element.102.refs_0_), channel_id=1, source_target_pairs={{0,1},{1,0},{2,3},{3,2},{4,5},{5,4},{6,7},{7,6},{8,9},{9,8},{10,11... | collective-permute-start | bytes 147464 | tf_op jit(solution)/shard_map/ppermute | solution.py:26
  41.4 2.0 %collective-permute-start.22 = (bf16[64,384]{1,0:T(8,128)(2,1)S(1)}, bf16[64,384]{1,0:T(8,128)(2,1)S(1)}, u32[]{:S(2)}, u32[]{:S(2)}) collective-permute-start(bf16[64,384]{1,0:T(8,128)(2,1)S(1)} %collective-permute-done.16.refs_1_), channel_id=1, source_target_pairs={{0,1},{1,0},{2,3},{3,2},{4,5},{5,4},{6,7},{7,6},{8,9},{9,8},{10,11... | collective-permute-start | bytes 147464 | tf_op jit(solution)/shard_map/ppermute | solution.py:26
  41.9 1.5 %collective-permute-start.23 = (bf16[64,384]{1,0:T(8,128)(2,1)S(1)}, bf16[64,384]{1,0:T(8,128)(2,1)S(1)}, u32[]{:S(2)}, u32[]{:S(2)}) collective-permute-start(bf16[64,384]{1,0:T(8,128)(2,1)S(1)} %collective-permute-done.17.refs_2_), channel_id=1, source_target_pairs={{0,1},{1,0},{2,3},{3,2},{4,5},{5,4},{6,7},{7,6},{8,9},{9,8},{10,11... | collective-permute-start | bytes 147464 | tf_op jit(solution)/shard_map/ppermute | solution.py:26
  41.9 1.4 %collective-permute-start.24 = (bf16[64,384]{1,0:T(8,128)(2,1)S(1)}, bf16[64,384]{1,0:T(8,128)(2,1)S(1)}, u32[]{:S(2)}, u32[]{:S(2)}) collective-permute-start(bf16[64,384]{1,0:T(8,128)(2,1)S(1)} %collective-permute-done.18.refs_3_), channel_id=1, source_target_pairs={{0,1},{1,0},{2,3},{3,2},{4,5},{5,4},{6,7},{7,6},{8,9},{9,8},{10,11... | collective-permute-start | bytes 147464 | tf_op jit(solution)/shard_map/ppermute | solution.py:26
  (2 other events, 2.4 us)
